TPU v7x, 32 devices: a whole 2x2x4 slice. The times are simulated.
32 devices in a mesh: member: 2 (over x), lon: 16 (over z, y, core).
Axes of the slice: x: 2, y: 2, z: 4, core: 2. Of those that a mesh axis runs over, the one named last changes fastest.
Arguments:
- surface_old: float32 [1024, 256], P(('member', 'lon')), parts along dimension 0, may hold values from -6 to 6
- surface_forcing: float32 [1024, 256], P(('member', 'lon')), parts along dimension 0, may hold values from -13 to 13
- surface_coeff: float32 [512, 256], P('lon'), may hold values from 0.1 to 1
- ocean_mask: int32 [512, 256], P('lon'), may hold values from 0 to 1, as said below
- column_depth: int32 [256, 512], P('lon'), may hold values from 0 to 16, as said below
- east_depth: int32 [256, 512], P('lon'), may hold values from 0 to 16, as said below
- tracers: float32 [16, 16, 256, 512], P('member', None, 'lon'), parts along dimension 0, may hold values from 0.05 to 2
- u_clinic: float32 [32, 256, 512], P('member', 'lon'), parts along dimension 0, may hold values from -0.9 to 0.9
- v_clinic: float32 [32, 256, 512], P('member', 'lon'), parts along dimension 0, may hold values from -0.9 to 0.9
Outputs:
- surface: float32 [1024, 256], P(('member', 'lon')), parts along dimension 0
- tracers_new: float32 [16, 16, 256, 512], P('member', None, 'lon'), parts along dimension 0
There are 2 independent parts, one for each index of `member`. A program takes and returns all parts, laid end to end along the dimension named above; an argument that names none is the same for every part. Nothing has to cross between parts.
Inputs may be any that keep to these rules, and one draw needn't show every extreme that they name: ocean_mask[j, i] is 1 exactly where column_depth[i, j] is positive, else 0. `column_depth`: 0 marks land. east_depth[i, j] is the smaller of column_depth[i, j] and column_depth[i + 1, j], longitudes periodic.
All inputs are finite; a program needn't handle non-finite values.
Results may differ from a plain program's by a relative error of at most 0.0003.
Values sent between devices are 32-bit elements; how exact they have to be, the bound alone decides.
No kernel may reach another device: no remote copies, remote signals or barrier semaphores. Data moves between devices by JAX's collectives and lax.ppermute only.
A program may use at most 64 MiB of HBM per device.

v0:
```python
import jax
import jax.numpy as jnp
from jax import lax
from jax.sharding import PartitionSpec as P

SOLVER_ITERS = 4


BARO_GAIN = 0.1
HORIZ_DIFF = 0.1
VERT_DIFF = 0.15
RATE_CARBON = 0.3
RATE_AMMONIUM = 0.2
RATE_NITRITE = 0.2
RATE_SULFIDE = 0.3
RATE_NITROUS = 0.2
HALF_OXYGEN = 0.3
HALF_NITRATE = 0.3
HALF_NITRITE = 0.3
YIELD_NITROUS = 0.3


def padded_2(block, sides, width, periodic):
    for axis, dim in sides:
        count = lax.axis_size(axis)
        forward = [(i, i + 1) for i in range(count - 1)]
        if periodic:
            forward.append((count - 1, 0))
        backward = [(target, source) for source, target in forward]
        low = lax.ppermute(
            lax.slice_in_dim(block, block.shape[dim] - width, None, axis=dim), axis, forward
        )
        high = lax.ppermute(lax.slice_in_dim(block, 0, width, axis=dim), axis, backward)
        block = jnp.concatenate([low, block, high], axis=dim)
    return block


def apply_operator(values_in, mask_float, coeff):
    masked = mask_float * values_in
    padded = padded_2(masked, (("lon", 0),), 1, False)
    top_device = lax.axis_index("lon") == lax.axis_size("lon") - 1
    folded = jnp.where(top_device, masked[-1:, ::-1], padded[-1:])
    northern = jnp.concatenate([padded[2:-1], folded], axis=0)
    southern = padded[:-2]
    eastern = jnp.roll(masked, -1, axis=1)
    western = jnp.roll(masked, 1, axis=1)
    return (coeff + 4.0 * mask_float) * values_in - mask_float * (
        northern + southern + eastern + western
    )


def squared_total(residual):
    return lax.psum(jnp.sum(residual * residual), "lon")


def plain_solve(right_side, mask_float, coeff):
    solution = jnp.zeros_like(right_side)
    residual = right_side
    direction = right_side
    norm_now = squared_total(residual)
    for sweep in range(SOLVER_ITERS):
        applied = apply_operator(direction, mask_float, coeff)
        curvature = lax.psum(jnp.sum(direction * applied), "lon")
        step_size = norm_now / curvature
        solution = solution + step_size * direction
        residual = residual - step_size * applied
        norm_next = squared_total(residual)
        direction = residual + norm_next / norm_now * direction
        norm_now = norm_next
    return solution


def open_faces(column_depth, east_depth, east_baro, north_baro, u_clinic, v_clinic):
    level_index = lax.broadcasted_iota(jnp.int32, u_clinic.shape, 0)
    wet = (level_index < column_depth[None]).astype(jnp.float32)
    east_open = (level_index < east_depth[None]).astype(jnp.float32)
    north_open = wet * jnp.concatenate([wet[:, :, 1:], jnp.zeros_like(wet[:, :, :1])], axis=2)
    below_open = wet * jnp.concatenate([wet[1:], jnp.zeros_like(wet[:1])], axis=0)
    east_flow = (u_clinic + east_baro[None]) * east_open
    north_flow = (v_clinic + north_baro[None]) * north_open
    return (wet, east_open, north_open, below_open, east_flow, north_flow)


def meridional_vertical(masked, north_flow, north_open, below_open):
    count_rows = masked.shape[-1]
    pad_widths = [(0, 0)] * (masked.ndim - 1) + [(2, 2)]
    padded = jnp.pad(masked, pad_widths)
    south_one = padded[..., 1 : count_rows + 1]
    north_one = padded[..., 3 : count_rows + 3]
    north_two = padded[..., 4 : count_rows + 4]
    face_north = (7.0 * (masked + north_one) - (south_one + north_two)) / 12.0
    flux_north = north_flow * face_north - HORIZ_DIFF * (north_one - masked) * north_open
    flux_south = jnp.concatenate(
        [jnp.zeros_like(flux_north[..., :1]), flux_north[..., :-1]], axis=-1
    )
    below = jnp.concatenate([masked[..., 1:, :, :], jnp.zeros_like(masked[..., :1, :, :])], axis=-3)
    flux_down = VERT_DIFF * (below - masked) * below_open
    flux_up = jnp.concatenate(
        [jnp.zeros_like(flux_down[..., :1, :, :]), flux_down[..., :-1, :, :]], axis=-3
    )
    return flux_south - flux_north + (flux_down - flux_up)


def redox_sources(masked):
    oxygen = masked[0]
    nitrate = masked[1]
    nitrite = masked[2]
    ammonium = masked[3]
    carbon = masked[5]
    sulfide = masked[6]
    nitrous = masked[7]
    breakdown = RATE_CARBON * carbon
    with_oxygen = oxygen / (oxygen + HALF_OXYGEN)
    with_nitrate = (1.0 - with_oxygen) * nitrate / (nitrate + HALF_NITRATE)
    with_nitrite = (1.0 - with_oxygen - with_nitrate) * nitrite / (nitrite + HALF_NITRITE)
    with_sulfate = 1.0 - with_oxygen - with_nitrate - with_nitrite
    first_nitr = RATE_AMMONIUM * ammonium * with_oxygen
    second_nitr = RATE_NITRITE * nitrite * with_oxygen
    sulfide_ox = RATE_SULFIDE * sulfide * with_oxygen
    return jnp.stack(
        [
            -1.3 * breakdown * with_oxygen
            - 1.5 * first_nitr
            - 0.5 * second_nitr
            - 2.0 * sulfide_ox,
            -0.9 * breakdown * with_nitrate + second_nitr,
            0.9 * breakdown * with_nitrate
            - 0.6 * breakdown * with_nitrite
            + (1.0 - YIELD_NITROUS) * first_nitr
            - second_nitr,
            0.15 * breakdown - first_nitr,
            0.1 * breakdown,
            -breakdown,
            0.5 * breakdown * with_sulfate - sulfide_ox,
            YIELD_NITROUS * first_nitr - RATE_NITROUS * nitrous * (1.0 - with_oxygen),
        ]
    )


def body(
    surface_old,
    surface_forcing,
    surface_coeff,
    ocean_mask,
    column_depth,
    east_depth,
    tracers,
    u_clinic,
    v_clinic,
):
    mask_float = ocean_mask.astype(jnp.float32)
    right_side = surface_coeff * surface_old + surface_forcing
    surface = plain_solve(right_side, mask_float, surface_coeff)
    band_flow = -BARO_GAIN * (jnp.roll(surface, -1, axis=1) - surface)
    moved = lax.all_to_all(
        jnp.stack([surface, band_flow]), "lon", split_axis=2, concat_axis=1, tiled=True
    )
    strip_surface = moved[0].T
    east_baro = moved[1].T
    above_surface = jnp.concatenate([strip_surface[:, 1:], strip_surface[:, -1:]], axis=1)
    north_baro = -BARO_GAIN * (above_surface - strip_surface)
    wet, east_open, north_open, below_open, east_flow, north_flow = open_faces(
        column_depth, east_depth, east_baro, north_baro, u_clinic, v_clinic
    )
    masked = tracers * wet[None]
    tracer_count = masked.shape[0]
    columns_here = masked.shape[2]
    stacked = jnp.concatenate([masked, east_flow[None], east_open[None]], axis=0)
    padded = padded_2(stacked, (("lon", 2),), 2, True)
    tracer_pad = padded[:tracer_count]
    west_flow = padded[tracer_count, :, 1:2]
    west_open = padded[tracer_count + 1, :, 1:2]
    flow_all = jnp.concatenate([west_flow, east_flow], axis=1)
    open_all = jnp.concatenate([west_open, east_open], axis=1)
    center = tracer_pad[:, :, 1 : columns_here + 2]
    east_one = tracer_pad[:, :, 2 : columns_here + 3]
    west_one = tracer_pad[:, :, 0 : columns_here + 1]
    east_two = tracer_pad[:, :, 3 : columns_here + 4]
    face_east = (7.0 * (center + east_one) - (west_one + east_two)) / 12.0
    flux_all = flow_all[None] * face_east - HORIZ_DIFF * (east_one - center) * open_all[None]
    conv_east = flux_all[:, :, :-1] - flux_all[:, :, 1:]
    transport = conv_east + meridional_vertical(
        masked, north_flow[None], north_open[None], below_open[None]
    )
    tendency = transport + redox_sources(masked)
    tracers_new = tracers + wet[None] * tendency
    return (surface, tracers_new)


def solution(mesh):
    in_specs = (
        P(("member", "lon"), None),
        P(("member", "lon"), None),
        P("lon", None),
        P("lon", None),
        P("lon", None),
        P("lon", None),
        P("member", None, "lon", None),
        P("member", "lon", None),
        P("member", "lon", None),
    )
    out_specs = (P(("member", "lon"), None), P("member", None, "lon", None))
    return jax.shard_map(body, mesh=mesh, in_specs=in_specs, out_specs=out_specs, check_vma=False)
```

profile of v0, /device:TPU:0, one launch (start us, length us, event | category | flops | bytes accessed | tf_op | source)
XLA Modules:
  0.0 328.7 jit_solution(14252063561252996319)
XLA Ops:
  1.5 2.4 collective-permute-start.1
  3.8 1.3 collective-permute-start
  6.0 4.9 %copy_multiply_fusion = f32[8,16,16,512]{3,1,2,0:T(8,128)S(1)} fusion(f32[8,16,16,512]{3,2,1,0:T(8,128)} %param.15, f32[16,16,512]{2,0,1:T(8,128)S(1)} %fusion.20), kind=kLoop, calls=%fused_computation.19 | loop fusion | flops 1048576 | bytes 8912896 | tf_op jit(solution)/shard_map/mul | solution.py:165
  13.2 2.0 copy-done.4
  16.3 36.4 %all-reduce.6 = (f32[]{:T(128)}, f32[]{:T(128)}) all-reduce(f32[]{:T(128)} %get-tuple-element.9, f32[]{:T(128)} %get-tuple-element.8), channel_id=1, replica_groups=mesh['member'=2,'lon'=16] {'lon'}, use_global_device_ids=true, to_apply=%region_1.0 | all-reduce | flops 2 | bytes 16 | tf_op jit(solution)/shard_map/psum | solution.py:53
  54.8 30.1 %psum.58 = f32[]{:T(128)} all-reduce(f32[]{:T(128)} %multiply_reduce_fusion.4), channel_id=1, replica_groups=mesh['member'=2,'lon'=16] {'lon'}, use_global_device_ids=true, to_apply=%region_5.6 | all-reduce | flops 1 | bytes 8 | tf_op jit(solution)/shard_map/psum | solution.py:53
  86.3 1.3 collective-permute-start.2
  87.7 3.0 collective-permute-start.3
  92.2 31.1 %psum.59 = f32[]{:T(128)} all-reduce(f32[]{:T(128)} %get-tuple-element.20), channel_id=1, replica_groups=mesh['member'=2,'lon'=16] {'lon'}, use_global_device_ids=true, to_apply=%region_7.8 | all-reduce | flops 1 | bytes 8 | tf_op jit(solution)/shard_map/psum | solution.py:63
  125.3 30.1 %psum.60 = f32[]{:T(128)} all-reduce(f32[]{:T(128)} %get-tuple-element.18), channel_id=1, replica_groups=mesh['member'=2,'lon'=16] {'lon'}, use_global_device_ids=true, to_apply=%region_9.10 | all-reduce | flops 1 | bytes 8 | tf_op jit(solution)/shard_map/psum | solution.py:53
  156.8 1.3 collective-permute-start.4
  158.2 3.0 collective-permute-start.5
  162.7 31.1 %psum.61 = f32[]{:T(128)} all-reduce(f32[]{:T(128)} %get-tuple-element.14), channel_id=1, replica_groups=mesh['member'=2,'lon'=16] {'lon'}, use_global_device_ids=true, to_apply=%region_11.12 | all-reduce | flops 1 | bytes 8 | tf_op jit(solution)/shard_map/psum | solution.py:63
  195.8 30.1 %psum.62 = f32[]{:T(128)} all-reduce(f32[]{:T(128)} %multiply_reduce_fusion), channel_id=1, replica_groups=mesh['member'=2,'lon'=16] {'lon'}, use_global_device_ids=true, to_apply=%region_13.14 | all-reduce | flops 1 | bytes 8 | tf_op jit(solution)/shard_map/psum | solution.py:53
  227.3 1.3 collective-permute-start.6
  228.7 3.0 collective-permute-start.7
  233.3 5.0 %slice.315 = f32[8,15,16,512]{3,1,2,0:T(8,128)} slice(f32[8,16,16,512]{3,1,2,0:T(8,128)} %copy-done), slice={[0:8], [1:16], [0:16], [0:512]} | slice | bytes 7864320 | tf_op jit(solution)/shard_map/slice | solution.py:96
  238.3 31.2 %psum.63 = f32[]{:T(128)} all-reduce(f32[]{:T(128)} %fusion.29), channel_id=1, replica_groups=mesh['member'=2,'lon'=16] {'lon'}, use_global_device_ids=true, to_apply=%region_15.16 | all-reduce | flops 1 | bytes 8 | tf_op jit(solution)/shard_map/psum | solution.py:63
  271.2 0.9 reshape.32
  272.1 3.5 %all-to-all-start = ((f32[16,1,1024]{2,1,0:T(1,128)}), f32[16,1,1024]{2,1,0:T(1,128)S(1)}, u32[]{:S(2)}, u32[]{:S(2)}) async-start(f32[16,1,1024]{2,1,0:T(1,128)} %reshape.32), calls=%async_computation | async-start | bytes 131072 | tf_op jit(solution)/shard_map/all_to_all | solution.py:155
  275.6 0.9 fusion.19
  276.5 6.0 %all-to-all-done = f32[16,1,1024]{2,1,0:T(1,128)S(1)} async-done(((f32[16,1,1024]{2,1,0:T(1,128)}), f32[16,1,1024]{2,1,0:T(1,128)S(1)}, u32[]{:S(2)}, u32[]{:S(2)}) %all-to-all-start) | async-done | bytes 65568 | tf_op jit(solution)/shard_map/all_to_all | solution.py:155
  283.1 0.8 reduce
  285.1 2.6 pad_maximum_fusion.3
  287.7 4.4 %collective-permute-start.9 = (f32[10,16,2,512]{3,1,2,0:T(8,128)}, f32[10,16,2,512]{3,1,2,0:T(8,128)}, u32[]{:S(2)}, u32[]{:S(2)}) collective-permute-start(f32[10,16,2,512]{3,1,2,0:T(8,128)} %get-tuple-element.30), channel_id=1, source_target_pairs={{1,0},{2,1},{3,2},{4,3},{5,4},{6,5},{7,6},{8,7},{9,8},{10,9},{11,1... | collective-permute-start | bytes 1966088 | tf_op jit(solution)/shard_map/ppermute | solution.py:33
  292.2 1.6 fusion.17
  293.8 3.8 %fusion.6 = (f32[8,16,16,512]{3,1,2,0:T(8,128)S(1)}, f32[8,16,16,512]{3,1,2,0:T(8,128)S(1)}) fusion(f32[8,16,16,512]{3,1,2,0:T(8,128)S(1)} %copy-done.1, f32[16,16,512]{2,0,1:T(8,128)S(1)} %get-tuple-element.36, f32[16,16,512]{2,0,1:T(8,128)S(1)} %get-tuple-element.35, f32[16,16,512]{2,0,1:T(8,128)S(1)} %get-tuple-element.39, f32[8,15,16,512]{3,1,2,0:T(8,128)S(1)} %copy-done.2), kind=kLoop, calls=%fused_computation.12 | loop fusion | flops 10485760 | bytes 18087936 | tf_op jit(solution)/shard_map/sub | solution.py:92
  298.0 2.8 collective-permute-done.8
  301.8 4.4 %maximum_maximum_fusion = (f32[10,16,18,512]{3,1,2,0:T(8,128)S(1)}, f32[10,16,18,512]{3,1,2,0:T(8,128)}) fusion(f32[1,16,16,512]{3,1,2,0:T(8,128)S(1)} %copy-done.6, f32[1,16,16,512]{3,1,2,0:T(8,128)S(1)} %fusion.64, f32[8,16,16,512]{3,1,2,0:T(8,128)S(1)} %copy-done.1, f32[10,16,2,512]{3,1,2,0:T(8,128)} %collective-permute-done.8, ...), kind=kLoop, calls=%fused_computation | loop fusion | flops 8847360 | bytes 18350080 | tf_op jit(solution)/shard_map/concatenate | solution.py:34
  306.2 6.3 %fusion.2 = f32[8,16,17,512]{3,1,2,0:T(8,128)} fusion(f32[10,16,18,512]{3,1,2,0:T(8,128)} %get-tuple-element.28, f32[10,16,18,512]{3,1,2,0:T(8,128)S(1)} %get-tuple-element.27, f32[16,17,512]{2,0,1:T(8,128)S(1)} %get-tuple-element.65, f32[16,17,512]{2,0,1:T(8,128)S(1)} %get-tuple-element.64), kind=kLoop, calls=%fused_computation.8 | loop fusion | flops 8912896 | bytes 23396352 | tf_op jit(solution)/shard_map/sub | solution.py:180
  312.5 11.7 %fusion.10 = f32[8,16,16,512]{3,1,2,0:T(8,128)S(1)} fusion(f32[8,16,16,512]{3,1,2,0:T(8,128)} %copy-done.4, f32[8,16,17,512]{3,1,2,0:T(8,128)} %fusion.2, f32[8,16,16,512]{3,1,2,0:T(8,128)S(1)} %get-tuple-element.32, f32[8,15,16,512]{3,1,2,0:T(8,128)S(1)} %bitcast.28, f32[8,16,16,512]{3,1,2,0:T(8,128)S(1)} %get-tuple-element.31, ...), kind=kLoop, calls=%fused_computation.17 | loop fusion | flops 8388608 | bytes 38002688 | tf_op jit(solution)/shard_map/add | solution.py:186
  324.2 4.5 %copy.35 = f32[8,16,16,512]{3,2,1,0:T(8,128)} copy(f32[8,16,16,512]{3,1,2,0:T(8,128)S(1)} %fusion.10) | data formatting | bytes 8388608
  (107 shorter events, 15.4 us)
Async XLA Ops:
  1.5 14.0 %collective-permute-start.1 = (f32[1,256]{1,0:T(1,128)S(1)}, f32[1,256]{1,0:T(1,128)S(1)}, u32[]{:S(2)}, u32[]{:S(2)}) collective-permute-start(f32[1,256]{1,0:T(1,128)S(1)} %get-tuple-element.59), channel_id=1, source_target_pairs={{0,1},{1,2},{2,3},{3,4},{4,5},{5,6},{6,7},{7,8},{8,9},{9,10},{10,1... | collective-permute-start | bytes 3080 | tf_op jit(solution)/shard_map/ppermute | solution.py:30
  3.8 11.7 %collective-permute-start = (f32[1,256]{1,0:T(1,128)S(1)}, f32[1,256]{1,0:T(1,128)S(1)}, u32[]{:S(2)}, u32[]{:S(2)}) collective-permute-start(f32[1,256]{1,0:T(1,128)S(1)} %get-tuple-element.58), channel_id=1, source_target_pairs={{1,0},{2,1},{3,2},{4,3},{5,4},{6,5},{7,6},{8,7},{9,8},{10,9},{11,1... | collective-permute-start | bytes 3080 | tf_op jit(solution)/shard_map/ppermute | solution.py:33
  6.0 189.7 %copy-start.3 = (f32[16,16,512]{2,0,1:T(8,128)}, f32[16,16,512]{2,0,1:T(8,128)S(1)}, u32[]{:S(2)}) copy-start(f32[16,16,512]{2,0,1:T(8,128)S(1)} %fusion.20) | copy-start | bytes 1572868
  11.0 1.9 copy-start
  12.3 2.9 copy-start.13
  12.3 3.2 copy-start.10
  12.3 3.2 copy-start.11
  13.1 2.0 copy-start.4
  15.2 269.8 %copy-start.5 = (f32[1,16,16,512]{3,1,2,0:T(8,128)}, f32[1,16,16,512]{3,1,2,0:T(8,128)S(1)}, u32[]{:S(2)}) copy-start(f32[1,16,16,512]{3,1,2,0:T(8,128)S(1)} %fusion.21) | copy-start | bytes 1572868
  86.3 4.6 %collective-permute-start.2 = (f32[1,256]{1,0:T(1,128)S(1)}, f32[1,256]{1,0:T(1,128)S(1)}, u32[]{:S(2)}, u32[]{:S(2)}) collective-permute-start(f32[1,256]{1,0:T(1,128)S(1)} %get-tuple-element.52), channel_id=1, source_target_pairs={{1,0},{2,1},{3,2},{4,3},{5,4},{6,5},{7,6},{8,7},{9,8},{10,9},{11,1... | collective-permute-start | bytes 3080 | tf_op jit(solution)/shard_map/ppermute | solution.py:33
  87.7 3.8 %collective-permute-start.3 = (f32[1,256]{1,0:T(1,128)S(1)}, f32[1,256]{1,0:T(1,128)S(1)}, u32[]{:S(2)}, u32[]{:S(2)}) collective-permute-start(f32[1,256]{1,0:T(1,128)S(1)} %get-tuple-element.53), channel_id=1, source_target_pairs={{0,1},{1,2},{2,3},{3,4},{4,5},{5,6},{6,7},{7,8},{8,9},{9,10},{10,1... | collective-permute-start | bytes 3080 | tf_op jit(solution)/shard_map/ppermute | solution.py:30
  156.8 4.6 %collective-permute-start.4 = (f32[1,256]{1,0:T(1,128)S(1)}, f32[1,256]{1,0:T(1,128)S(1)}, u32[]{:S(2)}, u32[]{:S(2)}) collective-permute-start(f32[1,256]{1,0:T(1,128)S(1)} %get-tuple-element.46), channel_id=1, source_target_pairs={{1,0},{2,1},{3,2},{4,3},{5,4},{6,5},{7,6},{8,7},{9,8},{10,9},{11,1... | collective-permute-start | bytes 3080 | tf_op jit(solution)/shard_map/ppermute | solution.py:33
  158.2 3.8 %collective-permute-start.5 = (f32[1,256]{1,0:T(1,128)S(1)}, f32[1,256]{1,0:T(1,128)S(1)}, u32[]{:S(2)}, u32[]{:S(2)}) collective-permute-start(f32[1,256]{1,0:T(1,128)S(1)} %get-tuple-element.47), channel_id=1, source_target_pairs={{0,1},{1,2},{2,3},{3,4},{4,5},{5,6},{6,7},{7,8},{8,9},{9,10},{10,1... | collective-permute-start | bytes 3080 | tf_op jit(solution)/shard_map/ppermute | solution.py:30
  227.3 4.6 %collective-permute-start.6 = (f32[1,256]{1,0:T(1,128)S(1)}, f32[1,256]{1,0:T(1,128)S(1)}, u32[]{:S(2)}, u32[]{:S(2)}) collective-permute-start(f32[1,256]{1,0:T(1,128)S(1)} %get-tuple-element.44), channel_id=1, source_target_pairs={{1,0},{2,1},{3,2},{4,3},{5,4},{6,5},{7,6},{8,7},{9,8},{10,9},{11,1... | collective-permute-start | bytes 3080 | tf_op jit(solution)/shard_map/ppermute | solution.py:33
  228.7 3.8 %collective-permute-start.7 = (f32[1,256]{1,0:T(1,128)S(1)}, f32[1,256]{1,0:T(1,128)S(1)}, u32[]{:S(2)}, u32[]{:S(2)}) collective-permute-start(f32[1,256]{1,0:T(1,128)S(1)} %get-tuple-element.45), channel_id=1, source_target_pairs={{0,1},{1,2},{2,3},{3,4},{4,5},{5,6},{6,7},{7,8},{8,9},{9,10},{10,1... | collective-permute-start | bytes 3080 | tf_op jit(solution)/shard_map/ppermute | solution.py:30
  238.3 46.3 %copy-start.8 = (f32[16,16,512]{2,1,0:T(8,128)S(1)}, f32[16,16,512]{2,1,0:T(8,128)}, u32[]{:S(2)}) copy-start(f32[16,16,512]{2,1,0:T(8,128)} %param.16) | copy-start | bytes 1572868
  270.9 16.8 %copy-start.12 = (f32[32,256]{1,0:T(8,128)}, f32[32,256]{1,0:T(8,128)S(1)}, u32[]{:S(2)}) copy-start(f32[32,256]{1,0:T(8,128)S(1)} %multiply_add_fusion) | copy-start | bytes 98308
  272.1 10.4 %all-to-all-start = ((f32[16,1,1024]{2,1,0:T(1,128)}), f32[16,1,1024]{2,1,0:T(1,128)S(1)}, u32[]{:S(2)}, u32[]{:S(2)}) async-start(f32[16,1,1024]{2,1,0:T(1,128)} %reshape.32), calls=%async_computation | async-start | bytes 131072 | tf_op jit(solution)/shard_map/all_to_all | solution.py:155
  284.3 8.0 %copy-start.14 = (s32[16,512]{1,0:T(8,128)S(1)}, s32[16,512]{1,0:T(8,128)}, u32[]{:S(2)}) copy-start(s32[16,512]{1,0:T(8,128)} %param.13) | copy-start | bytes 98308
  285.0 8.7 %copy-start.1 = (f32[8,16,16,512]{3,1,2,0:T(8,128)S(1)}, f32[8,16,16,512]{3,1,2,0:T(8,128)}, u32[]{:S(2)}) copy-start(f32[8,16,16,512]{3,1,2,0:T(8,128)} %copy-done) | copy-start | bytes 12582916
  285.1 8.7 %copy-start.2 = (f32[8,15,16,512]{3,1,2,0:T(8,128)S(1)}, f32[8,15,16,512]{3,1,2,0:T(8,128)}, u32[]{:S(2)}) copy-start(f32[8,15,16,512]{3,1,2,0:T(8,128)} %slice.315) | copy-start | bytes 11796484
  287.7 13.1 %collective-permute-start.8 = (f32[10,16,2,512]{3,1,2,0:T(8,128)}, f32[10,16,2,512]{3,1,2,0:T(8,128)}, u32[]{:S(2)}, u32[]{:S(2)}) collective-permute-start(f32[10,16,2,512]{3,1,2,0:T(8,128)} %get-tuple-element.29), channel_id=1, source_target_pairs={{0,1},{1,2},{2,3},{3,4},{4,5},{5,6},{6,7},{7,8},{8,9},{9,10},{10,1... | collective-permute-start | bytes 1966088 | tf_op jit(solution)/shard_map/ppermute | solution.py:30
  287.7 14.1 %collective-permute-start.9 = (f32[10,16,2,512]{3,1,2,0:T(8,128)}, f32[10,16,2,512]{3,1,2,0:T(8,128)}, u32[]{:S(2)}, u32[]{:S(2)}) collective-permute-start(f32[10,16,2,512]{3,1,2,0:T(8,128)} %get-tuple-element.30), channel_id=1, source_target_pairs={{1,0},{2,1},{3,2},{4,3},{5,4},{6,5},{7,6},{8,7},{9,8},{10,9},{11,1... | collective-permute-start | bytes 1966088 | tf_op jit(solution)/shard_map/ppermute | solution.py:33
  293.8 3.8 %copy-start.9 = (f32[16,16,512]{2,1,0:T(8,128)S(1)}, f32[16,16,512]{2,1,0:T(8,128)}, u32[]{:S(2)}) copy-start(f32[16,16,512]{2,1,0:T(8,128)} %param.16) | copy-start | bytes 1572868
  293.8 7.8 %copy-start.7 = (f32[16,16,512]{2,0,1:T(8,128)S(1)}, f32[16,16,512]{2,0,1:T(8,128)}, u32[]{:S(2)}) copy-start(f32[16,16,512]{2,0,1:T(8,128)} %fusion.19) | copy-start | bytes 1572868
  293.8 8.0 %copy-start.6 = (f32[1,16,16,512]{3,1,2,0:T(8,128)S(1)}, f32[1,16,16,512]{3,1,2,0:T(8,128)}, u32[]{:S(2)}) copy-start(f32[1,16,16,512]{3,1,2,0:T(8,128)} %copy-done.5) | copy-start | bytes 1572868
where the time goes:
time: 333 us; the launch traced here: 329 us
  blocking collectives  220 us (66%)
  other arithmetic  46.5 us (14%)
  starting transfers between devices  24.5 us (7%)
  local copies, waits for them, and re-layouts  16.6 us (5%)
  waiting for transfers between devices  10.6 us (3%)
  between operations  10.4 us (3%)
    psum x4, blocking collectives, squared_total(): return lax.psum(jnp.sum(residual * residual), 'lon')  127 us
    psum x3, blocking collectives, plain_solve(): curvature = lax.psum(jnp.sum(direction * applied), 'lon')  93.4 us
    add x1, other arithmetic, body(): tracers_new = tracers + wet[None] * tendency  11.7 us
    ppermute x5, starting transfers between devices, padded_2(): lax.ppermute(lax.slice_in_dim(block, block.shape[dim] - width, None, axis...  11.4 us
    ppermute x5, starting transfers between devices, padded_2(): lax.ppermute(lax.slice_in_dim(block, 0, width, axis=dim), axis, backward)  9.59 us
    unnamed x33, local copies, waits for them, and re-layouts  7.77 us
  transfers between devices with their start and end apart: 11, of which 5 were waited for; matrix products, arithmetic and copies ran while one was open for 5% of the time, Pallas kernels for 0%

commit v1 on v0

--- a/solution.py
+++ b/solution.py
@@ -1,10 +1,9 @@
 import jax
 import jax.numpy as jnp
 from jax import lax
+from jax.experimental import pallas as pl
+from jax.experimental.pallas import tpu as pltpu
 from jax.sharding import PartitionSpec as P
-
-SOLVER_ITERS = 4
-
 
 BARO_GAIN = 0.1
 HORIZ_DIFF = 0.1
@@ -35,39 +34,192 @@
     return block
 
 
-def apply_operator(values_in, mask_float, coeff):
-    masked = mask_float * values_in
-    padded = padded_2(masked, (("lon", 0),), 1, False)
-    top_device = lax.axis_index("lon") == lax.axis_size("lon") - 1
-    folded = jnp.where(top_device, masked[-1:, ::-1], padded[-1:])
-    northern = jnp.concatenate([padded[2:-1], folded], axis=0)
-    southern = padded[:-2]
-    eastern = jnp.roll(masked, -1, axis=1)
-    western = jnp.roll(masked, 1, axis=1)
-    return (coeff + 4.0 * mask_float) * values_in - mask_float * (
-        northern + southern + eastern + western
-    )
-
-
-def squared_total(residual):
-    return lax.psum(jnp.sum(residual * residual), "lon")
-
-
-def plain_solve(right_side, mask_float, coeff):
-    solution = jnp.zeros_like(right_side)
-    residual = right_side
-    direction = right_side
-    norm_now = squared_total(residual)
-    for sweep in range(SOLVER_ITERS):
-        applied = apply_operator(direction, mask_float, coeff)
-        curvature = lax.psum(jnp.sum(direction * applied), "lon")
-        step_size = norm_now / curvature
-        solution = solution + step_size * direction
-        residual = residual - step_size * applied
-        norm_next = squared_total(residual)
-        direction = residual + norm_next / norm_now * direction
-        norm_now = norm_next
-    return solution
+LANES = 128
+HALO = 8
+SLAB_ROWS = 24
+BASIS = 4
+CENTRE = 4.55
+SPREAD = 4.45
+PIVOT_FLOOR = 3e-7
+
+
+def pack_kernel(old_ref, force_ref, coeff_ref, mask_ref, low_ref, high_ref):
+    rows = old_ref.shape[0]
+    coeff = coeff_ref[...]
+    fields = (
+        coeff * old_ref[...] + force_ref[...],
+        coeff,
+        mask_ref[...].astype(jnp.float32),
+    )
+    for place, field in enumerate(fields):
+        low_ref[HALO * place : HALO * (place + 1)] = field[:HALO]
+        high_ref[HALO * place : HALO * (place + 1)] = field[rows - HALO :]
+
+
+def basis_kernel(
+    old_ref, force_ref, coeff_ref, mask_ref, below_ref, above_ref, folded_ref, slabs_ref, basis_ref
+):
+    rows, width = old_ref.shape
+    count = slabs_ref.shape[0]
+    columns = width // count
+    top_device = lax.axis_index("lon") == count - 1
+    above = jnp.where(top_device, folded_ref[...], above_ref[...])
+
+    def extended(place, own):
+        part = slice(HALO * place, HALO * (place + 1))
+        return jnp.concatenate([below_ref[part], own, above[part]], axis=0)
+
+    coeff_own = coeff_ref[...]
+    first = extended(0, coeff_own * old_ref[...] + force_ref[...])
+    coeff = extended(1, coeff_own)
+    mask = extended(2, mask_ref[...].astype(jnp.float32))
+    diagonal = (coeff + 4.0 * mask - CENTRE) * (1.0 / SPREAD)
+    beside = mask * (1.0 / SPREAD)
+    total = rows + 2 * HALO
+
+    def scaled(values):
+        masked = mask * values
+        around = (
+            pltpu.roll(masked, total - 1, 0)
+            + pltpu.roll(masked, 1, 0)
+            + pltpu.roll(masked, width - 1, 1)
+            + pltpu.roll(masked, 1, 1)
+        )
+        return diagonal * values - beside * around
+
+    vectors = [first, scaled(first)]
+    while len(vectors) < BASIS + 1:
+        vectors.append(2.0 * scaled(vectors[-1]) - vectors[-2])
+    own = [vector[HALO : HALO + rows] for vector in vectors]
+    sums = []
+    for order in range(2 * BASIS):
+        product = own[order // 2] * own[(order + 1) // 2]
+        sums.append(jnp.sum(product, axis=0, keepdims=True))
+    partial = jnp.sum(jnp.concatenate(sums, axis=0), axis=1, keepdims=True)
+    lane = lax.broadcasted_iota(jnp.int32, (2 * BASIS, LANES), 1)
+    place = lax.broadcasted_iota(jnp.int32, (2 * BASIS, LANES), 0)
+    moments = jnp.sum(jnp.where(lane == place, partial, 0.0), axis=0, keepdims=True)
+    stacked = jnp.concatenate(own[:BASIS], axis=0)
+    basis_ref[...] = stacked
+    if BASIS * rows < LANES:
+        stacked = jnp.concatenate(
+            [stacked, jnp.zeros((LANES - BASIS * rows, width), jnp.float32)], axis=0
+        )
+    turned = stacked.T
+    for target in range(count):
+        start = target * columns
+        east = (start + columns) % width
+        west = (start - 1) % width
+        slabs_ref[target, :columns] = turned[start : start + columns]
+        slabs_ref[target, columns : columns + 1] = turned[east : east + 1]
+        slabs_ref[target, columns + 1 : columns + 2] = turned[west : west + 1]
+        slabs_ref[target, columns + 2 : columns + 3] = moments
+
+
+def basis_weights(moments):
+    gram = {}
+
+    def inner(i, j):
+        key = (i + j, abs(i - j))
+        if key not in gram:
+            gram[key] = 0.5 * (moments[i + j] + moments[abs(i - j)])
+        return gram[key]
+
+    matrix = [[None] * BASIS for _ in range(BASIS)]
+    for i in range(BASIS):
+        for j in range(i + 1):
+            if i == 0:
+                image = moments[1]
+            elif j == 0:
+                image = inner(1, i)
+            else:
+                image = 0.5 * (inner(i, j + 1) + inner(i, j - 1))
+            matrix[i][j] = CENTRE * inner(i, j) + SPREAD * image
+    right = [inner(i, 0) for i in range(BASIS)]
+    start = [matrix[i][i] for i in range(BASIS)]
+    inverse = []
+    factors = [[None] * BASIS for _ in range(BASIS)]
+    for n in range(BASIS):
+        pivot = matrix[n][n]
+        inverse.append(jnp.where(pivot > PIVOT_FLOOR * start[n], 1.0 / pivot, 0.0))
+        for i in range(n + 1, BASIS):
+            factors[i][n] = matrix[i][n] * inverse[n]
+        for i in range(n + 1, BASIS):
+            for j in range(n + 1, i + 1):
+                matrix[i][j] = matrix[i][j] - factors[i][n] * matrix[j][n]
+            right[i] = right[i] - factors[i][n] * right[n]
+    weights = [None] * BASIS
+    for n in reversed(range(BASIS)):
+        value = right[n] * inverse[n]
+        for i in range(n + 1, BASIS):
+            value = value - factors[i][n] * weights[i]
+        weights[n] = value
+    return weights
+
+
+def combine_kernel(slabs_ref, basis_ref, strip_ref, surface_ref):
+    count, slab_rows, _ = slabs_ref.shape
+    rows, width = surface_ref.shape
+    columns = width // count
+    moment_row = slabs_ref[0, columns + 2 : columns + 3]
+    for source in range(1, count):
+        moment_row = moment_row + slabs_ref[source, columns + 2 : columns + 3]
+    dots = [moment_row[:, m : m + 1] for m in range(2 * BASIS)]
+    weights = basis_weights(
+        dots[:2] + [2.0 * dots[m] - dots[m % 2] for m in range(2, 2 * BASIS)]
+    )
+    group = lax.broadcasted_iota(jnp.int32, (1, LANES), 1) // rows
+    lane_weight = jnp.zeros((1, LANES), jnp.float32)
+    for k in range(BASIS):
+        lane_weight = jnp.where(group == k, weights[k], lane_weight)
+    surface = weights[0] * basis_ref[:rows]
+    for k in range(1, BASIS):
+        surface = surface + weights[k] * basis_ref[k * rows : (k + 1) * rows]
+    surface_ref[...] = surface
+    groups = LANES // rows
+    group_full = lax.broadcasted_iota(jnp.int32, (slab_rows, LANES), 1) // rows
+    for tile in range(count // groups):
+        joined = None
+        for p in range(groups):
+            part = slabs_ref[tile * groups + p] * lane_weight
+            shift = LANES // 2
+            while shift >= rows:
+                part = part + pltpu.roll(part, shift, 1)
+                shift //= 2
+            joined = part if joined is None else jnp.where(group_full == p, part, joined)
+        strip_ref[:, tile * LANES : (tile + 1) * LANES] = joined
+
+
+def solve_surface(surface_old, surface_forcing, surface_coeff, ocean_mask):
+    rows, width = surface_old.shape
+    count = lax.axis_size("lon")
+    f32 = jnp.float32
+    packed = jax.ShapeDtypeStruct((3 * HALO, width), f32)
+    fields = (surface_old, surface_forcing, surface_coeff, ocean_mask)
+    low, high = pl.pallas_call(pack_kernel, out_shape=(packed, packed), name="pack_edges")(*fields)
+    forward = [(i, i + 1) for i in range(count - 1)]
+    backward = [(target, source) for source, target in forward]
+    below = lax.ppermute(high, "lon", forward)
+    above = lax.ppermute(low, "lon", backward)
+    folded = jnp.flip(high.reshape(3, HALO, width), axis=(1, 2)).reshape(3 * HALO, width)
+    slabs, basis = pl.pallas_call(
+        basis_kernel,
+        out_shape=(
+            jax.ShapeDtypeStruct((count, SLAB_ROWS, LANES), f32),
+            jax.ShapeDtypeStruct((BASIS * rows, width), f32),
+        ),
+        name="solver_basis",
+    )(*fields, below, above, folded)
+    moved = lax.all_to_all(slabs, "lon", split_axis=0, concat_axis=0, tiled=True)
+    strip, surface = pl.pallas_call(
+        combine_kernel,
+        out_shape=(
+            jax.ShapeDtypeStruct((SLAB_ROWS, count * rows), f32),
+            jax.ShapeDtypeStruct((rows, width), f32),
+        ),
+        name="solver_combine",
+    )(moved, basis)
+    return strip, surface
 
 
 def open_faces(column_depth, east_depth, east_baro, north_baro, u_clinic, v_clinic):
@@ -148,15 +300,10 @@
     u_clinic,
     v_clinic,
 ):
-    mask_float = ocean_mask.astype(jnp.float32)
-    right_side = surface_coeff * surface_old + surface_forcing
-    surface = plain_solve(right_side, mask_float, surface_coeff)
-    band_flow = -BARO_GAIN * (jnp.roll(surface, -1, axis=1) - surface)
-    moved = lax.all_to_all(
-        jnp.stack([surface, band_flow]), "lon", split_axis=2, concat_axis=1, tiled=True
-    )
-    strip_surface = moved[0].T
-    east_baro = moved[1].T
+    strip, surface = solve_surface(surface_old, surface_forcing, surface_coeff, ocean_mask)
+    columns = tracers.shape[2]
+    strip_surface = strip[:columns]
+    east_baro = -BARO_GAIN * (strip[1 : columns + 1] - strip_surface)
     above_surface = jnp.concatenate([strip_surface[:, 1:], strip_surface[:, -1:]], axis=1)
     north_baro = -BARO_GAIN * (above_surface - strip_surface)
     wet, east_open, north_open, below_open, east_flow, north_flow = open_faces(

time: 333 us -> 90.1 us (0.27)
  the two profiles are of different devices: /device:TPU:0 before, /device:TPU:1 now
where the time goes in v1:
time: 90.1 us; the launch traced here: 89.5 us
  other arithmetic  38.3 us (43%)
  waiting for transfers between devices  17.4 us (19%)
  starting transfers between devices  14 us (16%)
  local copies, waits for them, and re-layouts  12.8 us (14%)
  Pallas kernels  6.23 us (7%)
    add x1, other arithmetic, body(): tracers_new = tracers + wet[None] * tendency  11.7 us
    unnamed x31, local copies, waits for them, and re-layouts  8.97 us
    ppermute x1, waiting for transfers between devices, padded_2(): lax.ppermute(lax.slice_in_dim(block, block.shape[dim] - width, None, axis...  8.92 us
    all_to_all x1, starting transfers between devices, solve_surface(): lax.all_to_all(slabs, 'lon', split_axis=0, concat_axis=0, tiled=True)  6.45 us
    sub x1, other arithmetic, body(): flow_all[None] * face_east  6.32 us
    all_to_all x1, waiting for transfers between devices, solve_surface(): lax.all_to_all(slabs, 'lon', split_axis=0, concat_axis=0, tiled=True)  5.6 us
    mul x1, other arithmetic, body(): masked = tracers * wet[None]  4.92 us
    ppermute x1, starting transfers between devices, solve_surface(): below = lax.ppermute(high, 'lon', forward)  4.53 us
  transfers between devices with their start and end apart: 5, of which 3 were waited for; matrix products, arithmetic and copies ran while one was open for 17% of the time, Pallas kernels for 0%

profile of v1, /device:TPU:1, one launch (start us, length us, event | category | flops | bytes accessed | tf_op | source)
XLA Modules:
  0.0 89.5 jit_solution(5757638960531202453)
XLA Ops:
  0.6 1.4 %pack_edges.1 = (f32[24,256]{1,0:T(8,128)}, f32[24,256]{1,0:T(8,128)}) custom-call(f32[32,256]{1,0:T(8,128)} %old_ref.3, f32[32,256]{1,0:T(8,128)} %force_ref.3, f32[32,256]{1,0:T(8,128)} %coeff_ref.3, s32[32,256]{1,0:T(8,128)} %mask_ref.3), custom_call_target="tpu_custom_call" | custom-call | tf_op jit(solution)/shard_map/pack_edges/pallas_call | solution.py:199
  2.1 4.5 %collective-permute-start = (f32[24,256]{1,0:T(8,128)}, f32[24,256]{1,0:T(8,128)S(1)}, u32[]{:S(2)}, u32[]{:S(2)}) collective-permute-start(f32[24,256]{1,0:T(8,128)} %get-tuple-element.8), channel_id=1, source_target_pairs={{0,1},{1,2},{2,3},{3,4},{4,5},{5,6},{6,7},{7,8},{8,9},{9,10},{10,1... | collective-permute-start | bytes 73736 | tf_op jit(solution)/shard_map/ppermute | solution.py:202
  6.6 1.9 %collective-permute-start.1 = (f32[24,256]{1,0:T(8,128)}, f32[24,256]{1,0:T(8,128)S(1)}, u32[]{:S(2)}, u32[]{:S(2)}) collective-permute-start(f32[24,256]{1,0:T(8,128)} %get-tuple-element.9), channel_id=1, source_target_pairs={{1,0},{2,1},{3,2},{4,3},{5,4},{6,5},{7,6},{8,7},{9,8},{10,9},{11,1... | collective-permute-start | bytes 73736 | tf_op jit(solution)/shard_map/ppermute | solution.py:203
  8.5 0.8 fusion.20
  9.3 4.9 %copy_multiply_fusion = f32[8,16,16,512]{3,1,2,0:T(8,128)S(1)} fusion(f32[8,16,16,512]{3,2,1,0:T(8,128)} %param.15, f32[16,16,512]{2,0,1:T(8,128)S(1)} %fusion.20), kind=kLoop, calls=%fused_computation.19 | loop fusion | flops 1048576 | bytes 8912896 | tf_op jit(solution)/shard_map/mul | solution.py:312
  14.3 0.4 subtract_dynamic-update-slice_fusion.3
  14.9 0.4 subtract_dynamic-update-slice_fusion.2
  15.7 0.5 copy-done
  16.2 0.3 subtract_dynamic-update-slice_fusion
  16.6 2.0 %copy-done.3 = f32[8,16,16,512]{3,1,2,0:T(8,128)} copy-done((f32[8,16,16,512]{3,1,2,0:T(8,128)}, f32[8,16,16,512]{3,1,2,0:T(8,128)S(1)}, u32[]{:S(2)}) %copy-start.3) | copy-done | bytes 4194328
  18.6 0.7 rev.4
  19.4 0.6 copy-done.12
  20.0 2.0 %solver_basis.1 = (f32[16,24,128]{2,1,0:T(8,128)}, f32[128,256]{1,0:T(8,128)}) custom-call(f32[32,256]{1,0:T(8,128)} %old_ref.3, f32[32,256]{1,0:T(8,128)} %force_ref.3, f32[32,256]{1,0:T(8,128)} %coeff_ref.3, s32[32,256]{1,0:T(8,128)} %mask_ref.3, f32[24,256]{1,0:T(8,128)} %copy-done.12, f32[24,256]{1,0:T(8,128)} %copy-done.13, f32[24,256]{1,0:T(8,128)} %bitcast.13), custom_call_target="tpu_custom_call" | custom-call | tf_op jit(solution)/shard_map/solver_basis/pallas_call | solution.py:205
  22.0 6.5 %all-to-all-start = ((f32[16,24,128]{2,1,0:T(8,128)}), f32[16,24,128]{2,1,0:T(8,128)S(1)}, u32[]{:S(2)}, u32[]{:S(2)}) async-start(f32[16,24,128]{2,1,0:T(8,128)} %get-tuple-element.10), calls=%async_computation | async-start | bytes 393216 | tf_op jit(solution)/shard_map/all_to_all | solution.py:213
  28.8 2.4 %fusion.13 = f32[8,16,16,512]{3,1,2,0:T(8,128)} fusion(f32[8,16,16,512]{3,1,2,0:T(8,128)} %copy-done.3, f32[8,16,16,512]{3,1,2,0:T(8,128)} %copy-done), kind=kLoop, calls=%fused_computation.29 | loop fusion | flops 1179648 | bytes 2097152 | tf_op jit(solution)/shard_map/stack | solution.py:272
  31.1 5.6 %all-to-all-done.slabs_ref = f32[16,24,128]{2,1,0:T(8,128)S(1)} async-done(((f32[16,24,128]{2,1,0:T(8,128)}), f32[16,24,128]{2,1,0:T(8,128)S(1)}, u32[]{:S(2)}, u32[]{:S(2)}) %all-to-all-start) | async-done | bytes 196640 | tf_op jit(solution)/shard_map/all_to_all | solution.py:213
  36.7 0.7 copy-done.7
  37.4 2.8 %solver_combine.1 = (f32[24,512]{1,0:T(8,128)}, f32[32,256]{1,0:T(8,128)}) custom-call(f32[16,24,128]{2,1,0:T(8,128)} %copy-done.7, f32[128,256]{1,0:T(8,128)} %get-tuple-element.11.basis_ref), custom_call_target="tpu_custom_call" | custom-call | tf_op jit(solution)/shard_map/solver_combine/pallas_call | solution.py:214
  40.2 1.0 %slice.113 = f32[16,511]{1,0:T(8,128)S(1)} slice(f32[24,512]{1,0:T(8,128)} %get-tuple-element.13), slice={[0:16], [1:512]} | slice | bytes 65408 | tf_op jit(solution)/shard_map/slice | solution.py:307
  41.2 1.0 %slice.114 = f32[16,1]{1,0:T(8,128)S(1)} slice(f32[24,512]{1,0:T(8,128)} %get-tuple-element.13), slice={[0:16], [511:512]} | slice | bytes 128 | tf_op jit(solution)/shard_map/slice | solution.py:307
  42.2 1.0 %fusion.23 = (f32[16,512]{1,0:T(8,128)S(1)}, f32[16,512]{1,0:T(8,128)S(1)}) fusion(f32[16,1]{1,0:T(8,128)S(1)} %slice.114, f32[16,511]{1,0:T(8,128)S(1)} %slice.113, f32[24,512]{1,0:T(8,128)} %get-tuple-element.13), kind=kLoop, calls=%fused_computation.62 | loop fusion | flops 40960 | bytes 163840 | tf_op jit(solution)/shard_map/mul | solution.py:308
  43.2 0.9 %fusion.17 = (f32[16,16,512]{2,0,1:T(8,128)S(1)}, f32[16,16,512]{2,0,1:T(8,128)S(1)}, f32[16,16,512]{2,0,1:T(8,128)S(1)}, f32[16,16,512]{2,0,1:T(8,128)S(1)}) fusion(f32[16,16,512]{2,1,0:T(8,128)S(1)} %copy-done.8, f32[16,16,511]{2,0,1:T(8,128)S(1)} %slice.135, f32[16,512]{1,0:T(8,128)S(1)} %get-tuple-element.26, s32[16,512]{1,0:T(8,128)S(1)} %copy-done.11, ...), kind=kLoop, calls=%fused_computation.36 | loop fusion | flops 1441792 | bytes 4291584 | tf_op jit(solution)/shard_map/mul | solution.py:244
  44.5 0.8 slice.137
  45.3 1.0 %collective-permute-start.3 = (f32[10,16,2,512]{3,1,2,0:T(8,128)S(1)}, f32[10,16,2,512]{3,1,2,0:T(8,128)}, u32[]{:S(2)}, u32[]{:S(2)}) collective-permute-start(f32[10,16,2,512]{3,1,2,0:T(8,128)S(1)} %get-tuple-element.19), channel_id=1, source_target_pairs={{1,0},{2,1},{3,2},{4,3},{5,4},{6,5},{7,6},{8,7},{9,8},{10,9},{11,1... | collective-permute-start | bytes 1966088 | tf_op jit(solution)/shard_map/ppermute | solution.py:32
  46.3 3.8 %fusion.6 = (f32[8,16,16,512]{3,1,2,0:T(8,128)S(1)}, f32[8,16,16,512]{3,1,2,0:T(8,128)S(1)}) fusion(f32[8,16,16,512]{3,1,2,0:T(8,128)S(1)} %copy-done.1, f32[16,16,512]{2,0,1:T(8,128)S(1)} %get-tuple-element.25, f32[16,16,512]{2,0,1:T(8,128)S(1)} %get-tuple-element.24, f32[16,16,512]{2,0,1:T(8,128)S(1)} %get-tuple-element.28, f32[8,15,16,512]{3,1,2,0:T(8,128)S(1)} %slice.137), kind=kLoop, calls=%fused_computation.12 | loop fusion | flops 10485760 | bytes 18087936 | tf_op jit(solution)/shard_map/sub | solution.py:244
  50.0 8.9 %collective-permute-done.2 = f32[10,16,2,512]{3,1,2,0:T(8,128)S(1)} collective-permute-done((f32[10,16,2,512]{3,1,2,0:T(8,128)S(1)}, f32[10,16,2,512]{3,1,2,0:T(8,128)S(1)}, u32[]{:S(2)}, u32[]{:S(2)}) %collective-permute-start.2) | collective-permute-done | bytes 655392 | tf_op jit(solution)/shard_map/ppermute | solution.py:29
  59.1 0.7 copy-done.6
  59.8 2.8 %collective-permute-done.3 = f32[10,16,2,512]{3,1,2,0:T(8,128)} collective-permute-done((f32[10,16,2,512]{3,1,2,0:T(8,128)S(1)}, f32[10,16,2,512]{3,1,2,0:T(8,128)}, u32[]{:S(2)}, u32[]{:S(2)}) %collective-permute-start.3) | collective-permute-done | bytes 655392 | tf_op jit(solution)/shard_map/ppermute | solution.py:32
  62.6 4.4 %maximum_maximum_fusion = (f32[10,16,18,512]{3,1,2,0:T(8,128)S(1)}, f32[10,16,18,512]{3,1,2,0:T(8,128)}) fusion(f32[1,16,16,512]{3,1,2,0:T(8,128)S(1)} %copy-done.5, f32[1,16,16,512]{3,1,2,0:T(8,128)S(1)} %bitcast.12, f32[8,16,16,512]{3,1,2,0:T(8,128)S(1)} %copy-done.1, f32[10,16,2,512]{3,1,2,0:T(8,128)} %copy-done.6, f32[10,16,2,512]{3,1,2,0:T(8,128)} %collective-permute-done.3), kind=kLoop, calls=%fused_computation | loop fusion | flops 8847360 | bytes 18350080 | tf_op jit(solution)/shard_map/concatenate | solution.py:33
  67.0 6.3 %fusion.2 = f32[8,16,17,512]{3,1,2,0:T(8,128)} fusion(f32[10,16,18,512]{3,1,2,0:T(8,128)} %get-tuple-element.17, f32[10,16,18,512]{3,1,2,0:T(8,128)S(1)} %get-tuple-element.16, f32[16,17,512]{2,0,1:T(8,128)S(1)} %maximum_multiply_fusion.1, f32[16,17,512]{2,0,1:T(8,128)S(1)} %maximum_multiply_fusion), kind=kLoop, calls=%fused_computation.8 | loop fusion | flops 8912896 | bytes 23396352 | tf_op jit(solution)/shard_map/sub | solution.py:327
  73.3 11.7 %fusion.10 = f32[8,16,16,512]{3,1,2,0:T(8,128)S(1)} fusion(f32[8,16,16,512]{3,1,2,0:T(8,128)} %fusion.13, f32[8,16,17,512]{3,1,2,0:T(8,128)} %fusion.2, f32[8,16,16,512]{3,1,2,0:T(8,128)S(1)} %get-tuple-element.21, f32[8,15,16,512]{3,1,2,0:T(8,128)S(1)} %bitcast.10, f32[8,16,16,512]{3,1,2,0:T(8,128)S(1)} %get-tuple-element.20, ...), kind=kLoop, calls=%fused_computation.17 | loop fusion | flops 8388608 | bytes 38002688 | tf_op jit(solution)/shard_map/add | solution.py:333
  85.0 4.5 %copy.15 = f32[8,16,16,512]{3,2,1,0:T(8,128)} copy(f32[8,16,16,512]{3,1,2,0:T(8,128)S(1)} %fusion.10) | data formatting | bytes 8388608
  (40 shorter events, 1.4 us)
Async XLA Ops:
  2.1 17.3 %collective-permute-start = (f32[24,256]{1,0:T(8,128)}, f32[24,256]{1,0:T(8,128)S(1)}, u32[]{:S(2)}, u32[]{:S(2)}) collective-permute-start(f32[24,256]{1,0:T(8,128)} %get-tuple-element.8), channel_id=1, source_target_pairs={{0,1},{1,2},{2,3},{3,4},{4,5},{5,6},{6,7},{7,8},{8,9},{9,10},{10,1... | collective-permute-start | bytes 73736 | tf_op jit(solution)/shard_map/ppermute | solution.py:202
  6.6 12.8 %collective-permute-start.1 = (f32[24,256]{1,0:T(8,128)}, f32[24,256]{1,0:T(8,128)S(1)}, u32[]{:S(2)}, u32[]{:S(2)}) collective-permute-start(f32[24,256]{1,0:T(8,128)} %get-tuple-element.9), channel_id=1, source_target_pairs={{1,0},{2,1},{3,2},{4,3},{5,4},{6,5},{7,6},{8,7},{9,8},{10,9},{11,1... | collective-permute-start | bytes 73736 | tf_op jit(solution)/shard_map/ppermute | solution.py:203
  9.3 19.4 %copy-start.2 = (f32[16,16,512]{2,0,1:T(8,128)}, f32[16,16,512]{2,0,1:T(8,128)S(1)}, u32[]{:S(2)}) copy-start(f32[16,16,512]{2,0,1:T(8,128)S(1)} %fusion.20) | copy-start | bytes 1572868
  14.3 2.0 %copy-start = (f32[8,16,16,512]{3,1,2,0:T(8,128)}, f32[8,16,16,512]{3,1,2,0:T(8,128)S(1)}, u32[]{:S(2)}) copy-start(f32[8,16,16,512]{3,1,2,0:T(8,128)S(1)} %copy_multiply_fusion) | copy-start | bytes 12582916
  15.4 3.2 %copy-start.14 = (f32[24,256]{1,0:T(8,128)S(1)}, f32[24,256]{1,0:T(8,128)}, u32[]{:S(2)}) copy-start(f32[24,256]{1,0:T(8,128)} %get-tuple-element.8) | copy-start | bytes 73732
  15.4 13.0 %copy-start.10 = (s32[16,512]{1,0:T(8,128)S(1)}, s32[16,512]{1,0:T(8,128)}, u32[]{:S(2)}) copy-start(s32[16,512]{1,0:T(8,128)} %param.14) | copy-start | bytes 98308
  16.2 27.0 %copy-start.8 = (f32[16,16,512]{2,1,0:T(8,128)S(1)}, f32[16,16,512]{2,1,0:T(8,128)}, u32[]{:S(2)}) copy-start(f32[16,16,512]{2,1,0:T(8,128)} %param.17) | copy-start | bytes 1572868
  16.2 27.0 %copy-start.9 = (f32[16,16,512]{2,1,0:T(8,128)S(1)}, f32[16,16,512]{2,1,0:T(8,128)}, u32[]{:S(2)}) copy-start(f32[16,16,512]{2,1,0:T(8,128)} %param.16) | copy-start | bytes 1572868
  16.2 27.0 %copy-start.11 = (s32[16,512]{1,0:T(8,128)S(1)}, s32[16,512]{1,0:T(8,128)}, u32[]{:S(2)}) copy-start(s32[16,512]{1,0:T(8,128)} %param.13) | copy-start | bytes 98308
  16.6 2.0 %copy-start.3 = (f32[8,16,16,512]{3,1,2,0:T(8,128)}, f32[8,16,16,512]{3,1,2,0:T(8,128)S(1)}, u32[]{:S(2)}) copy-start(f32[8,16,16,512]{3,1,2,0:T(8,128)S(1)} %subtract_dynamic-update-slice_fusion) | copy-start | bytes 12582916
  19.4 0.6 copy-start.12
  19.4 0.6 copy-start.13
  22.0 14.8 %all-to-all-start = ((f32[16,24,128]{2,1,0:T(8,128)}), f32[16,24,128]{2,1,0:T(8,128)S(1)}, u32[]{:S(2)}, u32[]{:S(2)}) async-start(f32[16,24,128]{2,1,0:T(8,128)} %get-tuple-element.10), calls=%async_computation | async-start | bytes 393216 | tf_op jit(solution)/shard_map/all_to_all | solution.py:213
  28.5 15.7 %copy-start.4 = (f32[1,16,16,512]{3,1,2,0:T(8,128)}, f32[1,16,16,512]{3,1,2,0:T(8,128)S(1)}, u32[]{:S(2)}) copy-start(f32[1,16,16,512]{3,1,2,0:T(8,128)S(1)} %fusion.21) | copy-start | bytes 1572868
  36.7 0.7 copy-start.7
  40.2 3.9 %copy-start.1 = (f32[8,16,16,512]{3,1,2,0:T(8,128)S(1)}, f32[8,16,16,512]{3,1,2,0:T(8,128)}, u32[]{:S(2)}) copy-start(f32[8,16,16,512]{3,1,2,0:T(8,128)} %copy-done) | copy-start | bytes 12582916
  44.3 14.6 %collective-permute-start.2 = (f32[10,16,2,512]{3,1,2,0:T(8,128)S(1)}, f32[10,16,2,512]{3,1,2,0:T(8,128)S(1)}, u32[]{:S(2)}, u32[]{:S(2)}) collective-permute-start(f32[10,16,2,512]{3,1,2,0:T(8,128)S(1)} %get-tuple-element.18), channel_id=1, source_target_pairs={{0,1},{1,2},{2,3},{3,4},{4,5},{5,6},{6,7},{7,8},{8,9},{9,10},{10,1... | collective-permute-start | bytes 1966088 | tf_op jit(solution)/shard_map/ppermute | solution.py:29
  45.3 17.4 %collective-permute-start.3 = (f32[10,16,2,512]{3,1,2,0:T(8,128)S(1)}, f32[10,16,2,512]{3,1,2,0:T(8,128)}, u32[]{:S(2)}, u32[]{:S(2)}) collective-permute-start(f32[10,16,2,512]{3,1,2,0:T(8,128)S(1)} %get-tuple-element.19), channel_id=1, source_target_pairs={{1,0},{2,1},{3,2},{4,3},{5,4},{6,5},{7,6},{8,7},{9,8},{10,9},{11,1... | collective-permute-start | bytes 1966088 | tf_op jit(solution)/shard_map/ppermute | solution.py:32
  46.3 16.4 %copy-start.5 = (f32[1,16,16,512]{3,1,2,0:T(8,128)S(1)}, f32[1,16,16,512]{3,1,2,0:T(8,128)}, u32[]{:S(2)}) copy-start(f32[1,16,16,512]{3,1,2,0:T(8,128)} %copy-done.4) | copy-start | bytes 1572868
  59.0 0.8 copy-start.6

commit v2 on v1

v2 whole, which is shorter than its diff:
```python
import functools

import jax
import jax.numpy as jnp
from jax import lax
from jax.experimental import pallas as pl
from jax.experimental.pallas import tpu as pltpu
from jax.sharding import PartitionSpec as P

BARO_GAIN = 0.1
HORIZ_DIFF = 0.1
VERT_DIFF = 0.15
RATE_CARBON = 0.3
RATE_AMMONIUM = 0.2
RATE_NITRITE = 0.2
RATE_SULFIDE = 0.3
RATE_NITROUS = 0.2
HALF_OXYGEN = 0.3
HALF_NITRATE = 0.3
HALF_NITRITE = 0.3
YIELD_NITROUS = 0.3


SUBLANES = 8
LANES = 128
SMALL_VMEM = 8 * 2**20
RESULT_VMEM = 14 * 2**20
HALO = 8
SLAB_ROWS = 24
BASIS = 4
CENTRE = 4.55
SPREAD = 4.45
PIVOT_FLOOR = 3e-7


def pack_kernel(old_ref, force_ref, coeff_ref, mask_ref, low_ref, high_ref):
    rows = old_ref.shape[0]
    coeff = coeff_ref[...]
    fields = (
        coeff * old_ref[...] + force_ref[...],
        coeff,
        mask_ref[...].astype(jnp.float32),
    )
    for place, field in enumerate(fields):
        low_ref[HALO * place : HALO * (place + 1)] = field[:HALO]
        high_ref[HALO * place : HALO * (place + 1)] = field[rows - HALO :]


def basis_kernel(
    old_ref,
    force_ref,
    coeff_ref,
    mask_ref,
    below_ref,
    above_ref,
    folded_ref,
    _,
    keep_ref,
    send_ref,
    basis_ref,
):
    rows, width = old_ref.shape
    count = 2 * keep_ref.shape[0]
    columns = width // count
    top_device = lax.axis_index("lon") == count - 1
    above = jnp.where(top_device, folded_ref[...], above_ref[...])

    def extended(place, own):
        part = slice(HALO * place, HALO * (place + 1))
        return jnp.concatenate([below_ref[part], own, above[part]], axis=0)

    coeff_own = coeff_ref[...]
    first = extended(0, coeff_own * old_ref[...] + force_ref[...])
    coeff = extended(1, coeff_own)
    mask = extended(2, mask_ref[...].astype(jnp.float32))
    diagonal = (coeff + 4.0 * mask - CENTRE) * (1.0 / SPREAD)
    beside = mask * (1.0 / SPREAD)
    total = rows + 2 * HALO

    def scaled(values):
        masked = mask * values
        around = (
            pltpu.roll(masked, total - 1, 0)
            + pltpu.roll(masked, 1, 0)
            + pltpu.roll(masked, width - 1, 1)
            + pltpu.roll(masked, 1, 1)
        )
        return diagonal * values - beside * around

    vectors = [first, scaled(first)]
    while len(vectors) < BASIS + 1:
        vectors.append(2.0 * scaled(vectors[-1]) - vectors[-2])
    own = [vector[HALO : HALO + rows] for vector in vectors]
    sums = []
    for order in range(2 * BASIS):
        product = own[order // 2] * own[(order + 1) // 2]
        sums.append(jnp.sum(product, axis=0, keepdims=True))
    partial = jnp.sum(jnp.concatenate(sums, axis=0), axis=1, keepdims=True)
    lane = lax.broadcasted_iota(jnp.int32, (2 * BASIS, LANES), 1)
    place = lax.broadcasted_iota(jnp.int32, (2 * BASIS, LANES), 0)
    moments = jnp.sum(jnp.where(lane == place, partial, 0.0), axis=0, keepdims=True)
    stacked = jnp.concatenate(own[:BASIS], axis=0)
    basis_ref[...] = stacked
    if BASIS * rows < LANES:
        stacked = jnp.concatenate(
            [stacked, jnp.zeros((LANES - BASIS * rows, width), jnp.float32)], axis=0
        )
    turned = stacked.T
    core = lax.rem(lax.axis_index("lon"), 2)
    slabs = []
    for target in range(count):
        start = target * columns
        east = (start + columns) % width
        west = (start - 1) % width
        pieces = [
            turned[start : start + columns],
            turned[east : east + 1],
            turned[west : west + 1],
            moments,
            jnp.zeros((SLAB_ROWS - columns - 3, LANES), jnp.float32),
        ]
        slabs.append(jnp.concatenate(pieces, axis=0))
    for pair in range(count // 2):
        even, odd = slabs[2 * pair], slabs[2 * pair + 1]
        keep_ref[pair] = jnp.where(core == 0, even, odd)
        send_ref[pair] = jnp.where(core == 0, odd, even)


def split_kernel(kept_ref, came_ref, keep_ref, send_ref):
    here = lax.axis_index("lon")
    core, half = lax.rem(here, 2), lax.rem(here // 2, 2)
    for group in range(keep_ref.shape[0]):
        for y in range(2):
            mine, other = kept_ref[2 * group + y], came_ref[2 * group + y]
            first = jnp.where(core == 0, mine, other)
            second = jnp.where(core == 0, other, mine)

            @pl.when(half == y)
            def _():
                keep_ref[group, 0] = first
                keep_ref[group, 1] = second

            @pl.when(half != y)
            def _():
                send_ref[group, 0] = first
                send_ref[group, 1] = second


def spread_kernel(kept_ref, came_ref, *out_refs):
    here = lax.axis_index("lon")
    half, group = lax.rem(here // 2, 2), here // 4
    groups = len(out_refs)
    for step in range(groups):
        target = lax.rem(group + step, groups)
        for core in range(2):
            mine, other = kept_ref[target, core], came_ref[target, core]
            out_refs[step][core] = jnp.where(half == 0, mine, other)
            out_refs[step][2 + core] = jnp.where(half == 0, other, mine)


def basis_weights(moments):
    gram = {}

    def inner(i, j):
        key = (i + j, abs(i - j))
        if key not in gram:
            gram[key] = 0.5 * (moments[i + j] + moments[abs(i - j)])
        return gram[key]

    matrix = [[None] * BASIS for _ in range(BASIS)]
    for i in range(BASIS):
        for j in range(i + 1):
            if i == 0:
                image = moments[1]
            elif j == 0:
                image = inner(1, i)
            else:
                image = 0.5 * (inner(i, j + 1) + inner(i, j - 1))
            matrix[i][j] = CENTRE * inner(i, j) + SPREAD * image
    right = [inner(i, 0) for i in range(BASIS)]
    start = [matrix[i][i] for i in range(BASIS)]
    inverse = []
    factors = [[None] * BASIS for _ in range(BASIS)]
    for n in range(BASIS):
        pivot = matrix[n][n]
        inverse.append(jnp.where(pivot > PIVOT_FLOOR * start[n], 1.0 / pivot, 0.0))
        for i in range(n + 1, BASIS):
            factors[i][n] = matrix[i][n] * inverse[n]
        for i in range(n + 1, BASIS):
            for j in range(n + 1, i + 1):
                matrix[i][j] = matrix[i][j] - factors[i][n] * matrix[j][n]
            right[i] = right[i] - factors[i][n] * right[n]
    weights = [None] * BASIS
    for n in reversed(range(BASIS)):
        value = right[n] * inverse[n]
        for i in range(n + 1, BASIS):
            value = value - factors[i][n] * weights[i]
        weights[n] = value
    return weights


def reverse_tile(tile):
    for axis, size in ((0, SUBLANES), (1, LANES)):
        place = lax.broadcasted_iota(jnp.int32, (SUBLANES, LANES), axis)
        step = size // 2
        while step:
            tile = jnp.where(
                (place & step) != 0,
                pltpu.roll(tile, step, axis),
                pltpu.roll(tile, size - step, axis),
            )
            step //= 2
    return tile


def edge_kernel(
    high_ref,
    tracers_ref,
    depth_ref,
    east_depth_ref,
    u_ref,
    folded_ref,
    east_going_ref,
    west_going_ref,
):
    tiles = high_ref.shape[1] // LANES
    for place in range(3):
        rows = slice(HALO * place, HALO * (place + 1))
        for tile in range(tiles):
            other = tiles - 1 - tile
            folded_ref[rows, tile * LANES : (tile + 1) * LANES] = reverse_tile(
                high_ref[rows, other * LANES : (other + 1) * LANES]
            )
    kinds, levels, columns, rows = tracers_ref.shape
    for z in range(levels):
        for side in range(2):
            column = columns - 2 + side
            west_wet = (z < depth_ref[side : side + 1]).astype(jnp.float32)
            east_wet = (z < depth_ref[column : column + 1]).astype(jnp.float32)
            for kind in range(kinds):
                west_going_ref[2 * z + side, kind : kind + 1] = (
                    tracers_ref[kind, z, side : side + 1] * west_wet
                )
                east_going_ref[2 * z + side, kind : kind + 1] = (
                    tracers_ref[kind, z, column : column + 1] * east_wet
                )
        place = 2 * levels + z // SUBLANES
        row = z % SUBLANES
        east_going_ref[place, row : row + 1] = u_ref[z, columns - 1 : columns]
    place = 2 * levels + levels // SUBLANES
    east_going_ref[place] = jnp.broadcast_to(
        east_depth_ref[columns - 1 : columns].astype(jnp.float32), (SUBLANES, rows)
    )


def grid_tiles(columns, rows):
    return [
        (block, tile)
        for block in range(columns // SUBLANES)
        for tile in range(rows // LANES)
    ]


def tile_index(place):
    block, tile = place
    return (
        slice(block * SUBLANES, (block + 1) * SUBLANES),
        slice(tile * LANES, (tile + 1) * LANES),
    )


def shift_columns(tiles, step, outer, blocks, count):
    sublane = lax.broadcasted_iota(jnp.int32, (SUBLANES, LANES), 0)
    turned = {p: pltpu.roll(x, SUBLANES - 1 if step > 0 else 1, 0) for p, x in tiles.items()}
    inside = sublane < SUBLANES - 1 if step > 0 else sublane > 0
    shifted = {}
    for block in range(blocks):
        for tile in range(count):
            beyond = block + step
            other = turned[beyond, tile] if 0 <= beyond < blocks else outer[tile]
            shifted[block, tile] = jnp.where(inside, turned[block, tile], other)
    return shifted


def shift_rows(tiles, step, blocks, count):
    lane = lax.broadcasted_iota(jnp.int32, (SUBLANES, LANES), 1)
    turned = {p: pltpu.roll(x, LANES - 1 if step > 0 else 1, 1) for p, x in tiles.items()}
    inside = lane < LANES - 1 if step > 0 else lane > 0
    shifted = {}
    for block in range(blocks):
        for tile in range(count):
            beyond = tile + step
            other = turned[block, beyond] if 0 <= beyond < count else 0.0
            shifted[block, tile] = jnp.where(inside, turned[block, tile], other)
    return shifted


def reciprocal(value):
    guess = pl.reciprocal(value, approx=True)
    return guess * (2.0 - value * guess)


def redox_sources(masked):
    oxygen, nitrate, nitrite, ammonium, _, carbon, sulfide, nitrous = masked
    over_oxygen = reciprocal(oxygen + HALF_OXYGEN)
    with_oxygen = oxygen * over_oxygen
    no_oxygen = HALF_OXYGEN * over_oxygen
    with_nitrate = no_oxygen * nitrate * reciprocal(nitrate + HALF_NITRATE)
    rest = no_oxygen - with_nitrate
    with_nitrite = rest * nitrite * reciprocal(nitrite + HALF_NITRITE)
    with_sulfate = rest - with_nitrite
    breakdown = RATE_CARBON * carbon
    first_nitr = RATE_AMMONIUM * ammonium * with_oxygen
    second_nitr = RATE_NITRITE * nitrite * with_oxygen
    sulfide_ox = RATE_SULFIDE * sulfide * with_oxygen
    by_nitrate = 0.9 * breakdown * with_nitrate
    return (
        -1.3 * breakdown * with_oxygen - 1.5 * first_nitr - 0.5 * second_nitr - 2.0 * sulfide_ox,
        second_nitr - by_nitrate,
        by_nitrate
        - 0.6 * breakdown * with_nitrite
        + (1.0 - YIELD_NITROUS) * first_nitr
        - second_nitr,
        0.15 * breakdown - first_nitr,
        0.1 * breakdown,
        -breakdown,
        0.5 * breakdown * with_sulfate - sulfide_ox,
        YIELD_NITROUS * first_nitr - RATE_NITROUS * nitrous * no_oxygen,
    )


def source_kernel(tracers_ref, depth_ref, base_ref):
    kinds, levels, columns, rows = tracers_ref.shape
    places = grid_tiles(columns, rows)

    @pl.loop(0, levels)
    def _(level):
        above = jnp.maximum(level - 1, 0)
        below = jnp.minimum(level + 1, levels - 1)
        mix_up_level = jnp.where(level > 0, VERT_DIFF, 0.0)
        for p in places:
            at = tile_index(p)
            depth_here = depth_ref[at]
            wet = jnp.where(level < depth_here, 1.0, 0.0)
            mix_up = wet * mix_up_level
            mix_down = jnp.where(level + 1 < depth_here, VERT_DIFF, 0.0)
            values = [tracers_ref[(kind, level) + at] for kind in range(kinds)]
            sources = redox_sources([value * wet for value in values])
            for kind in range(kinds):
                value = values[kind]
                down = (tracers_ref[(kind, below) + at] - value) * mix_down
                up = (value - tracers_ref[(kind, above) + at]) * mix_up
                base_ref[(kind, level) + at] = value + (wet * sources[kind] + (down - up))


def north_kernel(tracers_ref, depth_ref, v_ref, before_ref, _, base_ref, face_north_ref, north_ref):
    kinds, levels, columns, rows = tracers_ref.shape
    blocks, count = columns // SUBLANES, rows // LANES
    places = grid_tiles(columns, rows)
    depth = {p: depth_ref[tile_index(p)].astype(jnp.float32) for p in places}
    north_depth = shift_rows(depth, 1, blocks, count)
    for p in places:
        north_ref[tile_index(p)] = jnp.minimum(depth[p], north_depth[p]).astype(jnp.int32)

    @pl.loop(0, levels)
    def _(level):
        wet, scale, mix = {}, {}, {}
        for p in places:
            at = tile_index(p)
            wet[p] = jnp.where(level < depth_ref[at], 1.0, 0.0)
            is_open = level < north_ref[at]
            scale[p] = jnp.where(is_open, 1.0 / 12.0, 0.0)
            mix[p] = jnp.where(is_open, HORIZ_DIFF, 0.0)
        for kind in range(kinds):
            masked = {p: tracers_ref[(kind, level) + tile_index(p)] * wet[p] for p in places}
            one = shift_rows(masked, 1, blocks, count)
            two = shift_rows(one, 1, blocks, count)
            south = shift_rows(masked, -1, blocks, count)
            flux = {}
            for p in places:
                at = (kind, level) + tile_index(p)
                face = (7.0 * (masked[p] + one[p]) - (south[p] + two[p])) * scale[p]
                face_north_ref[at] = face
                flux[p] = v_ref[(level,) + tile_index(p)] * face - mix[p] * (one[p] - masked[p])
            incoming = shift_rows(flux, -1, blocks, count)
            for p in places:
                at = (kind, level) + tile_index(p)
                base_ref[at] = before_ref[at] + (incoming[p] - flux[p])


def east_kernel(
    tracers_ref,
    depth_ref,
    east_depth_ref,
    u_ref,
    from_west_ref,
    from_east_ref,
    own_west_ref,
    before_ref,
    _,
    base_ref,
    face_east_ref,
    face_west_ref,
    flux_west_ref,
):
    kinds, levels, columns, rows = tracers_ref.shape
    blocks, count = columns // SUBLANES, rows // LANES
    places = grid_tiles(columns, rows)
    depth_west = from_west_ref[2 * levels + levels // SUBLANES]
    for z in range(levels):
        row = z % SUBLANES
        u_west = from_west_ref[2 * levels + z // SUBLANES, row : row + 1]
        center, east_one = from_west_ref[2 * z + 1], own_west_ref[2 * z]
        outer = from_west_ref[2 * z] + own_west_ref[2 * z + 1]
        scale_west = jnp.where(z < depth_west, 1.0 / 12.0, 0.0)
        mix_west = jnp.where(z < depth_west, HORIZ_DIFF, 0.0)
        face = (7.0 * (center + east_one) - outer) * scale_west
        face_west_ref[z] = face
        flux_west_ref[z] = u_west * face - mix_west * (east_one - center)

    @pl.loop(0, levels)
    def _(level):
        wet, scale, mix = {}, {}, {}
        for p in places:
            at = tile_index(p)
            wet[p] = jnp.where(level < depth_ref[at], 1.0, 0.0)
            is_open = level < east_depth_ref[at]
            scale[p] = jnp.where(is_open, 1.0 / 12.0, 0.0)
            mix[p] = jnp.where(is_open, HORIZ_DIFF, 0.0)
        for kind in range(kinds):
            def halo(ref, index):
                return [
                    jnp.broadcast_to(
                        ref[index, kind : kind + 1, tile * LANES : (tile + 1) * LANES],
                        (SUBLANES, LANES),
                    )
                    for tile in range(count)
                ]

            masked = {p: tracers_ref[(kind, level) + tile_index(p)] * wet[p] for p in places}
            one = shift_columns(masked, 1, halo(from_east_ref, 2 * level), blocks, count)
            two = shift_columns(one, 1, halo(from_east_ref, 2 * level + 1), blocks, count)
            west = shift_columns(masked, -1, halo(from_west_ref, 2 * level + 1), blocks, count)
            flux = {}
            for p in places:
                at = (kind, level) + tile_index(p)
                face = (7.0 * (masked[p] + one[p]) - (west[p] + two[p])) * scale[p]
                face_east_ref[at] = face
                flux[p] = u_ref[(level,) + tile_index(p)] * face - mix[p] * (one[p] - masked[p])
            incoming = shift_columns(flux, -1, halo(flux_west_ref, level), blocks, count)
            for p in places:
                at = (kind, level) + tile_index(p)
                base_ref[at] = before_ref[at] + (incoming[p] - flux[p])


def update_kernel(groups, *refs):
    came_refs, refs = refs[:groups], refs[groups:]
    basis_ref, base_ref, face_east_ref, face_north_ref, face_west_ref = refs[:5]
    surface_ref, out_ref, slabs_ref, result_ref, sems = refs[5:]
    group = lax.axis_index("lon") // 4
    for step in range(groups):
        source = lax.rem(group + groups - step, groups)
        for place in range(4):
            slabs_ref[4 * source + place] = came_refs[step][place]
    kinds, levels, columns, rows = base_ref.shape
    blocks, count = columns // SUBLANES, rows // LANES
    places = grid_tiles(columns, rows)
    sources, slab_rows, _ = slabs_ref.shape
    band, width = surface_ref.shape
    moment_row = slabs_ref[0, columns + 2 : columns + 3]
    for source in range(1, sources):
        moment_row = moment_row + slabs_ref[source, columns + 2 : columns + 3]
    dots = [moment_row[:, m : m + 1] for m in range(2 * BASIS)]
    weights = basis_weights(
        dots[:2] + [2.0 * dots[m] - dots[m % 2] for m in range(2, 2 * BASIS)]
    )
    lane_group = lax.broadcasted_iota(jnp.int32, (1, LANES), 1) // band
    lane_weight = jnp.zeros((1, LANES), jnp.float32)
    for k in range(BASIS):
        lane_weight = jnp.where(lane_group == k, weights[k], lane_weight)
    surface = weights[0] * basis_ref[:band]
    for k in range(1, BASIS):
        surface = surface + weights[k] * basis_ref[k * band : (k + 1) * band]
    surface_ref[...] = surface

    fill = LANES // band
    group_full = lax.broadcasted_iota(jnp.int32, (slab_rows, LANES), 1) // band
    height, east_edge, west_edge = {}, [], []
    for tile in range(count):
        joined = None
        for p in range(fill):
            part = slabs_ref[tile * fill + p] * lane_weight
            shift = LANES // 2
            while shift >= band:
                part = part + pltpu.roll(part, shift, 1)
                shift //= 2
            joined = part if joined is None else jnp.where(group_full == p, part, joined)
        for block in range(blocks):
            height[block, tile] = joined[block * SUBLANES : (block + 1) * SUBLANES]
        east_edge.append(jnp.broadcast_to(joined[columns : columns + 1], (SUBLANES, LANES)))
        west_edge.append(
            jnp.broadcast_to(joined[columns + 1 : columns + 2], (SUBLANES, LANES))
        )
    height_east = shift_columns(height, 1, east_edge, blocks, count)
    height_north = shift_rows(height, 1, blocks, count)
    flow_east = {p: -BARO_GAIN * (height_east[p] - height[p]) for p in places}
    flow_north = {p: -BARO_GAIN * (height_north[p] - height[p]) for p in places}
    flow_west = [
        -BARO_GAIN * (jnp.broadcast_to(height[0, tile][:1], (SUBLANES, LANES)) - west_edge[tile])
        for tile in range(count)
    ]

    def copy(kind):
        return pltpu.make_async_copy(result_ref.at[kind], out_ref.at[kind], sems.at[kind])

    for kind in range(kinds):
        @pl.loop(0, levels, unroll=4)
        def _(level):
            flux_east, flux_north = {}, {}
            for p in places:
                at = (kind, level) + tile_index(p)
                flux_east[p] = flow_east[p] * face_east_ref[at]
                flux_north[p] = flow_north[p] * face_north_ref[at]
            edge = [
                flow_west[tile]
                * jnp.broadcast_to(
                    face_west_ref[level, kind : kind + 1, tile * LANES : (tile + 1) * LANES],
                    (SUBLANES, LANES),
                )
                for tile in range(count)
            ]
            from_west = shift_columns(flux_east, -1, edge, blocks, count)
            from_south = shift_rows(flux_north, -1, blocks, count)
            for p in places:
                at = (kind, level) + tile_index(p)
                result_ref[at] = base_ref[at] + (
                    (from_west[p] - flux_east[p]) + (from_south[p] - flux_north[p])
                )

        copy(kind).start()
    for kind in range(kinds):
        copy(kind).wait()


def body(
    surface_old,
    surface_forcing,
    surface_coeff,
    ocean_mask,
    column_depth,
    east_depth,
    tracers,
    u_clinic,
    v_clinic,
):
    band, width = surface_old.shape
    kinds, levels, columns, rows = tracers.shape
    count = lax.axis_size("lon")
    f32 = jnp.float32
    sds = jax.ShapeDtypeStruct
    vmem = pl.BlockSpec(memory_space=pltpu.VMEM)
    fields = (surface_old, surface_forcing, surface_coeff, ocean_mask)
    forward = [(i, i + 1) for i in range(count - 1)]
    backward = [(target, source) for source, target in forward]
    ring = [(i, (i + 1) % count) for i in range(count)]
    ring_back = [(target, source) for source, target in ring]

    def call(kernel, out_shape, name, operands, scratch=(), limit=SMALL_VMEM, cost=0):
        return pl.pallas_call(
            kernel,
            out_shape=out_shape,
            in_specs=[vmem] * len(operands),
            out_specs=[pl.BlockSpec(memory_space=pl.ANY) if x is result else vmem for x in out_shape],
            scratch_shapes=list(scratch),
            compiler_params=pltpu.CompilerParams(vmem_limit_bytes=limit),
            cost_estimate=pl.CostEstimate(
                flops=cost * tracers.size, bytes_accessed=8 * tracers.size, transcendentals=0
            )
            if cost
            else None,
            name=name,
        )(*operands)

    result = sds(tracers.shape, f32)
    packed = sds((3 * HALO, width), f32)
    held = pltpu.VMEM(tracers.shape, f32)

    low, high = call(pack_kernel, (packed, packed), "pack_edges", fields)
    below = lax.ppermute(high, "lon", forward)
    above = lax.ppermute(low, "lon", backward)

    folded, east_going, own_west = call(
        edge_kernel,
        (
            packed,
            sds((2 * levels + levels // SUBLANES + 1, kinds, rows), f32),
            sds((2 * levels, kinds, rows), f32),
        ),
        "pack_tracer_edges",
        (high, tracers, column_depth, east_depth, u_clinic),
    )
    from_west = lax.ppermute(east_going, "lon", ring)
    from_east = lax.ppermute(own_west, "lon", ring_back)
    (base,) = call(source_kernel, (held,), "sources", (tracers, column_depth), cost=70)

    groups = count // 4
    half_slabs = sds((count // 2, SLAB_ROWS, LANES), f32)
    keep, send, basis = call(
        basis_kernel,
        (half_slabs, half_slabs, sds((BASIS * band, width), f32)),
        "solver_basis",
        fields + (below, above, folded, base),
    )
    came = lax.ppermute(send, "lon", [(i, i ^ 1) for i in range(count)])
    quarter = sds((groups, 2, SLAB_ROWS, LANES), f32)
    keep, send = call(split_kernel, (quarter, quarter), "split_slabs", (keep, came))
    came = lax.ppermute(send, "lon", [(i, i ^ 2) for i in range(count)])
    base, face_north = call(
        north_kernel,
        (held, held),
        "north_fluxes",
        (tracers, column_depth, v_clinic, base, keep),
        scratch=[pltpu.VMEM((columns, rows), jnp.int32)],
        cost=70,
    )
    sends = call(
        spread_kernel,
        (sds((4, SLAB_ROWS, LANES), f32),) * groups,
        "spread_slabs",
        (keep, came),
    )
    slabs = [sends[0]]
    for step in range(1, groups):
        pairs = [(i, (i + 4 * step) % count) for i in range(count)]
        slabs.append(lax.ppermute(sends[step], "lon", pairs))
    base, face_east, face_west = call(
        east_kernel,
        (held, held, pltpu.VMEM((levels, kinds, rows), f32)),
        "east_fluxes",
        (
            tracers,
            column_depth,
            east_depth,
            u_clinic,
            from_west,
            from_east,
            own_west,
            base,
            sends[0],
        ),
        scratch=[pltpu.VMEM((levels, kinds, rows), f32)],
        cost=70,
    )
    return tuple(
        call(
            functools.partial(update_kernel, groups),
            (sds((band, width), f32), result),
            "surface_update",
            (*slabs, basis, base, face_east, face_north, face_west),
            scratch=[
                pltpu.VMEM((count, SLAB_ROWS, LANES), f32),
                pltpu.VMEM(tracers.shape, f32),
                pltpu.SemaphoreType.DMA((kinds,)),
            ],
            limit=RESULT_VMEM,
        )
    )


def solution(mesh):
    in_specs = (
        P(("member", "lon"), None),
        P(("member", "lon"), None),
        P("lon", None),
        P("lon", None),
        P("lon", None),
        P("lon", None),
        P("member", None, "lon", None),
        P("member", "lon", None),
        P("member", "lon", None),
    )
    out_specs = (P(("member", "lon"), None), P("member", None, "lon", None))
    return jax.shard_map(body, mesh=mesh, in_specs=in_specs, out_specs=out_specs, check_vma=False)
```

time: 90.1 us -> 58.8 us (0.65)
  the two profiles are of different devices: /device:TPU:1 before, /device:TPU:0 now
where the time goes in v2:
time: 58.8 us; the launch traced here: 58.1 us
  Pallas kernels  22.8 us (39%)
  starting transfers between devices  21.1 us (36%)
  local copies, waits for them, and re-layouts  7.8 us (13%)
  waiting for transfers between devices  5.52 us (9%)
  between operations  0.84 us (1%)
    pallas_call x9, Pallas kernels, call(): pl.pallas_call(kernel, out_shape=out_shape, in_specs=[vmem] * len(operand...  22.8 us
    unnamed x34, local copies, waits for them, and re-layouts  7.8 us
    ppermute x1, starting transfers between devices, body(): came = lax.ppermute(send, 'lon', [(i, i ^ 1) for i in range(count)])  5.67 us
    ppermute x1, starting transfers between devices, body(): from_east = lax.ppermute(own_west, 'lon', ring_back)  5.06 us
    ppermute x3, starting transfers between devices, body(): slabs.append(lax.ppermute(sends[step], 'lon', pairs))  4.91 us
    ppermute x1, waiting for transfers between devices, body(): came = lax.ppermute(send, 'lon', [(i, i ^ 2) for i in range(count)])  4.56 us
    ppermute x1, starting transfers between devices, body(): below = lax.ppermute(high, 'lon', forward)  3.03 us
    ppermute x1, starting transfers between devices, body(): above = lax.ppermute(low, 'lon', backward)  1.42 us
  transfers between devices with their start and end apart: 9, of which 2 were waited for; matrix products, arithmetic and copies ran while one was open for 0% of the time, Pallas kernels for 27%

profile of v2, /device:TPU:0, one launch (start us, length us, event | category | flops | bytes accessed | tf_op | source)
XLA Modules:
  0.0 58.1 jit_solution(5755352762345318194)
XLA Ops:
  0.6 0.0 copy-start.9
  0.6 0.7 %copy-done.9 = f32[32,256]{1,0:T(8,128)S(1)} copy-done((f32[32,256]{1,0:T(8,128)S(1)}, f32[32,256]{1,0:T(8,128)}, u32[]{:S(2)}) %copy-start.9) | copy-done | bytes 32792
  1.4 0.8 %copy-done.11 = f32[32,256]{1,0:T(8,128)S(1)} copy-done((f32[32,256]{1,0:T(8,128)S(1)}, f32[32,256]{1,0:T(8,128)}, u32[]{:S(2)}) %copy-start.11) | copy-done | bytes 32792
  2.2 0.8 %copy-done.13 = f32[32,256]{1,0:T(8,128)S(1)} copy-done((f32[32,256]{1,0:T(8,128)S(1)}, f32[32,256]{1,0:T(8,128)}, u32[]{:S(2)}) %copy-start.13) | copy-done | bytes 32792
  2.9 0.8 %copy-done.15 = s32[32,256]{1,0:T(8,128)S(1)} copy-done((s32[32,256]{1,0:T(8,128)S(1)}, s32[32,256]{1,0:T(8,128)}, u32[]{:S(2)}) %copy-start.15) | copy-done | bytes 32792
  3.7 2.2 %copy-done = f32[8,16,16,512]{3,2,1,0:T(8,128)S(1)} copy-done((f32[8,16,16,512]{3,2,1,0:T(8,128)S(1)}, f32[8,16,16,512]{3,2,1,0:T(8,128)}, u32[]{:S(2)}) %copy-start) | copy-done | bytes 4194328
  5.9 1.0 %copy-done.2 = f32[16,16,512]{2,1,0:T(8,128)S(1)} copy-done((f32[16,16,512]{2,1,0:T(8,128)S(1)}, f32[16,16,512]{2,1,0:T(8,128)}, u32[]{:S(2)}) %copy-start.2) | copy-done | bytes 524312
  6.9 0.8 %copy-done.4 = s32[16,512]{1,0:T(8,128)S(1)} copy-done((s32[16,512]{1,0:T(8,128)S(1)}, s32[16,512]{1,0:T(8,128)}, u32[]{:S(2)}) %copy-start.4) | copy-done | bytes 32792
  7.7 0.8 %copy-done.7 = s32[16,512]{1,0:T(8,128)S(1)} copy-done((s32[16,512]{1,0:T(8,128)S(1)}, s32[16,512]{1,0:T(8,128)}, u32[]{:S(2)}) %copy-start.7) | copy-done | bytes 32792
  8.4 0.8 %pack_tracer_edges.1 = (f32[24,256]{1,0:T(8,128)S(1)}, f32[35,8,512]{2,1,0:T(8,128)S(1)}, f32[32,8,512]{2,1,0:T(8,128)S(1)}) custom-call(f32[24,256]{1,0:T(8,128)S(1)} %get-tuple-element.21.high_ref, f32[8,16,16,512]{3,2,1,0:T(8,128)S(1)} %copy-done, s32[16,512]{1,0:T(8,128)S(1)} %copy-done.4, s32[16,512]{1,0:T(8,128)S(1)} %copy-done.7, ...), custom_call_target="tpu_custom_call" | custom-call | tf_op jit(solution)/shard_map/pack_tracer_edges/pallas_call | solution.py:569
  9.2 0.5 collective-permute-start.7
  9.7 5.1 %collective-permute-start.8 = (f32[32,8,512]{2,1,0:T(8,128)S(1)}, f32[32,8,512]{2,1,0:T(8,128)S(1)}, u32[]{:S(2)}, u32[]{:S(2)}) collective-permute-start(f32[32,8,512]{2,1,0:T(8,128)S(1)} %get-tuple-element.34.own_west_ref), channel_id=1, source_target_pairs={{1,0},{2,1},{3,2},{4,3},{5,4},{6,5},{7,6},{8,7},{9,8},{10,9},{11,1... | collective-permute-start | bytes 1572872 | tf_op jit(solution)/shard_map/ppermute | solution.py:603
  14.7 1.4 %collective-permute-start.1 = (f32[24,256]{1,0:T(8,128)S(1)}, f32[24,256]{1,0:T(8,128)S(1)}, u32[]{:S(2)}, u32[]{:S(2)}) collective-permute-start(f32[24,256]{1,0:T(8,128)S(1)} %get-tuple-element.22), channel_id=1, source_target_pairs={{1,0},{2,1},{3,2},{4,3},{5,4},{6,5},{7,6},{8,7},{9,8},{10,9},{11,1... | collective-permute-start | bytes 73736 | tf_op jit(solution)/shard_map/ppermute | solution.py:590
  16.2 3.0 %collective-permute-start = (f32[24,256]{1,0:T(8,128)S(1)}, f32[24,256]{1,0:T(8,128)S(1)}, u32[]{:S(2)}, u32[]{:S(2)}) collective-permute-start(f32[24,256]{1,0:T(8,128)S(1)} %get-tuple-element.21.high_ref), channel_id=1, source_target_pairs={{0,1},{1,2},{2,3},{3,4},{4,5},{5,6},{6,7},{7,8},{8,9},{9,10},{10,1... | collective-permute-start | bytes 73736 | tf_op jit(solution)/shard_map/ppermute | solution.py:589
  19.2 2.4 %sources.1._.before_ref = f32[8,16,16,512]{3,2,1,0:T(8,128)S(1)} custom-call(f32[8,16,16,512]{3,2,1,0:T(8,128)S(1)} %copy-done.1, s32[16,512]{1,0:T(8,128)S(1)} %copy-done.4), custom_call_target="tpu_custom_call" | custom-call | flops 73400320 | bytes 8388608 | tf_op jit(solution)/shard_map/sources/pallas_call | solution.py:569
  21.7 0.0 copy-start.6
  21.7 0.0 collective-permute-done.1.above_ref
  21.7 0.0 collective-permute-done.below_ref
  21.7 0.5 solver_basis.1
  22.2 5.7 %collective-permute-start.2 = (f32[8,24,128]{2,1,0:T(8,128)S(1)}, f32[8,24,128]{2,1,0:T(8,128)S(1)}, u32[]{:S(2)}, u32[]{:S(2)}) collective-permute-start(f32[8,24,128]{2,1,0:T(8,128)S(1)} %get-tuple-element.25), channel_id=1, source_target_pairs={{0,1},{1,0},{2,3},{3,2},{4,5},{5,4},{6,7},{7,6},{8,9},{9,8},{10,11... | collective-permute-start | bytes 294920 | tf_op jit(solution)/shard_map/ppermute | solution.py:614
  27.9 0.9 %collective-permute-done.2.came_ref = f32[8,24,128]{2,1,0:T(8,128)S(1)} collective-permute-done((f32[8,24,128]{2,1,0:T(8,128)S(1)}, f32[8,24,128]{2,1,0:T(8,128)S(1)}, u32[]{:S(2)}, u32[]{:S(2)}) %collective-permute-start.2) | collective-permute-done | bytes 98336 | tf_op jit(solution)/shard_map/ppermute | solution.py:614
  28.9 0.6 collective-permute-start.3
  29.4 4.6 %collective-permute-done.3.came_ref = f32[4,2,24,128]{3,2,1,0:T(8,128)S(1)} collective-permute-done((f32[4,2,24,128]{3,2,1,0:T(8,128)S(1)}, f32[4,2,24,128]{3,2,1,0:T(8,128)S(1)}, u32[]{:S(2)}, u32[]{:S(2)}) %collective-permute-start.3) | collective-permute-done | bytes 98336 | tf_op jit(solution)/shard_map/ppermute | solution.py:617
  34.0 1.0 %collective-permute-start.4 = (f32[4,24,128]{2,1,0:T(8,128)S(1)}, f32[4,24,128]{2,1,0:T(8,128)S(1)}, u32[]{:S(2)}, u32[]{:S(2)}) collective-permute-start(f32[4,24,128]{2,1,0:T(8,128)S(1)} %get-tuple-element.29), channel_id=1, source_target_pairs={{0,4},{1,5},{2,6},{3,7},{4,8},{5,9},{6,10},{7,11},{8,12},{9,13},{1... | collective-permute-start | bytes 147464 | tf_op jit(solution)/shard_map/ppermute | solution.py:635
  35.0 2.6 %collective-permute-start.5 = (f32[4,24,128]{2,1,0:T(8,128)S(1)}, f32[4,24,128]{2,1,0:T(8,128)S(1)}, u32[]{:S(2)}, u32[]{:S(2)}) collective-permute-start(f32[4,24,128]{2,1,0:T(8,128)S(1)} %get-tuple-element.30), channel_id=1, source_target_pairs={{0,8},{1,9},{2,10},{3,11},{4,12},{5,13},{6,14},{7,15},{8,0},{9,1},... | collective-permute-start | bytes 147464 | tf_op jit(solution)/shard_map/ppermute | solution.py:635
  37.6 1.3 %collective-permute-start.6 = (f32[4,24,128]{2,1,0:T(8,128)S(1)}, f32[4,24,128]{2,1,0:T(8,128)S(1)}, u32[]{:S(2)}, u32[]{:S(2)}) collective-permute-start(f32[4,24,128]{2,1,0:T(8,128)S(1)} %get-tuple-element.31), channel_id=1, source_target_pairs={{0,12},{1,13},{2,14},{3,15},{4,0},{5,1},{6,2},{7,3},{8,4},{9,5},{1... | collective-permute-start | bytes 147464 | tf_op jit(solution)/shard_map/ppermute | solution.py:635
  39.0 9.9 %north_fluxes.1 = (f32[8,16,16,512]{3,2,1,0:T(8,128)S(1)}, f32[8,16,16,512]{3,2,1,0:T(8,128)S(1)}) custom-call(f32[8,16,16,512]{3,2,1,0:T(8,128)S(1)} %copy-done.1, s32[16,512]{1,0:T(8,128)S(1)} %copy-done.4, f32[16,16,512]{2,1,0:T(8,128)S(1)} %copy-done.6, f32[8,16,16,512]{3,2,1,0:T(8,128)S(1)} %sources.1._.before_ref, ...), custom_call_target="tpu_custom_call" | custom-call | flops 73400320 | bytes 8388608 | tf_op jit(solution)/shard_map/north_fluxes/pallas_call | solution.py:569
  48.8 0.0 collective-permute-done.8.from_east_ref
  48.8 0.0 collective-permute-done.7.from_west_ref
  48.9 3.0 %east_fluxes.1 = (f32[8,16,16,512]{3,2,1,0:T(8,128)S(1)}, f32[8,16,16,512]{3,2,1,0:T(8,128)S(1)}, f32[16,8,512]{2,1,0:T(8,128)S(1)}) custom-call(f32[8,16,16,512]{3,2,1,0:T(8,128)S(1)} %copy-done.1, s32[16,512]{1,0:T(8,128)S(1)} %copy-done.5, s32[16,512]{1,0:T(8,128)S(1)} %copy-done.8, f32[16,16,512]{2,1,0:T(8,128)S(1)} %copy-done.3, ...), custom_call_target="tpu_custom_call" | custom-call | flops 73400320 | bytes 8388608 | tf_op jit(solution)/shard_map/east_fluxes/pallas_call | solution.py:569
  51.9 0.0 collective-permute-done.4.refs_1_
  51.9 6.2 %surface_update.1 = (f32[32,256]{1,0:T(8,128)}, f32[8,16,16,512]{3,2,1,0:T(8,128)}) custom-call(f32[4,24,128]{2,1,0:T(8,128)S(1)} %get-tuple-element.28._.refs_0_, f32[4,24,128]{2,1,0:T(8,128)S(1)} %collective-permute-done.4.refs_1_, f32[4,24,128]{2,1,0:T(8,128)S(1)} %collective-permute-done.5.refs_2_, f32[4,24,128]{2,1,0:T(8,128)S(1)} %collective-permute-done.6.refs_3_, ...), custom_call_target="tpu_custom_call" | custom-call | tf_op jit(solution)/shard_map/surface_update/pallas_call | solution.py:569
  (29 shorter events, 0.1 us)
Async XLA Ops:
  0.6 0.8 %copy-start.9 = (f32[32,256]{1,0:T(8,128)S(1)}, f32[32,256]{1,0:T(8,128)}, u32[]{:S(2)}) copy-start(f32[32,256]{1,0:T(8,128)} %old_ref.3) | copy-start | bytes 98308
  1.4 0.8 %copy-start.11 = (f32[32,256]{1,0:T(8,128)S(1)}, f32[32,256]{1,0:T(8,128)}, u32[]{:S(2)}) copy-start(f32[32,256]{1,0:T(8,128)} %force_ref.3) | copy-start | bytes 98308
  2.1 0.8 %copy-start.13 = (f32[32,256]{1,0:T(8,128)S(1)}, f32[32,256]{1,0:T(8,128)}, u32[]{:S(2)}) copy-start(f32[32,256]{1,0:T(8,128)} %coeff_ref.3) | copy-start | bytes 98308
  2.9 0.8 %copy-start.15 = (s32[32,256]{1,0:T(8,128)S(1)}, s32[32,256]{1,0:T(8,128)}, u32[]{:S(2)}) copy-start(s32[32,256]{1,0:T(8,128)} %mask_ref.3) | copy-start | bytes 98308
  3.7 2.2 %copy-start = (f32[8,16,16,512]{3,2,1,0:T(8,128)S(1)}, f32[8,16,16,512]{3,2,1,0:T(8,128)}, u32[]{:S(2)}) copy-start(f32[8,16,16,512]{3,2,1,0:T(8,128)} %tracers_ref.7) | copy-start | bytes 12582916
  5.9 1.0 %copy-start.2 = (f32[16,16,512]{2,1,0:T(8,128)S(1)}, f32[16,16,512]{2,1,0:T(8,128)}, u32[]{:S(2)}) copy-start(f32[16,16,512]{2,1,0:T(8,128)} %u_ref.3) | copy-start | bytes 1572868
  6.9 0.8 %copy-start.4 = (s32[16,512]{1,0:T(8,128)S(1)}, s32[16,512]{1,0:T(8,128)}, u32[]{:S(2)}) copy-start(s32[16,512]{1,0:T(8,128)} %depth_ref.7) | copy-start | bytes 98308
  7.7 0.8 %copy-start.7 = (s32[16,512]{1,0:T(8,128)S(1)}, s32[16,512]{1,0:T(8,128)}, u32[]{:S(2)}) copy-start(s32[16,512]{1,0:T(8,128)} %east_depth_ref.3) | copy-start | bytes 98308
  8.4 10.8 %copy-start.1 = (f32[8,16,16,512]{3,2,1,0:T(8,128)S(1)}, f32[8,16,16,512]{3,2,1,0:T(8,128)}, u32[]{:S(2)}) copy-start(f32[8,16,16,512]{3,2,1,0:T(8,128)} %tracers_ref.7) | copy-start | bytes 12582916
  9.2 39.6 %collective-permute-start.7 = (f32[35,8,512]{2,1,0:T(8,128)S(1)}, f32[35,8,512]{2,1,0:T(8,128)S(1)}, u32[]{:S(2)}, u32[]{:S(2)}) collective-permute-start(f32[35,8,512]{2,1,0:T(8,128)S(1)} %get-tuple-element.33), channel_id=1, source_target_pairs={{0,1},{1,2},{2,3},{3,4},{4,5},{5,6},{6,7},{7,8},{8,9},{9,10},{10,1... | collective-permute-start | bytes 1720328 | tf_op jit(solution)/shard_map/ppermute | solution.py:602
  9.7 39.2 %collective-permute-start.8 = (f32[32,8,512]{2,1,0:T(8,128)S(1)}, f32[32,8,512]{2,1,0:T(8,128)S(1)}, u32[]{:S(2)}, u32[]{:S(2)}) collective-permute-start(f32[32,8,512]{2,1,0:T(8,128)S(1)} %get-tuple-element.34.own_west_ref), channel_id=1, source_target_pairs={{1,0},{2,1},{3,2},{4,3},{5,4},{6,5},{7,6},{8,7},{9,8},{10,9},{11,1... | collective-permute-start | bytes 1572872 | tf_op jit(solution)/shard_map/ppermute | solution.py:603
  14.7 7.0 %copy-start.10 = (f32[32,256]{1,0:T(8,128)S(1)}, f32[32,256]{1,0:T(8,128)}, u32[]{:S(2)}) copy-start(f32[32,256]{1,0:T(8,128)} %old_ref.3) | copy-start | bytes 98308
  14.7 7.0 %copy-start.12 = (f32[32,256]{1,0:T(8,128)S(1)}, f32[32,256]{1,0:T(8,128)}, u32[]{:S(2)}) copy-start(f32[32,256]{1,0:T(8,128)} %force_ref.3) | copy-start | bytes 98308
  14.7 7.0 %copy-start.14 = (f32[32,256]{1,0:T(8,128)S(1)}, f32[32,256]{1,0:T(8,128)}, u32[]{:S(2)}) copy-start(f32[32,256]{1,0:T(8,128)} %coeff_ref.3) | copy-start | bytes 98308
  14.7 7.0 %copy-start.16 = (s32[32,256]{1,0:T(8,128)S(1)}, s32[32,256]{1,0:T(8,128)}, u32[]{:S(2)}) copy-start(s32[32,256]{1,0:T(8,128)} %mask_ref.3) | copy-start | bytes 98308
  14.7 6.9 %collective-permute-start.1 = (f32[24,256]{1,0:T(8,128)S(1)}, f32[24,256]{1,0:T(8,128)S(1)}, u32[]{:S(2)}, u32[]{:S(2)}) collective-permute-start(f32[24,256]{1,0:T(8,128)S(1)} %get-tuple-element.22), channel_id=1, source_target_pairs={{1,0},{2,1},{3,2},{4,3},{5,4},{6,5},{7,6},{8,7},{9,8},{10,9},{11,1... | collective-permute-start | bytes 73736 | tf_op jit(solution)/shard_map/ppermute | solution.py:590
  16.2 5.5 %collective-permute-start = (f32[24,256]{1,0:T(8,128)S(1)}, f32[24,256]{1,0:T(8,128)S(1)}, u32[]{:S(2)}, u32[]{:S(2)}) collective-permute-start(f32[24,256]{1,0:T(8,128)S(1)} %get-tuple-element.21.high_ref), channel_id=1, source_target_pairs={{0,1},{1,2},{2,3},{3,4},{4,5},{5,6},{6,7},{7,8},{8,9},{9,10},{10,1... | collective-permute-start | bytes 73736 | tf_op jit(solution)/shard_map/ppermute | solution.py:589
  21.7 17.3 %copy-start.6 = (f32[16,16,512]{2,1,0:T(8,128)S(1)}, f32[16,16,512]{2,1,0:T(8,128)}, u32[]{:S(2)}) copy-start(f32[16,16,512]{2,1,0:T(8,128)} %v_ref.1) | copy-start | bytes 1572868
  22.2 6.6 %collective-permute-start.2 = (f32[8,24,128]{2,1,0:T(8,128)S(1)}, f32[8,24,128]{2,1,0:T(8,128)S(1)}, u32[]{:S(2)}, u32[]{:S(2)}) collective-permute-start(f32[8,24,128]{2,1,0:T(8,128)S(1)} %get-tuple-element.25), channel_id=1, source_target_pairs={{0,1},{1,0},{2,3},{3,2},{4,5},{5,4},{6,7},{7,6},{8,9},{9,8},{10,11... | collective-permute-start | bytes 294920 | tf_op jit(solution)/shard_map/ppermute | solution.py:614
  28.9 5.1 %collective-permute-start.3 = (f32[4,2,24,128]{3,2,1,0:T(8,128)S(1)}, f32[4,2,24,128]{3,2,1,0:T(8,128)S(1)}, u32[]{:S(2)}, u32[]{:S(2)}) collective-permute-start(f32[4,2,24,128]{3,2,1,0:T(8,128)S(1)} %get-tuple-element.27), channel_id=1, source_target_pairs={{0,2},{1,3},{2,0},{3,1},{4,6},{5,7},{6,4},{7,5},{8,10},{9,11},{10,... | collective-permute-start | bytes 294920 | tf_op jit(solution)/shard_map/ppermute | solution.py:617
  34.0 17.9 %collective-permute-start.4 = (f32[4,24,128]{2,1,0:T(8,128)S(1)}, f32[4,24,128]{2,1,0:T(8,128)S(1)}, u32[]{:S(2)}, u32[]{:S(2)}) collective-permute-start(f32[4,24,128]{2,1,0:T(8,128)S(1)} %get-tuple-element.29), channel_id=1, source_target_pairs={{0,4},{1,5},{2,6},{3,7},{4,8},{5,9},{6,10},{7,11},{8,12},{9,13},{1... | collective-permute-start | bytes 147464 | tf_op jit(solution)/shard_map/ppermute | solution.py:635
  35.0 16.9 %collective-permute-start.5 = (f32[4,24,128]{2,1,0:T(8,128)S(1)}, f32[4,24,128]{2,1,0:T(8,128)S(1)}, u32[]{:S(2)}, u32[]{:S(2)}) collective-permute-start(f32[4,24,128]{2,1,0:T(8,128)S(1)} %get-tuple-element.30), channel_id=1, source_target_pairs={{0,8},{1,9},{2,10},{3,11},{4,12},{5,13},{6,14},{7,15},{8,0},{9,1},... | collective-permute-start | bytes 147464 | tf_op jit(solution)/shard_map/ppermute | solution.py:635
  37.6 11.2 %copy-start.3 = (f32[16,16,512]{2,1,0:T(8,128)S(1)}, f32[16,16,512]{2,1,0:T(8,128)}, u32[]{:S(2)}) copy-start(f32[16,16,512]{2,1,0:T(8,128)} %u_ref.3) | copy-start | bytes 1572868
  37.6 11.2 %copy-start.5 = (s32[16,512]{1,0:T(8,128)S(1)}, s32[16,512]{1,0:T(8,128)}, u32[]{:S(2)}) copy-start(s32[16,512]{1,0:T(8,128)} %depth_ref.7) | copy-start | bytes 98308
  37.6 11.3 %copy-start.8 = (s32[16,512]{1,0:T(8,128)S(1)}, s32[16,512]{1,0:T(8,128)}, u32[]{:S(2)}) copy-start(s32[16,512]{1,0:T(8,128)} %east_depth_ref.3) | copy-start | bytes 98308
  37.6 14.3 %collective-permute-start.6 = (f32[4,24,128]{2,1,0:T(8,128)S(1)}, f32[4,24,128]{2,1,0:T(8,128)S(1)}, u32[]{:S(2)}, u32[]{:S(2)}) collective-permute-start(f32[4,24,128]{2,1,0:T(8,128)S(1)} %get-tuple-element.31), channel_id=1, source_target_pairs={{0,12},{1,13},{2,14},{3,15},{4,0},{5,1},{6,2},{7,3},{8,4},{9,5},{1... | collective-permute-start | bytes 147464 | tf_op jit(solution)/shard_map/ppermute | solution.py:635

commit v3 on v2

--- a/solution.py
+++ b/solution.py
@@ -1,5 +1,3 @@
-import functools
-
 import jax
 import jax.numpy as jnp
 from jax import lax
@@ -23,7 +21,7 @@
 
 SUBLANES = 8
 LANES = 128
-SMALL_VMEM = 8 * 2**20
+SMALL_VMEM = 4 * 2**20
 RESULT_VMEM = 14 * 2**20
 HALO = 8
 SLAB_ROWS = 24
@@ -33,7 +31,18 @@
 PIVOT_FLOOR = 3e-7
 
 
-def pack_kernel(old_ref, force_ref, coeff_ref, mask_ref, low_ref, high_ref):
+def pack_kernel(old_in, force_in, coeff_in, mask_in, low_ref, high_ref, own_ref, *scratch):
+    old_ref, force_ref, coeff_ref, mask_ref, sems = scratch
+    copies = [
+        pltpu.make_async_copy(source, target, sems.at[place])
+        for place, (source, target) in enumerate(
+            zip((old_in, force_in, coeff_in, mask_in), (old_ref, force_ref, coeff_ref, mask_ref))
+        )
+    ]
+    for copy in copies:
+        copy.start()
+    for copy in copies:
+        copy.wait()
     rows = old_ref.shape[0]
     coeff = coeff_ref[...]
     fields = (
@@ -44,35 +53,30 @@
     for place, field in enumerate(fields):
         low_ref[HALO * place : HALO * (place + 1)] = field[:HALO]
         high_ref[HALO * place : HALO * (place + 1)] = field[rows - HALO :]
+        own_ref[rows * place : rows * (place + 1)] = field
 
 
 def basis_kernel(
-    old_ref,
-    force_ref,
-    coeff_ref,
-    mask_ref,
+    own_ref,
     below_ref,
     above_ref,
     folded_ref,
-    _,
-    keep_ref,
-    send_ref,
     basis_ref,
+    *refs,
 ):
-    rows, width = old_ref.shape
-    count = 2 * keep_ref.shape[0]
+    send_refs, slabs_ref = refs[:-1], refs[-1]
+    rows, width = own_ref.shape[0] // 3, own_ref.shape[1]
+    count = slabs_ref.shape[0]
     columns = width // count
     top_device = lax.axis_index("lon") == count - 1
     above = jnp.where(top_device, folded_ref[...], above_ref[...])
 
-    def extended(place, own):
+    def extended(place):
         part = slice(HALO * place, HALO * (place + 1))
+        own = own_ref[rows * place : rows * (place + 1)]
         return jnp.concatenate([below_ref[part], own, above[part]], axis=0)
 
-    coeff_own = coeff_ref[...]
-    first = extended(0, coeff_own * old_ref[...] + force_ref[...])
-    coeff = extended(1, coeff_own)
-    mask = extended(2, mask_ref[...].astype(jnp.float32))
+    first, coeff, mask = extended(0), extended(1), extended(2)
     diagonal = (coeff + 4.0 * mask - CENTRE) * (1.0 / SPREAD)
     beside = mask * (1.0 / SPREAD)
     total = rows + 2 * HALO
@@ -106,8 +110,6 @@
             [stacked, jnp.zeros((LANES - BASIS * rows, width), jnp.float32)], axis=0
         )
     turned = stacked.T
-    core = lax.rem(lax.axis_index("lon"), 2)
-    slabs = []
     for target in range(count):
         start = target * columns
         east = (start + columns) % width
@@ -119,43 +121,34 @@
             moments,
             jnp.zeros((SLAB_ROWS - columns - 3, LANES), jnp.float32),
         ]
-        slabs.append(jnp.concatenate(pieces, axis=0))
-    for pair in range(count // 2):
-        even, odd = slabs[2 * pair], slabs[2 * pair + 1]
-        keep_ref[pair] = jnp.where(core == 0, even, odd)
-        send_ref[pair] = jnp.where(core == 0, odd, even)
-
-
-def split_kernel(kept_ref, came_ref, keep_ref, send_ref):
+        slabs_ref[target] = jnp.concatenate(pieces, axis=0)
+    groups = len(send_refs)
+    group = lax.axis_index("lon") // 4
+    for step in range(groups):
+        target = lax.rem(group + step, groups)
+        for place in range(4):
+            send_refs[step][place] = slabs_ref[4 * target + place]
+
+
+def core_kernel(*refs):
+    came_refs, (_, keep_ref, send_ref) = refs[:-3], refs[-3:]
+    here = lax.axis_index("lon")
+    core, group = lax.rem(here, 2), here // 4
+    groups = len(came_refs)
+    for step in range(groups):
+        source = lax.rem(group + groups - step, groups)
+        for y in range(2):
+            keep_ref[y, source] = came_refs[step][2 * y + core]
+            send_ref[y, source] = came_refs[step][2 * y + 1 - core]
+
+
+def half_kernel(kept_ref, came_ref, keep_ref, send_ref):
     here = lax.axis_index("lon")
     core, half = lax.rem(here, 2), lax.rem(here // 2, 2)
-    for group in range(keep_ref.shape[0]):
-        for y in range(2):
-            mine, other = kept_ref[2 * group + y], came_ref[2 * group + y]
-            first = jnp.where(core == 0, mine, other)
-            second = jnp.where(core == 0, other, mine)
-
-            @pl.when(half == y)
-            def _():
-                keep_ref[group, 0] = first
-                keep_ref[group, 1] = second
-
-            @pl.when(half != y)
-            def _():
-                send_ref[group, 0] = first
-                send_ref[group, 1] = second
-
-
-def spread_kernel(kept_ref, came_ref, *out_refs):
-    here = lax.axis_index("lon")
-    half, group = lax.rem(here // 2, 2), here // 4
-    groups = len(out_refs)
-    for step in range(groups):
-        target = lax.rem(group + step, groups)
-        for core in range(2):
-            mine, other = kept_ref[target, core], came_ref[target, core]
-            out_refs[step][core] = jnp.where(half == 0, mine, other)
-            out_refs[step][2 + core] = jnp.where(half == 0, other, mine)
+    keep_ref[core] = kept_ref[half]
+    keep_ref[1 - core] = came_ref[half]
+    send_ref[core] = kept_ref[1 - half]
+    send_ref[1 - core] = came_ref[1 - half]
 
 
 def basis_weights(moments):
@@ -213,44 +206,72 @@
     return tile
 
 
-def edge_kernel(
+def load_kernel(
     high_ref,
+    tracers_in,
+    depth_in,
+    east_depth_in,
+    u_in,
+    v_in,
+    folded_ref,
     tracers_ref,
     depth_ref,
     east_depth_ref,
     u_ref,
-    folded_ref,
-    east_going_ref,
-    west_going_ref,
+    v_ref,
+    sems,
 ):
+    kinds = tracers_ref.shape[0]
+    copies = [
+        pltpu.make_async_copy(source, target, sems.at[place])
+        for place, (source, target) in enumerate(
+            [
+                (depth_in, depth_ref),
+                (east_depth_in, east_depth_ref),
+                (u_in, u_ref),
+                (v_in, v_ref),
+            ]
+            + [(tracers_in.at[kind], tracers_ref.at[kind]) for kind in range(kinds)]
+        )
+    ]
+    for copy in copies:
+        copy.start()
     tiles = high_ref.shape[1] // LANES
     for place in range(3):
-        rows = slice(HALO * place, HALO * (place + 1))
+        part = slice(HALO * place, HALO * (place + 1))
         for tile in range(tiles):
             other = tiles - 1 - tile
-            folded_ref[rows, tile * LANES : (tile + 1) * LANES] = reverse_tile(
-                high_ref[rows, other * LANES : (other + 1) * LANES]
+            folded_ref[part, tile * LANES : (tile + 1) * LANES] = reverse_tile(
+                high_ref[part, other * LANES : (other + 1) * LANES]
             )
+    for copy in copies:
+        copy.wait()
+
+
+def edge_kernel(
+    tracers_ref, depth_ref, east_depth_ref, u_ref, _, east_going_ref, west_going_ref
+):
     kinds, levels, columns, rows = tracers_ref.shape
     for z in range(levels):
-        for side in range(2):
-            column = columns - 2 + side
-            west_wet = (z < depth_ref[side : side + 1]).astype(jnp.float32)
-            east_wet = (z < depth_ref[column : column + 1]).astype(jnp.float32)
-            for kind in range(kinds):
+        place = 2 * levels + z // SUBLANES
+        row = z % SUBLANES
+        east_going_ref[place, row : row + 1] = u_ref[z, columns - 1 : columns]
+    place = 2 * levels + levels // SUBLANES
+    east_going_ref[place] = jnp.broadcast_to(
+        east_depth_ref[columns - 1 : columns].astype(jnp.float32), (SUBLANES, rows)
+    )
+    for kind in range(kinds):
+        for z in range(levels):
+            for side in range(2):
+                column = columns - 2 + side
+                west_wet = (z < depth_ref[side : side + 1]).astype(jnp.float32)
+                east_wet = (z < depth_ref[column : column + 1]).astype(jnp.float32)
                 west_going_ref[2 * z + side, kind : kind + 1] = (
                     tracers_ref[kind, z, side : side + 1] * west_wet
                 )
                 east_going_ref[2 * z + side, kind : kind + 1] = (
                     tracers_ref[kind, z, column : column + 1] * east_wet
                 )
-        place = 2 * levels + z // SUBLANES
-        row = z % SUBLANES
-        east_going_ref[place, row : row + 1] = u_ref[z, columns - 1 : columns]
-    place = 2 * levels + levels // SUBLANES
-    east_going_ref[place] = jnp.broadcast_to(
-        east_depth_ref[columns - 1 : columns].astype(jnp.float32), (SUBLANES, rows)
-    )
 
 
 def grid_tiles(columns, rows):
@@ -329,7 +350,7 @@
     )
 
 
-def source_kernel(tracers_ref, depth_ref, base_ref):
+def source_kernel(tracers_ref, depth_ref, _, base_ref):
     kinds, levels, columns, rows = tracers_ref.shape
     places = grid_tiles(columns, rows)
 
@@ -353,39 +374,78 @@
                 base_ref[(kind, level) + at] = value + (wet * sources[kind] + (down - up))
 
 
-def north_kernel(tracers_ref, depth_ref, v_ref, before_ref, _, base_ref, face_north_ref, north_ref):
+def north_kernel(
+    tracers_ref,
+    depth_ref,
+    v_ref,
+    before_ref,
+    base_ref,
+    face_ref,
+    face_south_ref,
+    band_ref,
+    north_ref,
+    south_ref,
+):
     kinds, levels, columns, rows = tracers_ref.shape
     blocks, count = columns // SUBLANES, rows // LANES
     places = grid_tiles(columns, rows)
+    source = lax.broadcasted_iota(jnp.int32, (rows, rows), 0)
+    target = lax.broadcasted_iota(jnp.int32, (rows, rows), 1)
+    for place, moved in enumerate((0, 1)):
+        offset = source - target + moved
+        near = (offset == 0) | (offset == 1)
+        far = (offset == -1) | (offset == 2)
+        band = jnp.where(near, 7.0, jnp.where(far, -1.0, 0.0))
+        band_ref[:, place * rows : (place + 1) * rows] = band.astype(jnp.bfloat16)
     depth = {p: depth_ref[tile_index(p)].astype(jnp.float32) for p in places}
-    north_depth = shift_rows(depth, 1, blocks, count)
+    depth_north = shift_rows(depth, 1, blocks, count)
+    depth_south = shift_rows(depth, -1, blocks, count)
     for p in places:
-        north_ref[tile_index(p)] = jnp.minimum(depth[p], north_depth[p]).astype(jnp.int32)
+        at = tile_index(p)
+        north_ref[at] = jnp.minimum(depth[p], depth_north[p]).astype(jnp.int32)
+        south_ref[at] = jnp.minimum(depth[p], depth_south[p]).astype(jnp.int32)
 
     @pl.loop(0, levels)
     def _(level):
-        wet, scale, mix = {}, {}, {}
+        wet, scale, mix, scale_s, mix_s, flow = {}, {}, {}, {}, {}, {}
         for p in places:
             at = tile_index(p)
             wet[p] = jnp.where(level < depth_ref[at], 1.0, 0.0)
             is_open = level < north_ref[at]
             scale[p] = jnp.where(is_open, 1.0 / 12.0, 0.0)
             mix[p] = jnp.where(is_open, HORIZ_DIFF, 0.0)
+            is_open = level < south_ref[at]
+            scale_s[p] = jnp.where(is_open, 1.0 / 12.0, 0.0)
+            mix_s[p] = jnp.where(is_open, HORIZ_DIFF, 0.0)
+            flow[p] = v_ref[(level,) + at]
+        flow_s = shift_rows(flow, -1, blocks, count)
+        wet_full = jnp.where(level < depth_ref[...], 1.0, 0.0)
+        masked_full = [tracers_ref[kind, level] * wet_full for kind in range(kinds)]
+        whole = jnp.concatenate(masked_full, axis=0)
+        first = whole.astype(jnp.bfloat16)
+        second = (whole - first.astype(jnp.float32)).astype(jnp.bfloat16)
+        weights = band_ref[...]
+        faces = jnp.dot(first, weights, preferred_element_type=jnp.float32) + jnp.dot(
+            second, weights, preferred_element_type=jnp.float32
+        )
         for kind in range(kinds):
-            masked = {p: tracers_ref[(kind, level) + tile_index(p)] * wet[p] for p in places}
-            one = shift_rows(masked, 1, blocks, count)
-            two = shift_rows(one, 1, blocks, count)
+            masked = {p: masked_full[kind][tile_index(p)] for p in places}
+            north = shift_rows(masked, 1, blocks, count)
             south = shift_rows(masked, -1, blocks, count)
-            flux = {}
             for p in places:
-                at = (kind, level) + tile_index(p)
-                face = (7.0 * (masked[p] + one[p]) - (south[p] + two[p])) * scale[p]
-                face_north_ref[at] = face
-                flux[p] = v_ref[(level,) + tile_index(p)] * face - mix[p] * (one[p] - masked[p])
-            incoming = shift_rows(flux, -1, blocks, count)
-            for p in places:
-                at = (kind, level) + tile_index(p)
-                base_ref[at] = before_ref[at] + (incoming[p] - flux[p])
+                rows_at, lanes_at = tile_index(p)
+                at = (kind, level, rows_at, lanes_at)
+                row = kind * columns + rows_at.start
+                picked = faces[row : row + SUBLANES]
+                face = picked[:, lanes_at] * scale[p]
+                face_south = (
+                    picked[:, rows + lanes_at.start : rows + lanes_at.stop] * scale_s[p]
+                )
+                face_ref[at] = face
+                face_south_ref[at] = face_south
+                flux = flow[p] * face - mix[p] * (north[p] - masked[p])
+                flux_south = flow_s[p] * face_south - mix_s[p] * (masked[p] - south[p])
+                base_ref[at] = before_ref[at] + (flux_south - flux)
 
 
 def east_kernel(
@@ -453,15 +513,26 @@
                 base_ref[at] = before_ref[at] + (incoming[p] - flux[p])
 
 
-def update_kernel(groups, *refs):
-    came_refs, refs = refs[:groups], refs[groups:]
-    basis_ref, base_ref, face_east_ref, face_north_ref, face_west_ref = refs[:5]
-    surface_ref, out_ref, slabs_ref, result_ref, sems = refs[5:]
-    group = lax.axis_index("lon") // 4
-    for step in range(groups):
-        source = lax.rem(group + groups - step, groups)
-        for place in range(4):
-            slabs_ref[4 * source + place] = came_refs[step][place]
+def update_kernel(
+    kept_ref,
+    came_ref,
+    basis_ref,
+    base_ref,
+    face_east_ref,
+    face_north_ref,
+    face_south_ref,
+    face_west_ref,
+    surface_ref,
+    out_ref,
+    slabs_ref,
+    result_ref,
+    sems,
+):
+    half = lax.rem(lax.axis_index("lon") // 2, 2)
+    for source in range(kept_ref.shape[1]):
+        for core in range(2):
+            slabs_ref[4 * source + 2 * half + core] = kept_ref[core, source]
+            slabs_ref[4 * source + 2 * (1 - half) + core] = came_ref[core, source]
     kinds, levels, columns, rows = base_ref.shape
     blocks, count = columns // SUBLANES, rows // LANES
     places = grid_tiles(columns, rows)
@@ -505,6 +576,7 @@
     height_north = shift_rows(height, 1, blocks, count)
     flow_east = {p: -BARO_GAIN * (height_east[p] - height[p]) for p in places}
     flow_north = {p: -BARO_GAIN * (height_north[p] - height[p]) for p in places}
+    flow_south = shift_rows(flow_north, -1, blocks, count)
     flow_west = [
         -BARO_GAIN * (jnp.broadcast_to(height[0, tile][:1], (SUBLANES, LANES)) - west_edge[tile])
         for tile in range(count)
@@ -516,11 +588,9 @@
     for kind in range(kinds):
         @pl.loop(0, levels, unroll=4)
         def _(level):
-            flux_east, flux_north = {}, {}
-            for p in places:
-                at = (kind, level) + tile_index(p)
-                flux_east[p] = flow_east[p] * face_east_ref[at]
-                flux_north[p] = flow_north[p] * face_north_ref[at]
+            flux_east = {
+                p: flow_east[p] * face_east_ref[(kind, level) + tile_index(p)] for p in places
+            }
             edge = [
                 flow_west[tile]
                 * jnp.broadcast_to(
@@ -530,11 +600,11 @@
                 for tile in range(count)
             ]
             from_west = shift_columns(flux_east, -1, edge, blocks, count)
-            from_south = shift_rows(flux_north, -1, blocks, count)
             for p in places:
                 at = (kind, level) + tile_index(p)
                 result_ref[at] = base_ref[at] + (
-                    (from_west[p] - flux_east[p]) + (from_south[p] - flux_north[p])
+                    (from_west[p] - flux_east[p])
+                    + (flow_south[p] * face_south_ref[at] - flow_north[p] * face_north_ref[at])
                 )
 
         copy(kind).start()
@@ -559,17 +629,20 @@
     f32 = jnp.float32
     sds = jax.ShapeDtypeStruct
     vmem = pl.BlockSpec(memory_space=pltpu.VMEM)
+    hbm = pl.BlockSpec(memory_space=pltpu.HBM)
     fields = (surface_old, surface_forcing, surface_coeff, ocean_mask)
     forward = [(i, i + 1) for i in range(count - 1)]
     backward = [(target, source) for source, target in forward]
     ring = [(i, (i + 1) % count) for i in range(count)]
     ring_back = [(target, source) for source, target in ring]
 
-    def call(kernel, out_shape, name, operands, scratch=(), limit=SMALL_VMEM, cost=0):
+    def call(
+        kernel, out_shape, name, operands, scratch=(), limit=SMALL_VMEM, cost=0, far=()
+    ):
         return pl.pallas_call(
             kernel,
             out_shape=out_shape,
-            in_specs=[vmem] * len(operands),
+            in_specs=[hbm if place in far else vmem for place in range(len(operands))],
             out_specs=[pl.BlockSpec(memory_space=pl.ANY) if x is result else vmem for x in out_shape],
             scratch_shapes=list(scratch),
             compiler_params=pltpu.CompilerParams(vmem_limit_bytes=limit),
@@ -579,60 +652,84 @@
             if cost
             else None,
             name=name,
-        )(*operands)
+        )(
+            *(
+                pltpu.with_memory_space_constraint(x, pltpu.HBM) if place in far else x
+                for place, x in enumerate(operands)
+            )
+        )
 
     result = sds(tracers.shape, f32)
     packed = sds((3 * HALO, width), f32)
     held = pltpu.VMEM(tracers.shape, f32)
 
-    low, high = call(pack_kernel, (packed, packed), "pack_edges", fields)
+    low, high, own = call(
+        pack_kernel,
+        (packed, packed, sds((3 * band, width), f32)),
+        "pack_edges",
+        fields,
+        scratch=[pltpu.VMEM(x.shape, x.dtype) for x in fields] + [pltpu.SemaphoreType.DMA((4,))],
+        far=range(4),
+    )
     below = lax.ppermute(high, "lon", forward)
     above = lax.ppermute(low, "lon", backward)
 
-    folded, east_going, own_west = call(
+    def fetched(x):
+        return pltpu.VMEM(x.shape, x.dtype)
+
+    inputs = (tracers, column_depth, east_depth, u_clinic, v_clinic)
+    folded, tracers, column_depth, east_depth, u_clinic, v_clinic = call(
+        load_kernel,
+        (
+            packed,
+            *(fetched(x) for x in inputs),
+        ),
+        "load",
+        (high, *inputs),
+        scratch=[pltpu.SemaphoreType.DMA((4 + kinds,))],
+        far=range(1, 6),
+    )
+    groups = count // 4
+    basis, *sends = call(
+        basis_kernel,
+        (sds((BASIS * band, width), f32),) + (sds((4, SLAB_ROWS, LANES), f32),) * groups,
+        "solver_basis",
+        (own, below, above, folded),
+        scratch=[pltpu.VMEM((count, SLAB_ROWS, LANES), f32)],
+    )
+    slabs = [sends[0]]
+    for step in range(1, groups):
+        pairs = [(i, (i + 4 * step) % count) for i in range(count)]
+        slabs.append(lax.ppermute(sends[step], "lon", pairs))
+    east_going, own_west = call(
         edge_kernel,
         (
-            packed,
             sds((2 * levels + levels // SUBLANES + 1, kinds, rows), f32),
             sds((2 * levels, kinds, rows), f32),
         ),
         "pack_tracer_edges",
-        (high, tracers, column_depth, east_depth, u_clinic),
+        (tracers, column_depth, east_depth, u_clinic, basis),
     )
     from_west = lax.ppermute(east_going, "lon", ring)
     from_east = lax.ppermute(own_west, "lon", ring_back)
-    (base,) = call(source_kernel, (held,), "sources", (tracers, column_depth), cost=70)
-
-    groups = count // 4
-    half_slabs = sds((count // 2, SLAB_ROWS, LANES), f32)
-    keep, send, basis = call(
-        basis_kernel,
-        (half_slabs, half_slabs, sds((BASIS * band, width), f32)),
-        "solver_basis",
-        fields + (below, above, folded, base),
-    )
+    (base,) = call(source_kernel, (held,), "sources", (tracers, column_depth, own_west), cost=70)
+    base, face_north, face_south = call(
+        north_kernel,
+        (held, held, held),
+        "north_fluxes",
+        (tracers, column_depth, v_clinic, base),
+        scratch=[
+            pltpu.VMEM((rows, 2 * rows), jnp.bfloat16),
+            pltpu.VMEM((columns, rows), jnp.int32),
+            pltpu.VMEM((columns, rows), jnp.int32),
+        ],
+        cost=70,
+    )
+    quarter = sds((2, groups, SLAB_ROWS, LANES), f32)
+    keep, send = call(core_kernel, (quarter, quarter), "split_cores", (*slabs, base))
     came = lax.ppermute(send, "lon", [(i, i ^ 1) for i in range(count)])
-    quarter = sds((groups, 2, SLAB_ROWS, LANES), f32)
-    keep, send = call(split_kernel, (quarter, quarter), "split_slabs", (keep, came))
+    keep, send = call(half_kernel, (quarter, quarter), "split_halves", (keep, came))
     came = lax.ppermute(send, "lon", [(i, i ^ 2) for i in range(count)])
-    base, face_north = call(
-        north_kernel,
-        (held, held),
-        "north_fluxes",
-        (tracers, column_depth, v_clinic, base, keep),
-        scratch=[pltpu.VMEM((columns, rows), jnp.int32)],
-        cost=70,
-    )
-    sends = call(
-        spread_kernel,
-        (sds((4, SLAB_ROWS, LANES), f32),) * groups,
-        "spread_slabs",
-        (keep, came),
-    )
-    slabs = [sends[0]]
-    for step in range(1, groups):
-        pairs = [(i, (i + 4 * step) % count) for i in range(count)]
-        slabs.append(lax.ppermute(sends[step], "lon", pairs))
     base, face_east, face_west = call(
         east_kernel,
         (held, held, pltpu.VMEM((levels, kinds, rows), f32)),
@@ -646,17 +743,17 @@
             from_east,
             own_west,
             base,
-            sends[0],
+            keep,
         ),
         scratch=[pltpu.VMEM((levels, kinds, rows), f32)],
         cost=70,
     )
     return tuple(
         call(
-            functools.partial(update_kernel, groups),
+            update_kernel,
             (sds((band, width), f32), result),
             "surface_update",
-            (*slabs, basis, base, face_east, face_north, face_west),
+            (keep, came, basis, base, face_east, face_north, face_south, face_west),
             scratch=[
                 pltpu.VMEM((count, SLAB_ROWS, LANES), f32),
                 pltpu.VMEM(tracers.shape, f32),

time: 58.8 us -> 42.7 us (0.73)
  local copies, waits for them, and re-layouts: 7.8 us -> 0 us
  starting transfers between devices: 21.1 us -> 15.8 us
  waiting for transfers between devices: 5.52 us -> 3.08 us
    unnamed x34 -> x0, local copies, waits for them, and re-layouts: 7.8 us -> none
    ppermute x1, starting transfers between devices: 5.67 us -> 0.07 us  [body(): came = lax.ppermute(send, 'lon', [(i, i ^ 1) for i in range(count)])]
    ppermute x1, waiting for transfers between devices: 4.56 us -> 1.77 us  [body(): came = lax.ppermute(send, 'lon', [(i, i ^ 2) for i in range(count)])]
    ppermute x1, starting transfers between devices: 5.06 us -> 2.48 us  [body(): from_east = lax.ppermute(own_west, 'lon', ring_back)]
    ppermute x1, starting transfers between devices: 0.46 us -> 2.64 us  [body(): from_west = lax.ppermute(east_going, 'lon', ring)]
    ppermute x3, starting transfers between devices: 4.91 us -> 6.19 us  [body(): slabs.append(lax.ppermute(sends[step], 'lon', pairs))]
    pallas_call x9 -> x10, Pallas kernels: 22.8 us -> 22.8 us  [call(): pl.pallas_call(kernel, out_shape=out_shape, in_specs=[hbm if place in far...]
  transfers between devices with their start and end apart: 9 -> 9, of which waited for: 2 -> 2; matrix products, arithmetic and copies ran while one was open for 0% -> 0% of each run, Pallas kernels for 27% -> 40%
where the time goes in v3:
time: 42.7 us; the launch traced here: 42.4 us
  Pallas kernels  22.8 us (53%)
  starting transfers between devices  15.8 us (37%)
  waiting for transfers between devices  3.08 us (7%)
  between operations  0.78 us (2%)
    pallas_call x10, Pallas kernels, call(): pl.pallas_call(kernel, out_shape=out_shape, in_specs=[hbm if place in far...  22.8 us
    ppermute x3, starting transfers between devices, body(): slabs.append(lax.ppermute(sends[step], 'lon', pairs))  6.19 us
    ppermute x1, starting transfers between devices, body(): below = lax.ppermute(high, 'lon', forward)  3.03 us
    ppermute x1, starting transfers between devices, body(): from_west = lax.ppermute(east_going, 'lon', ring)  2.64 us
    ppermute x1, starting transfers between devices, body(): from_east = lax.ppermute(own_west, 'lon', ring_back)  2.48 us
    ppermute x1, waiting for transfers between devices, body(): came = lax.ppermute(send, 'lon', [(i, i ^ 2) for i in range(count)])  1.77 us
    ppermute x1, starting transfers between devices, body(): above = lax.ppermute(low, 'lon', backward)  1.29 us
    ppermute x1, waiting for transfers between devices, body(): came = lax.ppermute(send, 'lon', [(i, i ^ 1) for i in range(count)])  1.29 us
  transfers between devices with their start and end apart: 9, of which 2 were waited for; matrix products, arithmetic and copies ran while one was open for 0% of the time, Pallas kernels for 40%

profile of v3, /device:TPU:0, one launch (start us, length us, event | category | flops | bytes accessed | tf_op | source)
XLA Modules:
  0.0 42.4 jit_solution(15410595961487780950)
XLA Ops:
  0.6 0.9 %pack_edges.1 = (f32[24,256]{1,0:T(8,128)S(1)}, f32[24,256]{1,0:T(8,128)S(1)}, f32[96,256]{1,0:T(8,128)S(1)}) custom-call(f32[32,256]{1,0:T(8,128)} %old_in.1, f32[32,256]{1,0:T(8,128)} %force_in.1, f32[32,256]{1,0:T(8,128)} %coeff_in.1, s32[32,256]{1,0:T(8,128)} %mask_in.1), custom_call_target="tpu_custom_call" | custom-call | tf_op jit(solution)/shard_map/pack_edges/pallas_call | solution.py:642
  1.5 1.3 %collective-permute-start.1 = (f32[24,256]{1,0:T(8,128)S(1)}, f32[24,256]{1,0:T(8,128)S(1)}, u32[]{:S(2)}, u32[]{:S(2)}) collective-permute-start(f32[24,256]{1,0:T(8,128)S(1)} %get-tuple-element.30), channel_id=1, source_target_pairs={{1,0},{2,1},{3,2},{4,3},{5,4},{6,5},{7,6},{8,7},{9,8},{10,9},{11,1... | collective-permute-start | bytes 73736 | tf_op jit(solution)/shard_map/ppermute | solution.py:675
  2.8 3.0 %collective-permute-start = (f32[24,256]{1,0:T(8,128)S(1)}, f32[24,256]{1,0:T(8,128)S(1)}, u32[]{:S(2)}, u32[]{:S(2)}) collective-permute-start(f32[24,256]{1,0:T(8,128)S(1)} %get-tuple-element.29.high_ref), channel_id=1, source_target_pairs={{0,1},{1,2},{2,3},{3,4},{4,5},{5,6},{6,7},{7,8},{8,9},{9,10},{10,1... | collective-permute-start | bytes 73736 | tf_op jit(solution)/shard_map/ppermute | solution.py:674
  5.8 2.8 %load.1 = (f32[24,256]{1,0:T(8,128)S(1)}, f32[8,16,16,512]{3,2,1,0:T(8,128)S(1)}, s32[16,512]{1,0:T(8,128)S(1)}, s32[16,512]{1,0:T(8,128)S(1)}, f32[16,16,512]{2,1,0:T(8,128)S(1)}, /*index=5*/f32[16,16,512]{2,1,0:T(8,128)S(1)}) custom-call(f32[24,256]{1,0:T(8,128)S(1)} %get-tuple-element.29.high_ref, f32[8,16,16,512]{3,2,1,0:T(8,128)} %tracers_in.1, ...), custom_call_target="tpu_custom_call" | custom-call | tf_op jit(solution)/shard_map/load/pallas_call | solution.py:642
  8.6 0.0 collective-permute-done.1.above_ref
  8.6 0.0 collective-permute-done.below_ref
  8.7 0.5 %solver_basis.1 = (f32[128,256]{1,0:T(8,128)S(1)}, f32[4,24,128]{2,1,0:T(8,128)S(1)}, f32[4,24,128]{2,1,0:T(8,128)S(1)}, f32[4,24,128]{2,1,0:T(8,128)S(1)}, f32[4,24,128]{2,1,0:T(8,128)S(1)}) custom-call(f32[96,256]{1,0:T(8,128)S(1)} %get-tuple-element.28.own_ref, f32[24,256]{1,0:T(8,128)S(1)} %collective-permute-done.below_ref, ...), custom_call_target="tpu_custom_call" | custom-call | tf_op jit(solution)/shard_map/solver_basis/pallas_call | solution.py:642
  9.2 0.4 pack_tracer_edges.1
  9.5 2.6 %collective-permute-start.7 = (f32[35,8,512]{2,1,0:T(8,128)S(1)}, f32[35,8,512]{2,1,0:T(8,128)S(1)}, u32[]{:S(2)}, u32[]{:S(2)}) collective-permute-start(f32[35,8,512]{2,1,0:T(8,128)S(1)} %get-tuple-element.48), channel_id=1, source_target_pairs={{0,1},{1,2},{2,3},{3,4},{4,5},{5,6},{6,7},{7,8},{8,9},{9,10},{10,1... | collective-permute-start | bytes 1720328 | tf_op jit(solution)/shard_map/ppermute | solution.py:713
  12.2 2.5 %collective-permute-start.8 = (f32[32,8,512]{2,1,0:T(8,128)S(1)}, f32[32,8,512]{2,1,0:T(8,128)S(1)}, u32[]{:S(2)}, u32[]{:S(2)}) collective-permute-start(f32[32,8,512]{2,1,0:T(8,128)S(1)} %get-tuple-element.42._.own_west_ref), channel_id=1, source_target_pairs={{1,0},{2,1},{3,2},{4,3},{5,4},{6,5},{7,6},{8,7},{9,8},{10,9},{11,1... | collective-permute-start | bytes 1572872 | tf_op jit(solution)/shard_map/ppermute | solution.py:714
  14.6 2.2 %collective-permute-start.2 = (f32[4,24,128]{2,1,0:T(8,128)S(1)}, f32[4,24,128]{2,1,0:T(8,128)S(1)}, u32[]{:S(2)}, u32[]{:S(2)}) collective-permute-start(f32[4,24,128]{2,1,0:T(8,128)S(1)} %get-tuple-element.33), channel_id=1, source_target_pairs={{0,4},{1,5},{2,6},{3,7},{4,8},{5,9},{6,10},{7,11},{8,12},{9,13},{1... | collective-permute-start | bytes 147464 | tf_op jit(solution)/shard_map/ppermute | solution.py:703
  16.9 2.6 %collective-permute-start.3 = (f32[4,24,128]{2,1,0:T(8,128)S(1)}, f32[4,24,128]{2,1,0:T(8,128)S(1)}, u32[]{:S(2)}, u32[]{:S(2)}) collective-permute-start(f32[4,24,128]{2,1,0:T(8,128)S(1)} %get-tuple-element.34), channel_id=1, source_target_pairs={{0,8},{1,9},{2,10},{3,11},{4,12},{5,13},{6,14},{7,15},{8,0},{9,1},... | collective-permute-start | bytes 147464 | tf_op jit(solution)/shard_map/ppermute | solution.py:703
  19.5 1.3 %collective-permute-start.4 = (f32[4,24,128]{2,1,0:T(8,128)S(1)}, f32[4,24,128]{2,1,0:T(8,128)S(1)}, u32[]{:S(2)}, u32[]{:S(2)}) collective-permute-start(f32[4,24,128]{2,1,0:T(8,128)S(1)} %get-tuple-element.35), channel_id=1, source_target_pairs={{0,12},{1,13},{2,14},{3,15},{4,0},{5,1},{6,2},{7,3},{8,4},{9,5},{1... | collective-permute-start | bytes 147464 | tf_op jit(solution)/shard_map/ppermute | solution.py:703
  20.8 2.4 %sources.1.before_ref = f32[8,16,16,512]{3,2,1,0:T(8,128)S(1)} custom-call(f32[8,16,16,512]{3,2,1,0:T(8,128)S(1)} %get-tuple-element.36.tracers_ref, s32[16,512]{1,0:T(8,128)S(1)} %get-tuple-element.37.depth_ref, f32[32,8,512]{2,1,0:T(8,128)S(1)} %get-tuple-element.42._.own_west_ref), custom_call_target="tpu_custom_call" | custom-call | flops 73400320 | bytes 8388608 | tf_op jit(solution)/shard_map/sources/pallas_call | solution.py:642
  23.3 8.4 %north_fluxes.1 = (f32[8,16,16,512]{3,2,1,0:T(8,128)S(1)}, f32[8,16,16,512]{3,2,1,0:T(8,128)S(1)}, f32[8,16,16,512]{3,2,1,0:T(8,128)S(1)}) custom-call(f32[8,16,16,512]{3,2,1,0:T(8,128)S(1)} %get-tuple-element.36.tracers_ref, s32[16,512]{1,0:T(8,128)S(1)} %get-tuple-element.37.depth_ref, f32[16,16,512]{2,1,0:T(8,128)S(1)} %get-tuple-element.38.v_ref, ...), custom_call_target="tpu_custom_call" | custom-call | flops 73400320 | bytes 8388608 | tf_op jit(solution)/shard_map/north_fluxes/pallas_call | solution.py:642
  31.7 0.0 collective-permute-done.2.refs_1_
  31.7 0.0 collective-permute-done.3.refs_2_
  31.7 0.0 collective-permute-done.4.refs_3_
  31.8 0.1 collective-permute-start.5
  31.9 1.3 %collective-permute-done.5.came_ref = f32[2,4,24,128]{3,2,1,0:T(8,128)S(1)} collective-permute-done((f32[2,4,24,128]{3,2,1,0:T(8,128)S(1)}, f32[2,4,24,128]{3,2,1,0:T(8,128)S(1)}, u32[]{:S(2)}, u32[]{:S(2)}) %collective-permute-start.5) | collective-permute-done | bytes 98336 | tf_op jit(solution)/shard_map/ppermute | solution.py:730
  33.2 0.1 collective-permute-start.6
  33.3 0.0 collective-permute-done.8.from_east_ref
  33.3 0.0 collective-permute-done.7.from_west_ref
  33.3 3.0 %east_fluxes.1 = (f32[8,16,16,512]{3,2,1,0:T(8,128)S(1)}, f32[8,16,16,512]{3,2,1,0:T(8,128)S(1)}, f32[16,8,512]{2,1,0:T(8,128)S(1)}) custom-call(f32[8,16,16,512]{3,2,1,0:T(8,128)S(1)} %get-tuple-element.36.tracers_ref, s32[16,512]{1,0:T(8,128)S(1)} %get-tuple-element.37.depth_ref, s32[16,512]{1,0:T(8,128)S(1)} %get-tuple-element.39.east_depth_ref, ...), custom_call_target="tpu_custom_call" | custom-call | flops 73400320 | bytes 8388608 | tf_op jit(solution)/shard_map/east_fluxes/pallas_call | solution.py:642
  36.3 1.8 %collective-permute-done.6.came_ref = f32[2,4,24,128]{3,2,1,0:T(8,128)S(1)} collective-permute-done((f32[2,4,24,128]{3,2,1,0:T(8,128)S(1)}, f32[2,4,24,128]{3,2,1,0:T(8,128)S(1)}, u32[]{:S(2)}, u32[]{:S(2)}) %collective-permute-start.6) | collective-permute-done | bytes 98336 | tf_op jit(solution)/shard_map/ppermute | solution.py:732
  38.1 4.3 %surface_update.1 = (f32[32,256]{1,0:T(8,128)}, f32[8,16,16,512]{3,2,1,0:T(8,128)}) custom-call(f32[2,4,24,128]{3,2,1,0:T(8,128)S(1)} %get-tuple-element.46._.kept_ref, f32[2,4,24,128]{3,2,1,0:T(8,128)S(1)} %collective-permute-done.6.came_ref, f32[128,256]{1,0:T(8,128)S(1)} %get-tuple-element.41._.basis_ref, ...), custom_call_target="tpu_custom_call" | custom-call | tf_op jit(solution)/shard_map/surface_update/pallas_call | solution.py:642
  (2 shorter events, 0.0 us)
Async XLA Ops:
  1.5 7.1 %collective-permute-start.1 = (f32[24,256]{1,0:T(8,128)S(1)}, f32[24,256]{1,0:T(8,128)S(1)}, u32[]{:S(2)}, u32[]{:S(2)}) collective-permute-start(f32[24,256]{1,0:T(8,128)S(1)} %get-tuple-element.30), channel_id=1, source_target_pairs={{1,0},{2,1},{3,2},{4,3},{5,4},{6,5},{7,6},{8,7},{9,8},{10,9},{11,1... | collective-permute-start | bytes 73736 | tf_op jit(solution)/shard_map/ppermute | solution.py:675
  2.8 5.9 %collective-permute-start = (f32[24,256]{1,0:T(8,128)S(1)}, f32[24,256]{1,0:T(8,128)S(1)}, u32[]{:S(2)}, u32[]{:S(2)}) collective-permute-start(f32[24,256]{1,0:T(8,128)S(1)} %get-tuple-element.29.high_ref), channel_id=1, source_target_pairs={{0,1},{1,2},{2,3},{3,4},{4,5},{5,6},{6,7},{7,8},{8,9},{9,10},{10,1... | collective-permute-start | bytes 73736 | tf_op jit(solution)/shard_map/ppermute | solution.py:674
  9.5 23.7 %collective-permute-start.7 = (f32[35,8,512]{2,1,0:T(8,128)S(1)}, f32[35,8,512]{2,1,0:T(8,128)S(1)}, u32[]{:S(2)}, u32[]{:S(2)}) collective-permute-start(f32[35,8,512]{2,1,0:T(8,128)S(1)} %get-tuple-element.48), channel_id=1, source_target_pairs={{0,1},{1,2},{2,3},{3,4},{4,5},{5,6},{6,7},{7,8},{8,9},{9,10},{10,1... | collective-permute-start | bytes 1720328 | tf_op jit(solution)/shard_map/ppermute | solution.py:713
  12.2 21.1 %collective-permute-start.8 = (f32[32,8,512]{2,1,0:T(8,128)S(1)}, f32[32,8,512]{2,1,0:T(8,128)S(1)}, u32[]{:S(2)}, u32[]{:S(2)}) collective-permute-start(f32[32,8,512]{2,1,0:T(8,128)S(1)} %get-tuple-element.42._.own_west_ref), channel_id=1, source_target_pairs={{1,0},{2,1},{3,2},{4,3},{5,4},{6,5},{7,6},{8,7},{9,8},{10,9},{11,1... | collective-permute-start | bytes 1572872 | tf_op jit(solution)/shard_map/ppermute | solution.py:714
  14.6 17.1 %collective-permute-start.2 = (f32[4,24,128]{2,1,0:T(8,128)S(1)}, f32[4,24,128]{2,1,0:T(8,128)S(1)}, u32[]{:S(2)}, u32[]{:S(2)}) collective-permute-start(f32[4,24,128]{2,1,0:T(8,128)S(1)} %get-tuple-element.33), channel_id=1, source_target_pairs={{0,4},{1,5},{2,6},{3,7},{4,8},{5,9},{6,10},{7,11},{8,12},{9,13},{1... | collective-permute-start | bytes 147464 | tf_op jit(solution)/shard_map/ppermute | solution.py:703
  16.9 14.8 %collective-permute-start.3 = (f32[4,24,128]{2,1,0:T(8,128)S(1)}, f32[4,24,128]{2,1,0:T(8,128)S(1)}, u32[]{:S(2)}, u32[]{:S(2)}) collective-permute-start(f32[4,24,128]{2,1,0:T(8,128)S(1)} %get-tuple-element.34), channel_id=1, source_target_pairs={{0,8},{1,9},{2,10},{3,11},{4,12},{5,13},{6,14},{7,15},{8,0},{9,1},... | collective-permute-start | bytes 147464 | tf_op jit(solution)/shard_map/ppermute | solution.py:703
  19.5 12.3 %collective-permute-start.4 = (f32[4,24,128]{2,1,0:T(8,128)S(1)}, f32[4,24,128]{2,1,0:T(8,128)S(1)}, u32[]{:S(2)}, u32[]{:S(2)}) collective-permute-start(f32[4,24,128]{2,1,0:T(8,128)S(1)} %get-tuple-element.35), channel_id=1, source_target_pairs={{0,12},{1,13},{2,14},{3,15},{4,0},{5,1},{6,2},{7,3},{8,4},{9,5},{1... | collective-permute-start | bytes 147464 | tf_op jit(solution)/shard_map/ppermute | solution.py:703
  31.8 1.4 %collective-permute-start.5 = (f32[2,4,24,128]{3,2,1,0:T(8,128)S(1)}, f32[2,4,24,128]{3,2,1,0:T(8,128)S(1)}, u32[]{:S(2)}, u32[]{:S(2)}) collective-permute-start(f32[2,4,24,128]{3,2,1,0:T(8,128)S(1)} %get-tuple-element.45), channel_id=1, source_target_pairs={{0,1},{1,0},{2,3},{3,2},{4,5},{5,4},{6,7},{7,6},{8,9},{9,8},{10,11... | collective-permute-start | bytes 294920 | tf_op jit(solution)/shard_map/ppermute | solution.py:730
  33.2 4.9 %collective-permute-start.6 = (f32[2,4,24,128]{3,2,1,0:T(8,128)S(1)}, f32[2,4,24,128]{3,2,1,0:T(8,128)S(1)}, u32[]{:S(2)}, u32[]{:S(2)}) collective-permute-start(f32[2,4,24,128]{3,2,1,0:T(8,128)S(1)} %get-tuple-element.47), channel_id=1, source_target_pairs={{0,2},{1,3},{2,0},{3,1},{4,6},{5,7},{6,4},{7,5},{8,10},{9,11},{10,... | collective-permute-start | bytes 294920 | tf_op jit(solution)/shard_map/ppermute | solution.py:732

commit v4 on v3

--- a/solution.py
+++ b/solution.py
@@ -374,78 +374,83 @@
                 base_ref[(kind, level) + at] = value + (wet * sources[kind] + (down - up))
 
 
+def turn(ref_block, target_ref, start=0):
+    rows = ref_block.shape[1]
+    for tile in range(rows // LANES):
+        part = slice(tile * LANES, (tile + 1) * LANES)
+        target_ref[start + part.start : start + part.stop] = ref_block[:, part].T
+
+
+def shifted(here, other, step):
+    sublane = lax.broadcasted_iota(jnp.int32, (SUBLANES, LANES), 0)
+    inside = sublane < SUBLANES - step if step > 0 else sublane >= -step
+    amount = (SUBLANES - step) % SUBLANES if step > 0 else -step
+    other = pltpu.roll(other, amount, 0) if other is not None else 0.0
+    return jnp.where(inside, pltpu.roll(here, amount, 0), other)
+
+
+def row_tile(block):
+    return slice(block * SUBLANES, (block + 1) * SUBLANES)
+
+
 def north_kernel(
     tracers_ref,
     depth_ref,
     v_ref,
-    before_ref,
-    base_ref,
+    _,
+    change_ref,
     face_ref,
-    face_south_ref,
-    band_ref,
-    north_ref,
-    south_ref,
+    depth_turned_ref,
+    wet_ref,
+    scale_ref,
+    flow_ref,
+    mix_ref,
+    masked_ref,
 ):
     kinds, levels, columns, rows = tracers_ref.shape
-    blocks, count = columns // SUBLANES, rows // LANES
-    places = grid_tiles(columns, rows)
-    source = lax.broadcasted_iota(jnp.int32, (rows, rows), 0)
-    target = lax.broadcasted_iota(jnp.int32, (rows, rows), 1)
-    for place, moved in enumerate((0, 1)):
-        offset = source - target + moved
-        near = (offset == 0) | (offset == 1)
-        far = (offset == -1) | (offset == 2)
-        band = jnp.where(near, 7.0, jnp.where(far, -1.0, 0.0))
-        band_ref[:, place * rows : (place + 1) * rows] = band.astype(jnp.bfloat16)
-    depth = {p: depth_ref[tile_index(p)].astype(jnp.float32) for p in places}
-    depth_north = shift_rows(depth, 1, blocks, count)
-    depth_south = shift_rows(depth, -1, blocks, count)
-    for p in places:
-        at = tile_index(p)
-        north_ref[at] = jnp.minimum(depth[p], depth_north[p]).astype(jnp.int32)
-        south_ref[at] = jnp.minimum(depth[p], depth_south[p]).astype(jnp.int32)
-
-    @pl.loop(0, levels)
-    def _(level):
-        wet, scale, mix, scale_s, mix_s, flow = {}, {}, {}, {}, {}, {}
-        for p in places:
-            at = tile_index(p)
-            wet[p] = jnp.where(level < depth_ref[at], 1.0, 0.0)
-            is_open = level < north_ref[at]
-            scale[p] = jnp.where(is_open, 1.0 / 12.0, 0.0)
-            mix[p] = jnp.where(is_open, HORIZ_DIFF, 0.0)
-            is_open = level < south_ref[at]
-            scale_s[p] = jnp.where(is_open, 1.0 / 12.0, 0.0)
-            mix_s[p] = jnp.where(is_open, HORIZ_DIFF, 0.0)
-            flow[p] = v_ref[(level,) + at]
-        flow_s = shift_rows(flow, -1, blocks, count)
-        wet_full = jnp.where(level < depth_ref[...], 1.0, 0.0)
-        masked_full = [tracers_ref[kind, level] * wet_full for kind in range(kinds)]
-        whole = jnp.concatenate(masked_full, axis=0)
-        first = whole.astype(jnp.bfloat16)
-        second = (whole - first.astype(jnp.float32)).astype(jnp.bfloat16)
-        weights = band_ref[...]
-        faces = jnp.dot(first, weights, preferred_element_type=jnp.float32) + jnp.dot(
-            second, weights, preferred_element_type=jnp.float32
-        )
-        for kind in range(kinds):
-            masked = {p: masked_full[kind][tile_index(p)] for p in places}
-            north = shift_rows(masked, 1, blocks, count)
-            south = shift_rows(masked, -1, blocks, count)
-            for p in places:
-                rows_at, lanes_at = tile_index(p)
-                at = (kind, level, rows_at, lanes_at)
-                row = kind * columns + rows_at.start
-                picked = faces[row : row + SUBLANES]
-                face = picked[:, lanes_at] * scale[p]
-                face_south = (
-                    picked[:, rows + lanes_at.start : rows + lanes_at.stop] * scale_s[p]
-                )
-                face_ref[at] = face
-                face_south_ref[at] = face_south
-                flux = flow[p] * face - mix[p] * (north[p] - masked[p])
-                flux_south = flow_s[p] * face_south - mix_s[p] * (masked[p] - south[p])
-                base_ref[at] = before_ref[at] + (flux_south - flux)
+    per_layer = LANES // columns
+    layers = levels // per_layer
+    blocks = rows // SUBLANES
+    depth = depth_ref[...].astype(jnp.float32)
+    turn(jnp.concatenate([depth] * per_layer, axis=0), depth_turned_ref)
+    lane_level = lax.broadcasted_iota(jnp.int32, (SUBLANES, LANES), 1) // columns
+    for layer in range(layers):
+        span = slice(layer * per_layer, (layer + 1) * per_layer)
+        turn(v_ref[span].reshape(LANES, rows), flow_ref.at[layer])
+        level = (lane_level + layer * per_layer).astype(jnp.float32)
+        for block in range(blocks):
+            at = row_tile(block)
+            here = depth_turned_ref[at]
+            after = depth_turned_ref[row_tile(block + 1)] if block + 1 < blocks else None
+            is_open = level < jnp.minimum(here, shifted(here, after, 1))
+            scale = jnp.where(is_open, 1.0 / 12.0, 0.0)
+            wet_ref[layer, at] = jnp.where(level < here, 1.0, 0.0)
+            scale_ref[layer, at] = scale
+            mix_ref[layer, at] = jnp.where(is_open, HORIZ_DIFF, 0.0)
+            flow_ref[layer, at] = flow_ref[layer, at] * scale
+
+    @pl.loop(0, kinds)
+    def _(kind):
+        for layer in range(layers):
+            span = slice(layer * per_layer, (layer + 1) * per_layer)
+            turn(tracers_ref[kind, span].reshape(LANES, rows), masked_ref.at[layer])
+            tiles = [
+                masked_ref[layer, row_tile(block)] * wet_ref[layer, row_tile(block)]
+                for block in range(blocks)
+            ]
+            before = None
+            for block in range(blocks):
+                at = row_tile(block)
+                here = tiles[block]
+                after = tiles[block + 1] if block + 1 < blocks else None
+                one = shifted(here, after, 1)
+                two = shifted(here, after, 2)
+                south = shifted(here, tiles[block - 1] if block else None, -1)
+                face = 7.0 * (here + one) - (south + two)
+                face_ref[kind, layer, at] = face * scale_ref[layer, at]
+                flux = face * flow_ref[layer, at] - (one - here) * mix_ref[layer, at]
+                change_ref[kind, layer, at] = shifted(flux, before, -1) - flux
+                before = flux
 
 
 def east_kernel(
@@ -475,7 +480,8 @@
         scale_west = jnp.where(z < depth_west, 1.0 / 12.0, 0.0)
         mix_west = jnp.where(z < depth_west, HORIZ_DIFF, 0.0)
         face = (7.0 * (center + east_one) - outer) * scale_west
-        face_west_ref[z] = face
+        for kind in range(kinds):
+            face_west_ref[kind, z : z + 1] = face[kind : kind + 1]
         flux_west_ref[z] = u_west * face - mix_west * (east_one - center)
 
     @pl.loop(0, levels)
@@ -519,12 +525,15 @@
     basis_ref,
     base_ref,
     face_east_ref,
+    face_west_ref,
+    change_ref,
     face_north_ref,
-    face_south_ref,
-    face_west_ref,
     surface_ref,
     out_ref,
     slabs_ref,
+    height_ref,
+    flow_ref,
+    turned_ref,
     result_ref,
     sems,
 ):
@@ -573,10 +582,20 @@
             jnp.broadcast_to(joined[columns + 1 : columns + 2], (SUBLANES, LANES))
         )
     height_east = shift_columns(height, 1, east_edge, blocks, count)
-    height_north = shift_rows(height, 1, blocks, count)
     flow_east = {p: -BARO_GAIN * (height_east[p] - height[p]) for p in places}
-    flow_north = {p: -BARO_GAIN * (height_north[p] - height[p]) for p in places}
-    flow_south = shift_rows(flow_north, -1, blocks, count)
+    per_layer = LANES // columns
+    layers = levels // per_layer
+    row_blocks = rows // SUBLANES
+    for p in places:
+        for repeat in range(per_layer):
+            at = tile_index(p)
+            start = repeat * columns
+            height_ref[start + at[0].start : start + at[0].stop, at[1]] = height[p]
+    turn(height_ref, turned_ref)
+    for block in range(row_blocks):
+        here = turned_ref[row_tile(block)]
+        after = turned_ref[row_tile(block + 1)] if block + 1 < row_blocks else None
+        flow_ref[row_tile(block)] = -BARO_GAIN * (shifted(here, after, 1) - here)
     flow_west = [
         -BARO_GAIN * (jnp.broadcast_to(height[0, tile][:1], (SUBLANES, LANES)) - west_edge[tile])
         for tile in range(count)
@@ -585,29 +604,38 @@
     def copy(kind):
         return pltpu.make_async_copy(result_ref.at[kind], out_ref.at[kind], sems.at[kind])
 
-    for kind in range(kinds):
-        @pl.loop(0, levels, unroll=4)
-        def _(level):
-            flux_east = {
-                p: flow_east[p] * face_east_ref[(kind, level) + tile_index(p)] for p in places
-            }
-            edge = [
-                flow_west[tile]
-                * jnp.broadcast_to(
-                    face_west_ref[level, kind : kind + 1, tile * LANES : (tile + 1) * LANES],
-                    (SUBLANES, LANES),
-                )
-                for tile in range(count)
-            ]
-            from_west = shift_columns(flux_east, -1, edge, blocks, count)
-            for p in places:
-                at = (kind, level) + tile_index(p)
-                result_ref[at] = base_ref[at] + (
-                    (from_west[p] - flux_east[p])
-                    + (flow_south[p] * face_south_ref[at] - flow_north[p] * face_north_ref[at])
-                )
-
+    @pl.loop(0, kinds)
+    def _(kind):
+        for layer in range(layers):
+            before = None
+            for block in range(row_blocks):
+                at = row_tile(block)
+                flux = flow_ref[at] * face_north_ref[kind, layer, at]
+                turned_ref[at] = change_ref[kind, layer, at] + (shifted(flux, before, -1) - flux)
+                before = flux
+            for tile in range(count):
+                part = slice(tile * LANES, (tile + 1) * LANES)
+                along = turned_ref[part].T
+                for z in range(per_layer):
+                    level = layer * per_layer + z
+                    flux_east = {
+                        (block, tile): flow_east[block, tile]
+                        * face_east_ref[(kind, level) + tile_index((block, tile))]
+                        for block in range(blocks)
+                    }
+                    edge = flow_west[tile] * jnp.broadcast_to(
+                        face_west_ref[kind, level : level + 1, part], (SUBLANES, LANES)
+                    )
+                    for block in range(blocks):
+                        at = (kind, level) + tile_index((block, tile))
+                        start = z * columns + block * SUBLANES
+                        west = flux_east[block - 1, tile] if block else edge
+                        flux = flux_east[block, tile]
+                        result_ref[at] = base_ref[at] + (
+                            (shifted(flux, west, -1) - flux) + along[start : start + SUBLANES]
+                        )
         copy(kind).start()
+
     for kind in range(kinds):
         copy(kind).wait()
 
@@ -713,26 +741,23 @@
     from_west = lax.ppermute(east_going, "lon", ring)
     from_east = lax.ppermute(own_west, "lon", ring_back)
     (base,) = call(source_kernel, (held,), "sources", (tracers, column_depth, own_west), cost=70)
-    base, face_north, face_south = call(
+    turned = (kinds, levels * columns // LANES, rows, LANES)
+    change, face_north = call(
         north_kernel,
-        (held, held, held),
+        (pltpu.VMEM(turned, f32), pltpu.VMEM(turned, f32)),
         "north_fluxes",
         (tracers, column_depth, v_clinic, base),
-        scratch=[
-            pltpu.VMEM((rows, 2 * rows), jnp.bfloat16),
-            pltpu.VMEM((columns, rows), jnp.int32),
-            pltpu.VMEM((columns, rows), jnp.int32),
-        ],
+        scratch=[pltpu.VMEM((rows, LANES), f32)] + [pltpu.VMEM(turned[1:], f32)] * 5,
         cost=70,
     )
     quarter = sds((2, groups, SLAB_ROWS, LANES), f32)
-    keep, send = call(core_kernel, (quarter, quarter), "split_cores", (*slabs, base))
+    keep, send = call(core_kernel, (quarter, quarter), "split_cores", (*slabs, change))
     came = lax.ppermute(send, "lon", [(i, i ^ 1) for i in range(count)])
     keep, send = call(half_kernel, (quarter, quarter), "split_halves", (keep, came))
     came = lax.ppermute(send, "lon", [(i, i ^ 2) for i in range(count)])
     base, face_east, face_west = call(
         east_kernel,
-        (held, held, pltpu.VMEM((levels, kinds, rows), f32)),
+        (held, held, pltpu.VMEM((kinds, levels, rows), f32)),
         "east_fluxes",
         (
             tracers,
@@ -753,9 +778,12 @@
             update_kernel,
             (sds((band, width), f32), result),
             "surface_update",
-            (keep, came, basis, base, face_east, face_north, face_south, face_west),
+            (keep, came, basis, base, face_east, face_west, change, face_north),
             scratch=[
                 pltpu.VMEM((count, SLAB_ROWS, LANES), f32),
+                pltpu.VMEM((LANES, rows), f32),
+                pltpu.VMEM((rows, LANES), f32),
+                pltpu.VMEM((rows, LANES), f32),
                 pltpu.VMEM(tracers.shape, f32),
                 pltpu.SemaphoreType.DMA((kinds,)),
             ],

time: 42.7 us -> 38.6 us (0.904)
  Pallas kernels: 22.8 us -> 18.2 us
  waiting for transfers between devices: 3.08 us -> 3.61 us
    pallas_call x10, Pallas kernels: 22.8 us -> 18.2 us  [call(): pl.pallas_call(kernel, out_shape=out_shape, in_specs=[hbm if place in far...]
    ppermute x3, waiting for transfers between devices: 0.01 us -> 0.58 us  [body(): slabs.append(lax.ppermute(sends[step], 'lon', pairs))]
  transfers between devices with their start and end apart: 9 -> 9, of which waited for: 2 -> 3; matrix products, arithmetic and copies ran while one was open for 0% -> 0% of each run, Pallas kernels for 40% -> 31%
where the time goes in v4:
time: 38.6 us; the launch traced here: 38.3 us
  Pallas kernels  18.2 us (47%)
  starting transfers between devices  15.8 us (41%)
  waiting for transfers between devices  3.61 us (9%)
  between operations  0.76 us (2%)
    pallas_call x10, Pallas kernels, call(): pl.pallas_call(kernel, out_shape=out_shape, in_specs=[hbm if place in far...  18.2 us
    ppermute x3, starting transfers between devices, body(): slabs.append(lax.ppermute(sends[step], 'lon', pairs))  6.19 us
    ppermute x1, starting transfers between devices, body(): below = lax.ppermute(high, 'lon', forward)  3.03 us
    ppermute x1, starting transfers between devices, body(): from_west = lax.ppermute(east_going, 'lon', ring)  2.64 us
    ppermute x1, starting transfers between devices, body(): from_east = lax.ppermute(own_west, 'lon', ring_back)  2.48 us
    ppermute x1, waiting for transfers between devices, body(): came = lax.ppermute(send, 'lon', [(i, i ^ 2) for i in range(count)])  1.73 us
    ppermute x1, starting transfers between devices, body(): above = lax.ppermute(low, 'lon', backward)  1.29 us
    ppermute x1, waiting for transfers between devices, body(): came = lax.ppermute(send, 'lon', [(i, i ^ 1) for i in range(count)])  1.29 us
  transfers between devices with their start and end apart: 9, of which 3 were waited for; matrix products, arithmetic and copies ran while one was open for 0% of the time, Pallas kernels for 31%

profile of v4, /device:TPU:0, one launch (start us, length us, event | category | flops | bytes accessed | tf_op | source)
XLA Modules:
  0.0 38.3 jit_solution(9060403808432802285)
XLA Ops:
  0.6 0.9 %pack_edges.1 = (f32[24,256]{1,0:T(8,128)S(1)}, f32[24,256]{1,0:T(8,128)S(1)}, f32[96,256]{1,0:T(8,128)S(1)}) custom-call(f32[32,256]{1,0:T(8,128)} %old_in.1, f32[32,256]{1,0:T(8,128)} %force_in.1, f32[32,256]{1,0:T(8,128)} %coeff_in.1, s32[32,256]{1,0:T(8,128)} %mask_in.1), custom_call_target="tpu_custom_call" | custom-call | tf_op jit(solution)/shard_map/pack_edges/pallas_call | solution.py:670
  1.5 1.3 %collective-permute-start.1 = (f32[24,256]{1,0:T(8,128)S(1)}, f32[24,256]{1,0:T(8,128)S(1)}, u32[]{:S(2)}, u32[]{:S(2)}) collective-permute-start(f32[24,256]{1,0:T(8,128)S(1)} %get-tuple-element.29), channel_id=1, source_target_pairs={{1,0},{2,1},{3,2},{4,3},{5,4},{6,5},{7,6},{8,7},{9,8},{10,9},{11,1... | collective-permute-start | bytes 73736 | tf_op jit(solution)/shard_map/ppermute | solution.py:703
  2.8 3.0 %collective-permute-start = (f32[24,256]{1,0:T(8,128)S(1)}, f32[24,256]{1,0:T(8,128)S(1)}, u32[]{:S(2)}, u32[]{:S(2)}) collective-permute-start(f32[24,256]{1,0:T(8,128)S(1)} %get-tuple-element.28.high_ref), channel_id=1, source_target_pairs={{0,1},{1,2},{2,3},{3,4},{4,5},{5,6},{6,7},{7,8},{8,9},{9,10},{10,1... | collective-permute-start | bytes 73736 | tf_op jit(solution)/shard_map/ppermute | solution.py:702
  5.8 2.8 %load.1 = (f32[24,256]{1,0:T(8,128)S(1)}, f32[8,16,16,512]{3,2,1,0:T(8,128)S(1)}, s32[16,512]{1,0:T(8,128)S(1)}, s32[16,512]{1,0:T(8,128)S(1)}, f32[16,16,512]{2,1,0:T(8,128)S(1)}, /*index=5*/f32[16,16,512]{2,1,0:T(8,128)S(1)}) custom-call(f32[24,256]{1,0:T(8,128)S(1)} %get-tuple-element.28.high_ref, f32[8,16,16,512]{3,2,1,0:T(8,128)} %tracers_in.1, ...), custom_call_target="tpu_custom_call" | custom-call | tf_op jit(solution)/shard_map/load/pallas_call | solution.py:670
  8.6 0.0 collective-permute-done.1.above_ref
  8.6 0.0 collective-permute-done.below_ref
  8.7 0.5 %solver_basis.1 = (f32[128,256]{1,0:T(8,128)S(1)}, f32[4,24,128]{2,1,0:T(8,128)S(1)}, f32[4,24,128]{2,1,0:T(8,128)S(1)}, f32[4,24,128]{2,1,0:T(8,128)S(1)}, f32[4,24,128]{2,1,0:T(8,128)S(1)}) custom-call(f32[96,256]{1,0:T(8,128)S(1)} %get-tuple-element.27.own_ref, f32[24,256]{1,0:T(8,128)S(1)} %collective-permute-done.below_ref, ...), custom_call_target="tpu_custom_call" | custom-call | tf_op jit(solution)/shard_map/solver_basis/pallas_call | solution.py:670
  9.2 0.4 pack_tracer_edges.1
  9.5 2.6 %collective-permute-start.7 = (f32[35,8,512]{2,1,0:T(8,128)S(1)}, f32[35,8,512]{2,1,0:T(8,128)S(1)}, u32[]{:S(2)}, u32[]{:S(2)}) collective-permute-start(f32[35,8,512]{2,1,0:T(8,128)S(1)} %get-tuple-element.47), channel_id=1, source_target_pairs={{0,1},{1,2},{2,3},{3,4},{4,5},{5,6},{6,7},{7,8},{8,9},{9,10},{10,1... | collective-permute-start | bytes 1720328 | tf_op jit(solution)/shard_map/ppermute | solution.py:741
  12.2 2.5 %collective-permute-start.8 = (f32[32,8,512]{2,1,0:T(8,128)S(1)}, f32[32,8,512]{2,1,0:T(8,128)S(1)}, u32[]{:S(2)}, u32[]{:S(2)}) collective-permute-start(f32[32,8,512]{2,1,0:T(8,128)S(1)} %get-tuple-element.41._.own_west_ref), channel_id=1, source_target_pairs={{1,0},{2,1},{3,2},{4,3},{5,4},{6,5},{7,6},{8,7},{9,8},{10,9},{11,1... | collective-permute-start | bytes 1572872 | tf_op jit(solution)/shard_map/ppermute | solution.py:742
  14.6 2.2 %collective-permute-start.2 = (f32[4,24,128]{2,1,0:T(8,128)S(1)}, f32[4,24,128]{2,1,0:T(8,128)S(1)}, u32[]{:S(2)}, u32[]{:S(2)}) collective-permute-start(f32[4,24,128]{2,1,0:T(8,128)S(1)} %get-tuple-element.32), channel_id=1, source_target_pairs={{0,4},{1,5},{2,6},{3,7},{4,8},{5,9},{6,10},{7,11},{8,12},{9,13},{1... | collective-permute-start | bytes 147464 | tf_op jit(solution)/shard_map/ppermute | solution.py:731
  16.9 2.6 %collective-permute-start.3 = (f32[4,24,128]{2,1,0:T(8,128)S(1)}, f32[4,24,128]{2,1,0:T(8,128)S(1)}, u32[]{:S(2)}, u32[]{:S(2)}) collective-permute-start(f32[4,24,128]{2,1,0:T(8,128)S(1)} %get-tuple-element.33), channel_id=1, source_target_pairs={{0,8},{1,9},{2,10},{3,11},{4,12},{5,13},{6,14},{7,15},{8,0},{9,1},... | collective-permute-start | bytes 147464 | tf_op jit(solution)/shard_map/ppermute | solution.py:731
  19.5 1.3 %collective-permute-start.4 = (f32[4,24,128]{2,1,0:T(8,128)S(1)}, f32[4,24,128]{2,1,0:T(8,128)S(1)}, u32[]{:S(2)}, u32[]{:S(2)}) collective-permute-start(f32[4,24,128]{2,1,0:T(8,128)S(1)} %get-tuple-element.34), channel_id=1, source_target_pairs={{0,12},{1,13},{2,14},{3,15},{4,0},{5,1},{6,2},{7,3},{8,4},{9,5},{1... | collective-permute-start | bytes 147464 | tf_op jit(solution)/shard_map/ppermute | solution.py:731
  20.8 2.4 %sources.1._.before_ref = f32[8,16,16,512]{3,2,1,0:T(8,128)S(1)} custom-call(f32[8,16,16,512]{3,2,1,0:T(8,128)S(1)} %get-tuple-element.35.tracers_ref, s32[16,512]{1,0:T(8,128)S(1)} %get-tuple-element.36.depth_ref, f32[32,8,512]{2,1,0:T(8,128)S(1)} %get-tuple-element.41._.own_west_ref), custom_call_target="tpu_custom_call" | custom-call | flops 73400320 | bytes 8388608 | tf_op jit(solution)/shard_map/sources/pallas_call | solution.py:670
  23.3 3.5 %north_fluxes.1 = (f32[8,2,512,128]{3,2,1,0:T(8,128)S(1)}, f32[8,2,512,128]{3,2,1,0:T(8,128)S(1)}) custom-call(f32[8,16,16,512]{3,2,1,0:T(8,128)S(1)} %get-tuple-element.35.tracers_ref, s32[16,512]{1,0:T(8,128)S(1)} %get-tuple-element.36.depth_ref, f32[16,16,512]{2,1,0:T(8,128)S(1)} %get-tuple-element.37.v_ref, f32[8,16,16,512]{3,2,1,0:T(8,128)S(1)} %sources.1._.before_ref), custom_call_target="tpu_custom_call" | custom-call | flops 73400320 | bytes 8388608 | tf_op jit(solution)/shard_map/north_fluxes/pallas_call | solution.py:670
  26.8 0.0 collective-permute-done.2.refs_1_
  26.8 0.6 %collective-permute-done.3.refs_2_ = f32[4,24,128]{2,1,0:T(8,128)S(1)} collective-permute-done((f32[4,24,128]{2,1,0:T(8,128)S(1)}, f32[4,24,128]{2,1,0:T(8,128)S(1)}, u32[]{:S(2)}, u32[]{:S(2)}) %collective-permute-start.3) | collective-permute-done | bytes 49184 | tf_op jit(solution)/shard_map/ppermute | solution.py:731
  27.3 0.0 collective-permute-done.4.refs_3_
  27.4 0.1 collective-permute-start.5
  27.5 1.3 %collective-permute-done.5.came_ref = f32[2,4,24,128]{3,2,1,0:T(8,128)S(1)} collective-permute-done((f32[2,4,24,128]{3,2,1,0:T(8,128)S(1)}, f32[2,4,24,128]{3,2,1,0:T(8,128)S(1)}, u32[]{:S(2)}, u32[]{:S(2)}) %collective-permute-start.5) | collective-permute-done | bytes 98336 | tf_op jit(solution)/shard_map/ppermute | solution.py:755
  28.8 0.1 collective-permute-start.6
  28.8 0.0 collective-permute-done.8.from_east_ref
  28.8 0.0 collective-permute-done.7.from_west_ref
  28.9 3.1 %east_fluxes.1 = (f32[8,16,16,512]{3,2,1,0:T(8,128)S(1)}, f32[8,16,16,512]{3,2,1,0:T(8,128)S(1)}, f32[8,16,512]{2,1,0:T(8,128)S(1)}) custom-call(f32[8,16,16,512]{3,2,1,0:T(8,128)S(1)} %get-tuple-element.35.tracers_ref, s32[16,512]{1,0:T(8,128)S(1)} %get-tuple-element.36.depth_ref, s32[16,512]{1,0:T(8,128)S(1)} %get-tuple-element.38.east_depth_ref, ...), custom_call_target="tpu_custom_call" | custom-call | flops 73400320 | bytes 8388608 | tf_op jit(solution)/shard_map/east_fluxes/pallas_call | solution.py:670
  31.9 1.7 %collective-permute-done.6.came_ref = f32[2,4,24,128]{3,2,1,0:T(8,128)S(1)} collective-permute-done((f32[2,4,24,128]{3,2,1,0:T(8,128)S(1)}, f32[2,4,24,128]{3,2,1,0:T(8,128)S(1)}, u32[]{:S(2)}, u32[]{:S(2)}) %collective-permute-start.6) | collective-permute-done | bytes 98336 | tf_op jit(solution)/shard_map/ppermute | solution.py:757
  33.7 4.6 %surface_update.1 = (f32[32,256]{1,0:T(8,128)}, f32[8,16,16,512]{3,2,1,0:T(8,128)}) custom-call(f32[2,4,24,128]{3,2,1,0:T(8,128)S(1)} %get-tuple-element.45._.kept_ref, f32[2,4,24,128]{3,2,1,0:T(8,128)S(1)} %collective-permute-done.6.came_ref, f32[128,256]{1,0:T(8,128)S(1)} %get-tuple-element.40._.basis_ref, ...), custom_call_target="tpu_custom_call" | custom-call | tf_op jit(solution)/shard_map/surface_update/pallas_call | solution.py:670
  (2 shorter events, 0.0 us)
Async XLA Ops:
  1.5 7.1 %collective-permute-start.1 = (f32[24,256]{1,0:T(8,128)S(1)}, f32[24,256]{1,0:T(8,128)S(1)}, u32[]{:S(2)}, u32[]{:S(2)}) collective-permute-start(f32[24,256]{1,0:T(8,128)S(1)} %get-tuple-element.29), channel_id=1, source_target_pairs={{1,0},{2,1},{3,2},{4,3},{5,4},{6,5},{7,6},{8,7},{9,8},{10,9},{11,1... | collective-permute-start | bytes 73736 | tf_op jit(solution)/shard_map/ppermute | solution.py:703
  2.8 5.9 %collective-permute-start = (f32[24,256]{1,0:T(8,128)S(1)}, f32[24,256]{1,0:T(8,128)S(1)}, u32[]{:S(2)}, u32[]{:S(2)}) collective-permute-start(f32[24,256]{1,0:T(8,128)S(1)} %get-tuple-element.28.high_ref), channel_id=1, source_target_pairs={{0,1},{1,2},{2,3},{3,4},{4,5},{5,6},{6,7},{7,8},{8,9},{9,10},{10,1... | collective-permute-start | bytes 73736 | tf_op jit(solution)/shard_map/ppermute | solution.py:702
  9.5 19.3 %collective-permute-start.7 = (f32[35,8,512]{2,1,0:T(8,128)S(1)}, f32[35,8,512]{2,1,0:T(8,128)S(1)}, u32[]{:S(2)}, u32[]{:S(2)}) collective-permute-start(f32[35,8,512]{2,1,0:T(8,128)S(1)} %get-tuple-element.47), channel_id=1, source_target_pairs={{0,1},{1,2},{2,3},{3,4},{4,5},{5,6},{6,7},{7,8},{8,9},{9,10},{10,1... | collective-permute-start | bytes 1720328 | tf_op jit(solution)/shard_map/ppermute | solution.py:741
  12.2 16.7 %collective-permute-start.8 = (f32[32,8,512]{2,1,0:T(8,128)S(1)}, f32[32,8,512]{2,1,0:T(8,128)S(1)}, u32[]{:S(2)}, u32[]{:S(2)}) collective-permute-start(f32[32,8,512]{2,1,0:T(8,128)S(1)} %get-tuple-element.41._.own_west_ref), channel_id=1, source_target_pairs={{1,0},{2,1},{3,2},{4,3},{5,4},{6,5},{7,6},{8,7},{9,8},{10,9},{11,1... | collective-permute-start | bytes 1572872 | tf_op jit(solution)/shard_map/ppermute | solution.py:742
  14.6 12.1 %collective-permute-start.2 = (f32[4,24,128]{2,1,0:T(8,128)S(1)}, f32[4,24,128]{2,1,0:T(8,128)S(1)}, u32[]{:S(2)}, u32[]{:S(2)}) collective-permute-start(f32[4,24,128]{2,1,0:T(8,128)S(1)} %get-tuple-element.32), channel_id=1, source_target_pairs={{0,4},{1,5},{2,6},{3,7},{4,8},{5,9},{6,10},{7,11},{8,12},{9,13},{1... | collective-permute-start | bytes 147464 | tf_op jit(solution)/shard_map/ppermute | solution.py:731
  16.9 10.5 %collective-permute-start.3 = (f32[4,24,128]{2,1,0:T(8,128)S(1)}, f32[4,24,128]{2,1,0:T(8,128)S(1)}, u32[]{:S(2)}, u32[]{:S(2)}) collective-permute-start(f32[4,24,128]{2,1,0:T(8,128)S(1)} %get-tuple-element.33), channel_id=1, source_target_pairs={{0,8},{1,9},{2,10},{3,11},{4,12},{5,13},{6,14},{7,15},{8,0},{9,1},... | collective-permute-start | bytes 147464 | tf_op jit(solution)/shard_map/ppermute | solution.py:731
  19.5 7.9 %collective-permute-start.4 = (f32[4,24,128]{2,1,0:T(8,128)S(1)}, f32[4,24,128]{2,1,0:T(8,128)S(1)}, u32[]{:S(2)}, u32[]{:S(2)}) collective-permute-start(f32[4,24,128]{2,1,0:T(8,128)S(1)} %get-tuple-element.34), channel_id=1, source_target_pairs={{0,12},{1,13},{2,14},{3,15},{4,0},{5,1},{6,2},{7,3},{8,4},{9,5},{1... | collective-permute-start | bytes 147464 | tf_op jit(solution)/shard_map/ppermute | solution.py:731
  27.4 1.4 %collective-permute-start.5 = (f32[2,4,24,128]{3,2,1,0:T(8,128)S(1)}, f32[2,4,24,128]{3,2,1,0:T(8,128)S(1)}, u32[]{:S(2)}, u32[]{:S(2)}) collective-permute-start(f32[2,4,24,128]{3,2,1,0:T(8,128)S(1)} %get-tuple-element.44), channel_id=1, source_target_pairs={{0,1},{1,0},{2,3},{3,2},{4,5},{5,4},{6,7},{7,6},{8,9},{9,8},{10,11... | collective-permute-start | bytes 294920 | tf_op jit(solution)/shard_map/ppermute | solution.py:755
  28.8 4.9 %collective-permute-start.6 = (f32[2,4,24,128]{3,2,1,0:T(8,128)S(1)}, f32[2,4,24,128]{3,2,1,0:T(8,128)S(1)}, u32[]{:S(2)}, u32[]{:S(2)}) collective-permute-start(f32[2,4,24,128]{3,2,1,0:T(8,128)S(1)} %get-tuple-element.46), channel_id=1, source_target_pairs={{0,2},{1,3},{2,0},{3,1},{4,6},{5,7},{6,4},{7,5},{8,10},{9,11},{10,... | collective-permute-start | bytes 294920 | tf_op jit(solution)/shard_map/ppermute | solution.py:757

commit v5 on v4

--- a/solution.py
+++ b/solution.py
@@ -31,35 +31,14 @@
 PIVOT_FLOOR = 3e-7
 
 
-def pack_kernel(old_in, force_in, coeff_in, mask_in, low_ref, high_ref, own_ref, *scratch):
-    old_ref, force_ref, coeff_ref, mask_ref, sems = scratch
-    copies = [
-        pltpu.make_async_copy(source, target, sems.at[place])
-        for place, (source, target) in enumerate(
-            zip((old_in, force_in, coeff_in, mask_in), (old_ref, force_ref, coeff_ref, mask_ref))
-        )
-    ]
-    for copy in copies:
-        copy.start()
-    for copy in copies:
-        copy.wait()
-    rows = old_ref.shape[0]
-    coeff = coeff_ref[...]
-    fields = (
-        coeff * old_ref[...] + force_ref[...],
-        coeff,
-        mask_ref[...].astype(jnp.float32),
-    )
-    for place, field in enumerate(fields):
-        low_ref[HALO * place : HALO * (place + 1)] = field[:HALO]
-        high_ref[HALO * place : HALO * (place + 1)] = field[rows - HALO :]
-        own_ref[rows * place : rows * (place + 1)] = field
+def is_even():
+    return lax.rem(lax.axis_index("lon"), 2) == 0
 
 
 def basis_kernel(
     own_ref,
-    below_ref,
-    above_ref,
+    inner_ref,
+    outer_ref,
     folded_ref,
     basis_ref,
     *refs,
@@ -69,12 +48,14 @@
     count = slabs_ref.shape[0]
     columns = width // count
     top_device = lax.axis_index("lon") == count - 1
-    above = jnp.where(top_device, folded_ref[...], above_ref[...])
+    below = jnp.where(is_even(), outer_ref[...], inner_ref[...])
+    above = jnp.where(is_even(), inner_ref[...], outer_ref[...])
+    above = jnp.where(top_device, folded_ref[...], above)
 
     def extended(place):
         part = slice(HALO * place, HALO * (place + 1))
         own = own_ref[rows * place : rows * (place + 1)]
-        return jnp.concatenate([below_ref[part], own, above[part]], axis=0)
+        return jnp.concatenate([below[part], own, above[part]], axis=0)
 
     first, coeff, mask = extended(0), extended(1), extended(2)
     diagonal = (coeff + 4.0 * mask - CENTRE) * (1.0 / SPREAD)
@@ -207,71 +188,111 @@
 
 
 def load_kernel(
-    high_ref,
+    old_in,
+    force_in,
+    coeff_in,
+    mask_in,
     tracers_in,
     depth_in,
     east_depth_in,
     u_in,
     v_in,
+    inner_ref,
+    outer_ref,
+    own_ref,
     folded_ref,
     tracers_ref,
     depth_ref,
     east_depth_ref,
     u_ref,
     v_ref,
+    edge_inner_ref,
+    edge_outer_ref,
+    old_ref,
+    force_ref,
+    coeff_ref,
+    mask_ref,
     sems,
 ):
-    kinds = tracers_ref.shape[0]
+    kinds, levels, columns, rows = tracers_ref.shape
+    band = old_ref.shape[0]
+    moves = [
+        (old_in, old_ref),
+        (force_in, force_ref),
+        (coeff_in, coeff_ref),
+        (mask_in, mask_ref),
+        (depth_in, depth_ref),
+        (east_depth_in, east_depth_ref),
+        (u_in, u_ref),
+    ]
+    moves += [(tracers_in.at[kind], tracers_ref.at[kind]) for kind in range(kinds)]
+    moves += [(v_in, v_ref)]
     copies = [
         pltpu.make_async_copy(source, target, sems.at[place])
-        for place, (source, target) in enumerate(
-            [
-                (depth_in, depth_ref),
-                (east_depth_in, east_depth_ref),
-                (u_in, u_ref),
-                (v_in, v_ref),
-            ]
-            + [(tracers_in.at[kind], tracers_ref.at[kind]) for kind in range(kinds)]
-        )
+        for place, (source, target) in enumerate(moves)
     ]
     for copy in copies:
         copy.start()
-    tiles = high_ref.shape[1] // LANES
-    for place in range(3):
+    for copy in copies[:4]:
+        copy.wait()
+    coeff = coeff_ref[...]
+    fields = (
+        coeff * old_ref[...] + force_ref[...],
+        coeff,
+        mask_ref[...].astype(jnp.float32),
+    )
+    for place, field in enumerate(fields):
+        low, high = field[:HALO], field[band - HALO :]
         part = slice(HALO * place, HALO * (place + 1))
+        inner_ref[part] = jnp.where(is_even(), high, low)
+        outer_ref[part] = jnp.where(is_even(), low, high)
+        own_ref[band * place : band * (place + 1)] = field
+        tiles = high.shape[1] // LANES
         for tile in range(tiles):
             other = tiles - 1 - tile
             folded_ref[part, tile * LANES : (tile + 1) * LANES] = reverse_tile(
-                high_ref[part, other * LANES : (other + 1) * LANES]
+                high[:, other * LANES : (other + 1) * LANES]
             )
-    for copy in copies:
+    for copy in copies[4:7]:
         copy.wait()
 
-
-def edge_kernel(
-    tracers_ref, depth_ref, east_depth_ref, u_ref, _, east_going_ref, west_going_ref
-):
-    kinds, levels, columns, rows = tracers_ref.shape
-    for z in range(levels):
-        place = 2 * levels + z // SUBLANES
-        row = z % SUBLANES
-        east_going_ref[place, row : row + 1] = u_ref[z, columns - 1 : columns]
-    place = 2 * levels + levels // SUBLANES
-    east_going_ref[place] = jnp.broadcast_to(
-        east_depth_ref[columns - 1 : columns].astype(jnp.float32), (SUBLANES, rows)
-    )
-    for kind in range(kinds):
+    def pack(kind, first, target_ref):
+        for side in range(2):
+            column = first + side
+            for z in range(levels):
+                wet = (z < depth_ref[column : column + 1]).astype(jnp.float32)
+                target_ref[2 * z + side, kind : kind + 1] = (
+                    tracers_ref[kind, z, column : column + 1] * wet
+                )
+
+    def pack_faces(target_ref):
         for z in range(levels):
-            for side in range(2):
-                column = columns - 2 + side
-                west_wet = (z < depth_ref[side : side + 1]).astype(jnp.float32)
-                east_wet = (z < depth_ref[column : column + 1]).astype(jnp.float32)
-                west_going_ref[2 * z + side, kind : kind + 1] = (
-                    tracers_ref[kind, z, side : side + 1] * west_wet
-                )
-                east_going_ref[2 * z + side, kind : kind + 1] = (
-                    tracers_ref[kind, z, column : column + 1] * east_wet
-                )
+            place = 2 * levels + z // SUBLANES
+            row = z % SUBLANES
+            target_ref[place, row : row + 1] = u_ref[z, columns - 1 : columns]
+        place = 2 * levels + levels // SUBLANES
+        target_ref[place] = jnp.broadcast_to(
+            east_depth_ref[columns - 1 : columns].astype(jnp.float32), (SUBLANES, rows)
+        )
+
+    pack_faces(edge_inner_ref)
+    pack_faces(edge_outer_ref)
+
+    def pack_all(inner_column, outer_column):
+        for kind in range(kinds):
+            copies[7 + kind].wait()
+            pack(kind, inner_column, edge_inner_ref)
+            pack(kind, outer_column, edge_outer_ref)
+
+    @pl.when(is_even())
+    def _():
+        pack_all(columns - 2, 0)
+
+    @pl.when(jnp.logical_not(is_even()))
+    def _():
+        pack_all(0, columns - 2)
+
+    copies[-1].wait()
 
 
 def grid_tiles(columns, rows):
@@ -458,19 +479,28 @@
     depth_ref,
     east_depth_ref,
     u_ref,
-    from_west_ref,
-    from_east_ref,
-    own_west_ref,
+    inner_ref,
+    outer_ref,
+    own_inner_ref,
+    own_outer_ref,
     before_ref,
     _,
     base_ref,
     face_east_ref,
     face_west_ref,
     flux_west_ref,
+    from_west_ref,
+    from_east_ref,
+    own_west_ref,
 ):
     kinds, levels, columns, rows = tracers_ref.shape
     blocks, count = columns // SUBLANES, rows // LANES
     places = grid_tiles(columns, rows)
+    for place in range(inner_ref.shape[0]):
+        from_west_ref[place] = jnp.where(is_even(), outer_ref[place], inner_ref[place])
+    for place in range(2 * levels):
+        from_east_ref[place] = jnp.where(is_even(), inner_ref[place], outer_ref[place])
+        own_west_ref[place] = jnp.where(is_even(), own_outer_ref[place], own_inner_ref[place])
     depth_west = from_west_ref[2 * levels + levels // SUBLANES]
     for z in range(levels):
         row = z % SUBLANES
@@ -659,10 +689,9 @@
     vmem = pl.BlockSpec(memory_space=pltpu.VMEM)
     hbm = pl.BlockSpec(memory_space=pltpu.HBM)
     fields = (surface_old, surface_forcing, surface_coeff, ocean_mask)
-    forward = [(i, i + 1) for i in range(count - 1)]
-    backward = [(target, source) for source, target in forward]
-    ring = [(i, (i + 1) % count) for i in range(count)]
-    ring_back = [(target, source) for source, target in ring]
+    pairs_inner = [(i, i ^ 1) for i in range(count)]
+    ring = [(i, (i + 1 if i % 2 else i - 1) % count) for i in range(count)]
+    pairs_outer = [(i, j) for i, j in ring if abs(i - j) == 1]
 
     def call(
         kernel, out_shape, name, operands, scratch=(), limit=SMALL_VMEM, cost=0, far=()
@@ -691,56 +720,48 @@
     packed = sds((3 * HALO, width), f32)
     held = pltpu.VMEM(tracers.shape, f32)
 
-    low, high, own = call(
-        pack_kernel,
-        (packed, packed, sds((3 * band, width), f32)),
-        "pack_edges",
-        fields,
-        scratch=[pltpu.VMEM(x.shape, x.dtype) for x in fields] + [pltpu.SemaphoreType.DMA((4,))],
-        far=range(4),
-    )
-    below = lax.ppermute(high, "lon", forward)
-    above = lax.ppermute(low, "lon", backward)
-
     def fetched(x):
         return pltpu.VMEM(x.shape, x.dtype)
 
+    edges = sds((2 * levels + levels // SUBLANES + 1, kinds, rows), f32)
     inputs = (tracers, column_depth, east_depth, u_clinic, v_clinic)
-    folded, tracers, column_depth, east_depth, u_clinic, v_clinic = call(
+    (inner, outer, own, folded, *inputs, own_inner, own_outer) = call(
         load_kernel,
         (
             packed,
+            packed,
+            sds((3 * band, width), f32),
+            packed,
             *(fetched(x) for x in inputs),
+            edges,
+            edges,
         ),
         "load",
-        (high, *inputs),
-        scratch=[pltpu.SemaphoreType.DMA((4 + kinds,))],
-        far=range(1, 6),
-    )
+        (*fields, *inputs),
+        scratch=[pltpu.VMEM(x.shape, x.dtype) for x in fields]
+        + [pltpu.SemaphoreType.DMA((8 + kinds,))],
+        far=range(9),
+    )
+    tracers, column_depth, east_depth, u_clinic, v_clinic = inputs
+    came_inner = lax.ppermute(inner, "lon", pairs_inner)
+    came_outer = lax.ppermute(outer, "lon", pairs_outer)
+
     groups = count // 4
     basis, *sends = call(
         basis_kernel,
         (sds((BASIS * band, width), f32),) + (sds((4, SLAB_ROWS, LANES), f32),) * groups,
         "solver_basis",
-        (own, below, above, folded),
+        (own, came_inner, came_outer, folded),
         scratch=[pltpu.VMEM((count, SLAB_ROWS, LANES), f32)],
+        cost=2000,
     )
     slabs = [sends[0]]
     for step in range(1, groups):
         pairs = [(i, (i + 4 * step) % count) for i in range(count)]
         slabs.append(lax.ppermute(sends[step], "lon", pairs))
-    east_going, own_west = call(
-        edge_kernel,
-        (
-            sds((2 * levels + levels // SUBLANES + 1, kinds, rows), f32),
-            sds((2 * levels, kinds, rows), f32),
-        ),
-        "pack_tracer_edges",
-        (tracers, column_depth, east_depth, u_clinic, basis),
-    )
-    from_west = lax.ppermute(east_going, "lon", ring)
-    from_east = lax.ppermute(own_west, "lon", ring_back)
-    (base,) = call(source_kernel, (held,), "sources", (tracers, column_depth, own_west), cost=70)
+    edge_inner = lax.ppermute(own_inner, "lon", pairs_inner)
+    edge_outer = lax.ppermute(own_outer, "lon", ring)
+    (base,) = call(source_kernel, (held,), "sources", (tracers, column_depth, own_inner), cost=2000)
     turned = (kinds, levels * columns // LANES, rows, LANES)
     change, face_north = call(
         north_kernel,
@@ -748,11 +769,11 @@
         "north_fluxes",
         (tracers, column_depth, v_clinic, base),
         scratch=[pltpu.VMEM((rows, LANES), f32)] + [pltpu.VMEM(turned[1:], f32)] * 5,
-        cost=70,
+        cost=2000,
     )
     quarter = sds((2, groups, SLAB_ROWS, LANES), f32)
     keep, send = call(core_kernel, (quarter, quarter), "split_cores", (*slabs, change))
-    came = lax.ppermute(send, "lon", [(i, i ^ 1) for i in range(count)])
+    came = lax.ppermute(send, "lon", pairs_inner)
     keep, send = call(half_kernel, (quarter, quarter), "split_halves", (keep, came))
     came = lax.ppermute(send, "lon", [(i, i ^ 2) for i in range(count)])
     base, face_east, face_west = call(
@@ -764,14 +785,20 @@
             column_depth,
             east_depth,
             u_clinic,
-            from_west,
-            from_east,
-            own_west,
+            edge_inner,
+            edge_outer,
+            own_inner,
+            own_outer,
             base,
             keep,
         ),
-        scratch=[pltpu.VMEM((levels, kinds, rows), f32)],
-        cost=70,
+        scratch=[
+            pltpu.VMEM((levels, kinds, rows), f32),
+            pltpu.VMEM(edges.shape, f32),
+            pltpu.VMEM(edges.shape, f32),
+            pltpu.VMEM(edges.shape, f32),
+        ],
+        cost=2000,
     )
     return tuple(
         call(

time: 38.6 us -> 34.2 us (0.89)
  starting transfers between devices: 15.8 us -> 12.4 us
  Pallas kernels: 18.2 us -> 17.1 us
    ppermute x5, starting transfers between devices: 9.51 us -> 6.97 us  [the longest x1 5.73 us: body(): edge_outer = lax.ppermute(own_outer, 'lon', ring)]
    ppermute x3, starting transfers between devices: 6.19 us -> 4.81 us  [body(): slabs.append(lax.ppermute(sends[step], 'lon', pairs))]
    pallas_call x10 -> x8, Pallas kernels: 18.2 us -> 17.1 us  [call(): pl.pallas_call(kernel, out_shape=out_shape, in_specs=[hbm if place in far...]
    ppermute x3, waiting for transfers between devices: 0.58 us -> 1.51 us  [body(): slabs.append(lax.ppermute(sends[step], 'lon', pairs))]
    ppermute x1, waiting for transfers between devices: 1.73 us -> 1.02 us  [body(): came = lax.ppermute(send, 'lon', [(i, i ^ 2) for i in range(count)])]
    ppermute x1, starting transfers between devices: 0.07 us -> 0.6 us  [body(): came = lax.ppermute(send, 'lon', [(i, i ^ 2) for i in range(count)])]
  transfers between devices with their start and end apart: 9 -> 9, of which waited for: 3 -> 3; matrix products, arithmetic and copies ran while one was open for 0% -> 0% of each run, Pallas kernels for 31% -> 29%
where the time goes in v5:
time: 34.2 us; the launch traced here: 34 us
  Pallas kernels  17.1 us (50%)
  starting transfers between devices  12.4 us (36%)
  waiting for transfers between devices  3.83 us (11%)
  between operations  0.72 us (2%)
    pallas_call x8, Pallas kernels, call(): pl.pallas_call(kernel, out_shape=out_shape, in_specs=[hbm if place in far...  17.1 us
    ppermute x1, starting transfers between devices, body(): edge_outer = lax.ppermute(own_outer, 'lon', ring)  5.73 us
    ppermute x3, starting transfers between devices, body(): slabs.append(lax.ppermute(sends[step], 'lon', pairs))  4.81 us
    ppermute x3, waiting for transfers between devices, body(): slabs.append(lax.ppermute(sends[step], 'lon', pairs))  1.51 us
    ppermute x1, waiting for transfers between devices, body(): came = lax.ppermute(send, 'lon', pairs_inner)  1.29 us
    ppermute x1, waiting for transfers between devices, body(): came = lax.ppermute(send, 'lon', [(i, i ^ 2) for i in range(count)])  1.02 us
  transfers between devices with their start and end apart: 9, of which 3 were waited for; matrix products, arithmetic and copies ran while one was open for 0% of the time, Pallas kernels for 29%

profile of v5, /device:TPU:0, one launch (start us, length us, event | category | flops | bytes accessed | tf_op | source)
XLA Modules:
  0.0 34.0 jit_solution(10238118002414991699)
XLA Ops:
  0.6 2.7 %load.1 = (f32[24,256]{1,0:T(8,128)S(1)}, f32[24,256]{1,0:T(8,128)S(1)}, f32[96,256]{1,0:T(8,128)S(1)}, f32[24,256]{1,0:T(8,128)S(1)}, f32[8,16,16,512]{3,2,1,0:...) custom-call(f32[32,256]{1,0:T(8,128)} %old_in.1, ...), custom_call_target="tpu_custom_call" | custom-call | tf_op jit(solution)/shard_map/load/pallas_call | solution.py:699
  3.4 0.5 %collective-permute-start = (f32[24,256]{1,0:T(8,128)S(1)}, f32[24,256]{1,0:T(8,128)S(1)}, u32[]{:S(2)}, u32[]{:S(2)}) collective-permute-start(f32[24,256]{1,0:T(8,128)S(1)} %get-tuple-element.28), channel_id=1, source_target_pairs={{0,1},{1,0},{2,3},{3,2},{4,5},{5,4},{6,7},{7,6},{8,9},{9,8},{10,11... | collective-permute-start | bytes 73736 | tf_op jit(solution)/shard_map/ppermute | solution.py:746
  3.9 0.7 %collective-permute-start.1 = (f32[24,256]{1,0:T(8,128)S(1)}, f32[24,256]{1,0:T(8,128)S(1)}, u32[]{:S(2)}, u32[]{:S(2)}) collective-permute-start(f32[24,256]{1,0:T(8,128)S(1)} %get-tuple-element.29), channel_id=1, source_target_pairs={{1,2},{2,1},{3,4},{4,3},{5,6},{6,5},{7,8},{8,7},{9,10},{10,9},{11,... | collective-permute-start | bytes 73736 | tf_op jit(solution)/shard_map/ppermute | solution.py:747
  4.5 5.7 %collective-permute-start.8 = (f32[35,8,512]{2,1,0:T(8,128)S(1)}, f32[35,8,512]{2,1,0:T(8,128)S(1)}, u32[]{:S(2)}, u32[]{:S(2)}) collective-permute-start(f32[35,8,512]{2,1,0:T(8,128)S(1)} %get-tuple-element.47.own_outer_ref), channel_id=1, source_target_pairs={{0,15},{1,2},{2,1},{3,4},{4,3},{5,6},{6,5},{7,8},{8,7},{9,10},{10,... | collective-permute-start | bytes 1720328 | tf_op jit(solution)/shard_map/ppermute | solution.py:763
  10.3 0.0 collective-permute-start.7
  10.3 2.4 %sources.1._.before_ref = f32[8,16,16,512]{3,2,1,0:T(8,128)S(1)} custom-call(f32[8,16,16,512]{3,2,1,0:T(8,128)S(1)} %get-tuple-element.35.tracers_ref, s32[16,512]{1,0:T(8,128)S(1)} %get-tuple-element.36.depth_ref, f32[35,8,512]{2,1,0:T(8,128)S(1)} %get-tuple-element.38._.own_inner_ref), custom_call_target="tpu_custom_call" | custom-call | flops 2097152000 | bytes 8388608 | tf_op jit(solution)/shard_map/sources/pallas_call | solution.py:699
  12.7 0.0 collective-permute-done.inner_ref
  12.7 0.0 collective-permute-done.1.outer_ref
  12.7 0.5 %solver_basis.1 = (f32[128,256]{1,0:T(8,128)S(1)}, f32[4,24,128]{2,1,0:T(8,128)S(1)}, f32[4,24,128]{2,1,0:T(8,128)S(1)}, f32[4,24,128]{2,1,0:T(8,128)S(1)}, f32[4,24,128]{2,1,0:T(8,128)S(1)}) custom-call(f32[96,256]{1,0:T(8,128)S(1)} %get-tuple-element.27.own_ref, f32[24,256]{1,0:T(8,128)S(1)} %collective-permute-done.inner_ref, ...), custom_call_target="tpu_custom_call" | custom-call | flops 2097152000 | bytes 8388608 | tf_op jit(solution)/shard_map/solver_basis/pallas_call | solution.py:699
  13.3 0.9 %collective-permute-start.2 = (f32[4,24,128]{2,1,0:T(8,128)S(1)}, f32[4,24,128]{2,1,0:T(8,128)S(1)}, u32[]{:S(2)}, u32[]{:S(2)}) collective-permute-start(f32[4,24,128]{2,1,0:T(8,128)S(1)} %get-tuple-element.32), channel_id=1, source_target_pairs={{0,4},{1,5},{2,6},{3,7},{4,8},{5,9},{6,10},{7,11},{8,12},{9,13},{1... | collective-permute-start | bytes 147464 | tf_op jit(solution)/shard_map/ppermute | solution.py:761
  14.1 2.6 %collective-permute-start.3 = (f32[4,24,128]{2,1,0:T(8,128)S(1)}, f32[4,24,128]{2,1,0:T(8,128)S(1)}, u32[]{:S(2)}, u32[]{:S(2)}) collective-permute-start(f32[4,24,128]{2,1,0:T(8,128)S(1)} %get-tuple-element.33), channel_id=1, source_target_pairs={{0,8},{1,9},{2,10},{3,11},{4,12},{5,13},{6,14},{7,15},{8,0},{9,1},... | collective-permute-start | bytes 147464 | tf_op jit(solution)/shard_map/ppermute | solution.py:761
  16.7 1.3 %collective-permute-start.4 = (f32[4,24,128]{2,1,0:T(8,128)S(1)}, f32[4,24,128]{2,1,0:T(8,128)S(1)}, u32[]{:S(2)}, u32[]{:S(2)}) collective-permute-start(f32[4,24,128]{2,1,0:T(8,128)S(1)} %get-tuple-element.34), channel_id=1, source_target_pairs={{0,12},{1,13},{2,14},{3,15},{4,0},{5,1},{6,2},{7,3},{8,4},{9,5},{1... | collective-permute-start | bytes 147464 | tf_op jit(solution)/shard_map/ppermute | solution.py:761
  18.1 3.5 %north_fluxes.1 = (f32[8,2,512,128]{3,2,1,0:T(8,128)S(1)}, f32[8,2,512,128]{3,2,1,0:T(8,128)S(1)}) custom-call(f32[8,16,16,512]{3,2,1,0:T(8,128)S(1)} %get-tuple-element.35.tracers_ref, s32[16,512]{1,0:T(8,128)S(1)} %get-tuple-element.36.depth_ref, f32[16,16,512]{2,1,0:T(8,128)S(1)} %get-tuple-element.37.v_ref, f32[8,16,16,512]{3,2,1,0:T(8,128)S(1)} %sources.1._.before_ref), custom_call_target="tpu_custom_call" | custom-call | flops 2097152000 | bytes 8388608 | tf_op jit(solution)/shard_map/north_fluxes/pallas_call | solution.py:699
  21.5 1.5 %collective-permute-done.2.refs_1_ = f32[4,24,128]{2,1,0:T(8,128)S(1)} collective-permute-done((f32[4,24,128]{2,1,0:T(8,128)S(1)}, f32[4,24,128]{2,1,0:T(8,128)S(1)}, u32[]{:S(2)}, u32[]{:S(2)}) %collective-permute-start.2) | collective-permute-done | bytes 49184 | tf_op jit(solution)/shard_map/ppermute | solution.py:761
  23.1 0.0 collective-permute-done.3.refs_2_
  23.1 0.0 collective-permute-done.4.refs_3_
  23.1 0.1 collective-permute-start.5
  23.2 1.3 %collective-permute-done.5.came_ref = f32[2,4,24,128]{3,2,1,0:T(8,128)S(1)} collective-permute-done((f32[2,4,24,128]{3,2,1,0:T(8,128)S(1)}, f32[2,4,24,128]{3,2,1,0:T(8,128)S(1)}, u32[]{:S(2)}, u32[]{:S(2)}) %collective-permute-start.5) | collective-permute-done | bytes 98336 | tf_op jit(solution)/shard_map/ppermute | solution.py:776
  24.5 0.6 %collective-permute-start.6 = (f32[2,4,24,128]{3,2,1,0:T(8,128)S(1)}, f32[2,4,24,128]{3,2,1,0:T(8,128)S(1)}, u32[]{:S(2)}, u32[]{:S(2)}) collective-permute-start(f32[2,4,24,128]{3,2,1,0:T(8,128)S(1)} %get-tuple-element.43), channel_id=1, source_target_pairs={{0,2},{1,3},{2,0},{3,1},{4,6},{5,7},{6,4},{7,5},{8,10},{9,11},{10,... | collective-permute-start | bytes 294920 | tf_op jit(solution)/shard_map/ppermute | solution.py:778
  25.1 0.0 collective-permute-done.8.outer_ref
  25.1 0.0 collective-permute-done.7.inner_ref
  25.1 3.3 %east_fluxes.1 = (f32[8,16,16,512]{3,2,1,0:T(8,128)S(1)}, f32[8,16,16,512]{3,2,1,0:T(8,128)S(1)}, f32[8,16,512]{2,1,0:T(8,128)S(1)}) custom-call(f32[8,16,16,512]{3,2,1,0:T(8,128)S(1)} %get-tuple-element.35.tracers_ref, s32[16,512]{1,0:T(8,128)S(1)} %get-tuple-element.36.depth_ref, s32[16,512]{1,0:T(8,128)S(1)} %get-tuple-element.45.east_depth_ref, ...), custom_call_target="tpu_custom_call" | custom-call | flops 2097152000 | bytes 8388608 | tf_op jit(solution)/shard_map/east_fluxes/pallas_call | solution.py:699
  28.4 1.0 %collective-permute-done.6.came_ref = f32[2,4,24,128]{3,2,1,0:T(8,128)S(1)} collective-permute-done((f32[2,4,24,128]{3,2,1,0:T(8,128)S(1)}, f32[2,4,24,128]{3,2,1,0:T(8,128)S(1)}, u32[]{:S(2)}, u32[]{:S(2)}) %collective-permute-start.6) | collective-permute-done | bytes 98336 | tf_op jit(solution)/shard_map/ppermute | solution.py:778
  29.4 4.6 %surface_update.1 = (f32[32,256]{1,0:T(8,128)}, f32[8,16,16,512]{3,2,1,0:T(8,128)}) custom-call(f32[2,4,24,128]{3,2,1,0:T(8,128)S(1)} %get-tuple-element.42._.kept_ref, f32[2,4,24,128]{3,2,1,0:T(8,128)S(1)} %collective-permute-done.6.came_ref, f32[128,256]{1,0:T(8,128)S(1)} %get-tuple-element.44.basis_ref, ...), custom_call_target="tpu_custom_call" | custom-call | tf_op jit(solution)/shard_map/surface_update/pallas_call | solution.py:699
  (2 shorter events, 0.0 us)
Async XLA Ops:
  3.4 9.4 %collective-permute-start = (f32[24,256]{1,0:T(8,128)S(1)}, f32[24,256]{1,0:T(8,128)S(1)}, u32[]{:S(2)}, u32[]{:S(2)}) collective-permute-start(f32[24,256]{1,0:T(8,128)S(1)} %get-tuple-element.28), channel_id=1, source_target_pairs={{0,1},{1,0},{2,3},{3,2},{4,5},{5,4},{6,7},{7,6},{8,9},{9,8},{10,11... | collective-permute-start | bytes 73736 | tf_op jit(solution)/shard_map/ppermute | solution.py:746
  3.9 8.9 %collective-permute-start.1 = (f32[24,256]{1,0:T(8,128)S(1)}, f32[24,256]{1,0:T(8,128)S(1)}, u32[]{:S(2)}, u32[]{:S(2)}) collective-permute-start(f32[24,256]{1,0:T(8,128)S(1)} %get-tuple-element.29), channel_id=1, source_target_pairs={{1,2},{2,1},{3,4},{4,3},{5,6},{6,5},{7,8},{8,7},{9,10},{10,9},{11,... | collective-permute-start | bytes 73736 | tf_op jit(solution)/shard_map/ppermute | solution.py:747
  4.5 20.5 %collective-permute-start.8 = (f32[35,8,512]{2,1,0:T(8,128)S(1)}, f32[35,8,512]{2,1,0:T(8,128)S(1)}, u32[]{:S(2)}, u32[]{:S(2)}) collective-permute-start(f32[35,8,512]{2,1,0:T(8,128)S(1)} %get-tuple-element.47.own_outer_ref), channel_id=1, source_target_pairs={{0,15},{1,2},{2,1},{3,4},{4,3},{5,6},{6,5},{7,8},{8,7},{9,10},{10,... | collective-permute-start | bytes 1720328 | tf_op jit(solution)/shard_map/ppermute | solution.py:763
  10.3 14.8 %collective-permute-start.7 = (f32[35,8,512]{2,1,0:T(8,128)S(1)}, f32[35,8,512]{2,1,0:T(8,128)S(1)}, u32[]{:S(2)}, u32[]{:S(2)}) collective-permute-start(f32[35,8,512]{2,1,0:T(8,128)S(1)} %get-tuple-element.38._.own_inner_ref), channel_id=1, source_target_pairs={{0,1},{1,0},{2,3},{3,2},{4,5},{5,4},{6,7},{7,6},{8,9},{9,8},{10,11... | collective-permute-start | bytes 1720328 | tf_op jit(solution)/shard_map/ppermute | solution.py:762
  13.3 9.8 %collective-permute-start.2 = (f32[4,24,128]{2,1,0:T(8,128)S(1)}, f32[4,24,128]{2,1,0:T(8,128)S(1)}, u32[]{:S(2)}, u32[]{:S(2)}) collective-permute-start(f32[4,24,128]{2,1,0:T(8,128)S(1)} %get-tuple-element.32), channel_id=1, source_target_pairs={{0,4},{1,5},{2,6},{3,7},{4,8},{5,9},{6,10},{7,11},{8,12},{9,13},{1... | collective-permute-start | bytes 147464 | tf_op jit(solution)/shard_map/ppermute | solution.py:761
  14.1 8.9 %collective-permute-start.3 = (f32[4,24,128]{2,1,0:T(8,128)S(1)}, f32[4,24,128]{2,1,0:T(8,128)S(1)}, u32[]{:S(2)}, u32[]{:S(2)}) collective-permute-start(f32[4,24,128]{2,1,0:T(8,128)S(1)} %get-tuple-element.33), channel_id=1, source_target_pairs={{0,8},{1,9},{2,10},{3,11},{4,12},{5,13},{6,14},{7,15},{8,0},{9,1},... | collective-permute-start | bytes 147464 | tf_op jit(solution)/shard_map/ppermute | solution.py:761
  16.7 6.3 %collective-permute-start.4 = (f32[4,24,128]{2,1,0:T(8,128)S(1)}, f32[4,24,128]{2,1,0:T(8,128)S(1)}, u32[]{:S(2)}, u32[]{:S(2)}) collective-permute-start(f32[4,24,128]{2,1,0:T(8,128)S(1)} %get-tuple-element.34), channel_id=1, source_target_pairs={{0,12},{1,13},{2,14},{3,15},{4,0},{5,1},{6,2},{7,3},{8,4},{9,5},{1... | collective-permute-start | bytes 147464 | tf_op jit(solution)/shard_map/ppermute | solution.py:761
  23.1 1.4 %collective-permute-start.5 = (f32[2,4,24,128]{3,2,1,0:T(8,128)S(1)}, f32[2,4,24,128]{3,2,1,0:T(8,128)S(1)}, u32[]{:S(2)}, u32[]{:S(2)}) collective-permute-start(f32[2,4,24,128]{3,2,1,0:T(8,128)S(1)} %get-tuple-element.41), channel_id=1, source_target_pairs={{0,1},{1,0},{2,3},{3,2},{4,5},{5,4},{6,7},{7,6},{8,9},{9,8},{10,11... | collective-permute-start | bytes 294920 | tf_op jit(solution)/shard_map/ppermute | solution.py:776
  24.5 4.9 %collective-permute-start.6 = (f32[2,4,24,128]{3,2,1,0:T(8,128)S(1)}, f32[2,4,24,128]{3,2,1,0:T(8,128)S(1)}, u32[]{:S(2)}, u32[]{:S(2)}) collective-permute-start(f32[2,4,24,128]{3,2,1,0:T(8,128)S(1)} %get-tuple-element.43), channel_id=1, source_target_pairs={{0,2},{1,3},{2,0},{3,1},{4,6},{5,7},{6,4},{7,5},{8,10},{9,11},{10,... | collective-permute-start | bytes 294920 | tf_op jit(solution)/shard_map/ppermute | solution.py:778

commit v6 on v5

--- a/solution.py
+++ b/solution.py
@@ -41,9 +41,10 @@
     outer_ref,
     folded_ref,
     basis_ref,
-    *refs,
+    keep_ref,
+    send_ref,
+    slabs_ref,
 ):
-    send_refs, slabs_ref = refs[:-1], refs[-1]
     rows, width = own_ref.shape[0] // 3, own_ref.shape[1]
     count = slabs_ref.shape[0]
     columns = width // count
@@ -103,33 +104,32 @@
             jnp.zeros((SLAB_ROWS - columns - 3, LANES), jnp.float32),
         ]
         slabs_ref[target] = jnp.concatenate(pieces, axis=0)
-    groups = len(send_refs)
-    group = lax.axis_index("lon") // 4
+    core = lax.rem(lax.axis_index("lon"), 2)
+    for pair in range(count // 2):
+        keep_ref[pair] = slabs_ref[2 * pair + core]
+        send_ref[pair] = slabs_ref[2 * pair + 1 - core]
+
+
+def spread_kernel(kept_ref, came_ref, *out_refs):
+    here = lax.axis_index("lon")
+    core, group = lax.rem(here, 2), here // 4
+    groups = len(out_refs)
     for step in range(groups):
         target = lax.rem(group + step, groups)
-        for place in range(4):
-            send_refs[step][place] = slabs_ref[4 * target + place]
-
-
-def core_kernel(*refs):
+        for y in range(2):
+            out_refs[step][y, core] = kept_ref[2 * target + y]
+            out_refs[step][y, 1 - core] = came_ref[2 * target + y]
+
+
+def half_kernel(*refs):
     came_refs, (_, keep_ref, send_ref) = refs[:-3], refs[-3:]
     here = lax.axis_index("lon")
-    core, group = lax.rem(here, 2), here // 4
+    half, group = lax.rem(here // 2, 2), here // 4
     groups = len(came_refs)
     for step in range(groups):
         source = lax.rem(group + groups - step, groups)
-        for y in range(2):
-            keep_ref[y, source] = came_refs[step][2 * y + core]
-            send_ref[y, source] = came_refs[step][2 * y + 1 - core]
-
-
-def half_kernel(kept_ref, came_ref, keep_ref, send_ref):
-    here = lax.axis_index("lon")
-    core, half = lax.rem(here, 2), lax.rem(here // 2, 2)
-    keep_ref[core] = kept_ref[half]
-    keep_ref[1 - core] = came_ref[half]
-    send_ref[core] = kept_ref[1 - half]
-    send_ref[1 - core] = came_ref[1 - half]
+        keep_ref[source] = came_refs[step][half]
+        send_ref[source] = came_refs[step][1 - half]
 
 
 def basis_weights(moments):
@@ -568,19 +568,19 @@
     sems,
 ):
     half = lax.rem(lax.axis_index("lon") // 2, 2)
-    for source in range(kept_ref.shape[1]):
+    for source in range(kept_ref.shape[0]):
         for core in range(2):
-            slabs_ref[4 * source + 2 * half + core] = kept_ref[core, source]
-            slabs_ref[4 * source + 2 * (1 - half) + core] = came_ref[core, source]
+            slabs_ref[4 * source + 2 * half + core] = kept_ref[source, core]
+            slabs_ref[4 * source + 2 * (1 - half) + core] = came_ref[source, core]
     kinds, levels, columns, rows = base_ref.shape
     blocks, count = columns // SUBLANES, rows // LANES
     places = grid_tiles(columns, rows)
     sources, slab_rows, _ = slabs_ref.shape
     band, width = surface_ref.shape
-    moment_row = slabs_ref[0, columns + 2 : columns + 3]
-    for source in range(1, sources):
-        moment_row = moment_row + slabs_ref[source, columns + 2 : columns + 3]
-    dots = [moment_row[:, m : m + 1] for m in range(2 * BASIS)]
+    parts = [slabs_ref[source, columns + 2 : columns + 3] for source in range(sources)]
+    while len(parts) > 1:
+        parts = [a + b for a, b in zip(parts[::2], parts[1::2])]
+    dots = [jnp.broadcast_to(parts[0][:, m : m + 1], (1, LANES)) for m in range(2 * BASIS)]
     weights = basis_weights(
         dots[:2] + [2.0 * dots[m] - dots[m % 2] for m in range(2, 2 * BASIS)]
     )
@@ -588,10 +588,12 @@
     lane_weight = jnp.zeros((1, LANES), jnp.float32)
     for k in range(BASIS):
         lane_weight = jnp.where(lane_group == k, weights[k], lane_weight)
-    surface = weights[0] * basis_ref[:band]
-    for k in range(1, BASIS):
-        surface = surface + weights[k] * basis_ref[k * band : (k + 1) * band]
-    surface_ref[...] = surface
+    for tile in range(width // LANES):
+        part = slice(tile * LANES, (tile + 1) * LANES)
+        surface = weights[0] * basis_ref[:band, part]
+        for k in range(1, BASIS):
+            surface = surface + weights[k] * basis_ref[k * band : (k + 1) * band, part]
+        surface_ref[:, part] = surface
 
     fill = LANES // band
     group_full = lax.broadcasted_iota(jnp.int32, (slab_rows, LANES), 1) // band
@@ -747,13 +749,21 @@
     came_outer = lax.ppermute(outer, "lon", pairs_outer)
 
     groups = count // 4
-    basis, *sends = call(
+    half_slabs = sds((count // 2, SLAB_ROWS, LANES), f32)
+    basis, keep, send = call(
         basis_kernel,
-        (sds((BASIS * band, width), f32),) + (sds((4, SLAB_ROWS, LANES), f32),) * groups,
+        (sds((BASIS * band, width), f32), half_slabs, half_slabs),
         "solver_basis",
         (own, came_inner, came_outer, folded),
         scratch=[pltpu.VMEM((count, SLAB_ROWS, LANES), f32)],
         cost=2000,
+    )
+    came = lax.ppermute(send, "lon", pairs_inner)
+    sends = call(
+        spread_kernel,
+        (sds((2, 2, SLAB_ROWS, LANES), f32),) * groups,
+        "spread_slabs",
+        (keep, came),
     )
     slabs = [sends[0]]
     for step in range(1, groups):
@@ -767,14 +777,12 @@
         north_kernel,
         (pltpu.VMEM(turned, f32), pltpu.VMEM(turned, f32)),
         "north_fluxes",
-        (tracers, column_depth, v_clinic, base),
+        (tracers, column_depth, v_clinic, sends[0]),
         scratch=[pltpu.VMEM((rows, LANES), f32)] + [pltpu.VMEM(turned[1:], f32)] * 5,
         cost=2000,
     )
-    quarter = sds((2, groups, SLAB_ROWS, LANES), f32)
-    keep, send = call(core_kernel, (quarter, quarter), "split_cores", (*slabs, change))
-    came = lax.ppermute(send, "lon", pairs_inner)
-    keep, send = call(half_kernel, (quarter, quarter), "split_halves", (keep, came))
+    quarter = sds((groups, 2, SLAB_ROWS, LANES), f32)
+    keep, send = call(half_kernel, (quarter, quarter), "split_halves", (*slabs, change))
     came = lax.ppermute(send, "lon", [(i, i ^ 2) for i in range(count)])
     base, face_east, face_west = call(
         east_kernel,

time: 34.2 us -> 32.6 us (0.953)
  waiting for transfers between devices: 3.83 us -> 0.11 us
  starting transfers between devices: 12.4 us -> 15.3 us
  Pallas kernels: 17.1 us -> 16.3 us
    ppermute x1, starting transfers between devices: 0.6 us -> 2.09 us  [body(): came = lax.ppermute(send, 'lon', [(i, i ^ 2) for i in range(count)])]
    ppermute x3, waiting for transfers between devices: 1.51 us -> 0.09 us  [body(): slabs.append(lax.ppermute(sends[step], 'lon', pairs))]
    ppermute x1, waiting for transfers between devices: 1.29 us -> 0.01 us  [body(): came = lax.ppermute(send, 'lon', pairs_inner)]
    ppermute x1, waiting for transfers between devices: 1.02 us -> 0.01 us  [body(): came = lax.ppermute(send, 'lon', [(i, i ^ 2) for i in range(count)])]
    ppermute x3, starting transfers between devices: 4.81 us -> 5.75 us  [body(): slabs.append(lax.ppermute(sends[step], 'lon', pairs))]
    pallas_call x8, Pallas kernels: 17.1 us -> 16.3 us  [call(): pl.pallas_call(kernel, out_shape=out_shape, in_specs=[hbm if place in far...]
    ppermute x1, starting transfers between devices: 0.07 us -> 0.58 us  [body(): came = lax.ppermute(send, 'lon', pairs_inner)]
  transfers between devices with their start and end apart: 9 -> 9, of which waited for: 3 -> 1; matrix products, arithmetic and copies ran while one was open for 0% -> 0% of each run, Pallas kernels for 29% -> 30%
where the time goes in v6:
time: 32.6 us; the launch traced here: 32.4 us
  Pallas kernels  16.3 us (50%)
  starting transfers between devices  15.3 us (47%)
  between operations  0.72 us (2%)
    pallas_call x8, Pallas kernels, call(): pl.pallas_call(kernel, out_shape=out_shape, in_specs=[hbm if place in far...  16.3 us
    ppermute x3, starting transfers between devices, body(): slabs.append(lax.ppermute(sends[step], 'lon', pairs))  5.75 us
    ppermute x1, starting transfers between devices, body(): edge_outer = lax.ppermute(own_outer, 'lon', ring)  5.73 us
    ppermute x1, starting transfers between devices, body(): came = lax.ppermute(send, 'lon', [(i, i ^ 2) for i in range(count)])  2.09 us
  transfers between devices with their start and end apart: 9, of which 1 were waited for; matrix products, arithmetic and copies ran while one was open for 0% of the time, Pallas kernels for 30%

profile of v6, /device:TPU:0, one launch (start us, length us, event | category | flops | bytes accessed | tf_op | source)
XLA Modules:
  0.0 32.4 jit_solution(17964773622695108386)
XLA Ops:
  0.6 2.7 %load.1 = (f32[24,256]{1,0:T(8,128)S(1)}, f32[24,256]{1,0:T(8,128)S(1)}, f32[96,256]{1,0:T(8,128)S(1)}, f32[24,256]{1,0:T(8,128)S(1)}, f32[8,16,16,512]{3,2,1,0:...) custom-call(f32[32,256]{1,0:T(8,128)} %old_in.1, ...), custom_call_target="tpu_custom_call" | custom-call | tf_op jit(solution)/shard_map/load/pallas_call | solution.py:701
  3.4 0.5 %collective-permute-start = (f32[24,256]{1,0:T(8,128)S(1)}, f32[24,256]{1,0:T(8,128)S(1)}, u32[]{:S(2)}, u32[]{:S(2)}) collective-permute-start(f32[24,256]{1,0:T(8,128)S(1)} %get-tuple-element.28), channel_id=1, source_target_pairs={{0,1},{1,0},{2,3},{3,2},{4,5},{5,4},{6,7},{7,6},{8,9},{9,8},{10,11... | collective-permute-start | bytes 73736 | tf_op jit(solution)/shard_map/ppermute | solution.py:748
  3.9 0.7 %collective-permute-start.1 = (f32[24,256]{1,0:T(8,128)S(1)}, f32[24,256]{1,0:T(8,128)S(1)}, u32[]{:S(2)}, u32[]{:S(2)}) collective-permute-start(f32[24,256]{1,0:T(8,128)S(1)} %get-tuple-element.29), channel_id=1, source_target_pairs={{1,2},{2,1},{3,4},{4,3},{5,6},{6,5},{7,8},{8,7},{9,10},{10,9},{11,... | collective-permute-start | bytes 73736 | tf_op jit(solution)/shard_map/ppermute | solution.py:749
  4.5 5.7 %collective-permute-start.8 = (f32[35,8,512]{2,1,0:T(8,128)S(1)}, f32[35,8,512]{2,1,0:T(8,128)S(1)}, u32[]{:S(2)}, u32[]{:S(2)}) collective-permute-start(f32[35,8,512]{2,1,0:T(8,128)S(1)} %get-tuple-element.47.own_outer_ref), channel_id=1, source_target_pairs={{0,15},{1,2},{2,1},{3,4},{4,3},{5,6},{6,5},{7,8},{8,7},{9,10},{10,... | collective-permute-start | bytes 1720328 | tf_op jit(solution)/shard_map/ppermute | solution.py:773
  10.3 0.0 collective-permute-start.7
  10.3 0.0 collective-permute-done.inner_ref
  10.3 0.0 collective-permute-done.1.outer_ref
  10.3 0.5 %solver_basis.1 = (f32[128,256]{1,0:T(8,128)S(1)}, f32[8,24,128]{2,1,0:T(8,128)S(1)}, f32[8,24,128]{2,1,0:T(8,128)S(1)}) custom-call(f32[96,256]{1,0:T(8,128)S(1)} %get-tuple-element.27.own_ref, f32[24,256]{1,0:T(8,128)S(1)} %collective-permute-done.inner_ref, f32[24,256]{1,0:T(8,128)S(1)} %collective-permute-done.1.outer_ref, ...), custom_call_target="tpu_custom_call" | custom-call | flops 2097152000 | bytes 8388608 | tf_op jit(solution)/shard_map/solver_basis/pallas_call | solution.py:701
  10.8 0.6 %collective-permute-start.2 = (f32[8,24,128]{2,1,0:T(8,128)S(1)}, f32[8,24,128]{2,1,0:T(8,128)S(1)}, u32[]{:S(2)}, u32[]{:S(2)}) collective-permute-start(f32[8,24,128]{2,1,0:T(8,128)S(1)} %get-tuple-element.32), channel_id=1, source_target_pairs={{0,1},{1,0},{2,3},{3,2},{4,5},{5,4},{6,7},{7,6},{8,9},{9,8},{10,11... | collective-permute-start | bytes 294920 | tf_op jit(solution)/shard_map/ppermute | solution.py:761
  11.4 2.4 %sources.1.before_ref = f32[8,16,16,512]{3,2,1,0:T(8,128)S(1)} custom-call(f32[8,16,16,512]{3,2,1,0:T(8,128)S(1)} %get-tuple-element.37.tracers_ref, s32[16,512]{1,0:T(8,128)S(1)} %get-tuple-element.38.depth_ref, f32[35,8,512]{2,1,0:T(8,128)S(1)} %get-tuple-element.46._.own_inner_ref), custom_call_target="tpu_custom_call" | custom-call | flops 2097152000 | bytes 8388608 | tf_op jit(solution)/shard_map/sources/pallas_call | solution.py:701
  13.8 0.0 collective-permute-done.2.came_ref
  13.9 1.8 %collective-permute-start.3 = (f32[2,2,24,128]{3,2,1,0:T(8,128)S(1)}, f32[2,2,24,128]{3,2,1,0:T(8,128)S(1)}, u32[]{:S(2)}, u32[]{:S(2)}) collective-permute-start(f32[2,2,24,128]{3,2,1,0:T(8,128)S(1)} %get-tuple-element.34), channel_id=1, source_target_pairs={{0,4},{1,5},{2,6},{3,7},{4,8},{5,9},{6,10},{7,11},{8,12},{9,13},{1... | collective-permute-start | bytes 147464 | tf_op jit(solution)/shard_map/ppermute | solution.py:771
  15.7 2.6 %collective-permute-start.4 = (f32[2,2,24,128]{3,2,1,0:T(8,128)S(1)}, f32[2,2,24,128]{3,2,1,0:T(8,128)S(1)}, u32[]{:S(2)}, u32[]{:S(2)}) collective-permute-start(f32[2,2,24,128]{3,2,1,0:T(8,128)S(1)} %get-tuple-element.35), channel_id=1, source_target_pairs={{0,8},{1,9},{2,10},{3,11},{4,12},{5,13},{6,14},{7,15},{8,0},{9,1},... | collective-permute-start | bytes 147464 | tf_op jit(solution)/shard_map/ppermute | solution.py:771
  18.3 1.3 %collective-permute-start.5 = (f32[2,2,24,128]{3,2,1,0:T(8,128)S(1)}, f32[2,2,24,128]{3,2,1,0:T(8,128)S(1)}, u32[]{:S(2)}, u32[]{:S(2)}) collective-permute-start(f32[2,2,24,128]{3,2,1,0:T(8,128)S(1)} %get-tuple-element.36), channel_id=1, source_target_pairs={{0,12},{1,13},{2,14},{3,15},{4,0},{5,1},{6,2},{7,3},{8,4},{9,5},{1... | collective-permute-start | bytes 147464 | tf_op jit(solution)/shard_map/ppermute | solution.py:771
  19.6 3.5 %north_fluxes.1 = (f32[8,2,512,128]{3,2,1,0:T(8,128)S(1)}, f32[8,2,512,128]{3,2,1,0:T(8,128)S(1)}) custom-call(f32[8,16,16,512]{3,2,1,0:T(8,128)S(1)} %get-tuple-element.37.tracers_ref, s32[16,512]{1,0:T(8,128)S(1)} %get-tuple-element.38.depth_ref, f32[16,16,512]{2,1,0:T(8,128)S(1)} %get-tuple-element.39.v_ref, f32[2,2,24,128]{3,2,1,0:T(8,128)S(1)} %get-tuple-element.33._.refs_0_), custom_call_target="tpu_custom_call" | custom-call | flops 2097152000 | bytes 8388608 | tf_op jit(solution)/shard_map/north_fluxes/pallas_call | solution.py:701
  23.1 0.0 collective-permute-done.3.refs_1_
  23.1 0.0 collective-permute-done.4.refs_2_
  23.1 0.1 collective-permute-done.5.refs_3_
  23.2 2.1 %collective-permute-start.6 = (f32[4,2,24,128]{3,2,1,0:T(8,128)S(1)}, f32[4,2,24,128]{3,2,1,0:T(8,128)S(1)}, u32[]{:S(2)}, u32[]{:S(2)}) collective-permute-start(f32[4,2,24,128]{3,2,1,0:T(8,128)S(1)} %get-tuple-element.42), channel_id=1, source_target_pairs={{0,2},{1,3},{2,0},{3,1},{4,6},{5,7},{6,4},{7,5},{8,10},{9,11},{10,... | collective-permute-start | bytes 294920 | tf_op jit(solution)/shard_map/ppermute | solution.py:786
  25.3 0.0 collective-permute-done.8.outer_ref
  25.3 0.0 collective-permute-done.7.inner_ref
  25.3 3.3 %east_fluxes.1 = (f32[8,16,16,512]{3,2,1,0:T(8,128)S(1)}, f32[8,16,16,512]{3,2,1,0:T(8,128)S(1)}, f32[8,16,512]{2,1,0:T(8,128)S(1)}) custom-call(f32[8,16,16,512]{3,2,1,0:T(8,128)S(1)} %get-tuple-element.37.tracers_ref, s32[16,512]{1,0:T(8,128)S(1)} %get-tuple-element.38.depth_ref, s32[16,512]{1,0:T(8,128)S(1)} %get-tuple-element.44.east_depth_ref, ...), custom_call_target="tpu_custom_call" | custom-call | flops 2097152000 | bytes 8388608 | tf_op jit(solution)/shard_map/east_fluxes/pallas_call | solution.py:701
  28.6 0.0 collective-permute-done.6.came_ref
  28.7 3.8 %surface_update.1 = (f32[32,256]{1,0:T(8,128)}, f32[8,16,16,512]{3,2,1,0:T(8,128)}) custom-call(f32[4,2,24,128]{3,2,1,0:T(8,128)S(1)} %get-tuple-element.41._.kept_ref, f32[4,2,24,128]{3,2,1,0:T(8,128)S(1)} %collective-permute-done.6.came_ref, f32[128,256]{1,0:T(8,128)S(1)} %get-tuple-element.43.basis_ref, ...), custom_call_target="tpu_custom_call" | custom-call | tf_op jit(solution)/shard_map/surface_update/pallas_call | solution.py:701
  (2 shorter events, 0.1 us)
Async XLA Ops:
  3.4 6.9 %collective-permute-start = (f32[24,256]{1,0:T(8,128)S(1)}, f32[24,256]{1,0:T(8,128)S(1)}, u32[]{:S(2)}, u32[]{:S(2)}) collective-permute-start(f32[24,256]{1,0:T(8,128)S(1)} %get-tuple-element.28), channel_id=1, source_target_pairs={{0,1},{1,0},{2,3},{3,2},{4,5},{5,4},{6,7},{7,6},{8,9},{9,8},{10,11... | collective-permute-start | bytes 73736 | tf_op jit(solution)/shard_map/ppermute | solution.py:748
  3.9 6.4 %collective-permute-start.1 = (f32[24,256]{1,0:T(8,128)S(1)}, f32[24,256]{1,0:T(8,128)S(1)}, u32[]{:S(2)}, u32[]{:S(2)}) collective-permute-start(f32[24,256]{1,0:T(8,128)S(1)} %get-tuple-element.29), channel_id=1, source_target_pairs={{1,2},{2,1},{3,4},{4,3},{5,6},{6,5},{7,8},{8,7},{9,10},{10,9},{11,... | collective-permute-start | bytes 73736 | tf_op jit(solution)/shard_map/ppermute | solution.py:749
  4.5 20.8 %collective-permute-start.8 = (f32[35,8,512]{2,1,0:T(8,128)S(1)}, f32[35,8,512]{2,1,0:T(8,128)S(1)}, u32[]{:S(2)}, u32[]{:S(2)}) collective-permute-start(f32[35,8,512]{2,1,0:T(8,128)S(1)} %get-tuple-element.47.own_outer_ref), channel_id=1, source_target_pairs={{0,15},{1,2},{2,1},{3,4},{4,3},{5,6},{6,5},{7,8},{8,7},{9,10},{10,... | collective-permute-start | bytes 1720328 | tf_op jit(solution)/shard_map/ppermute | solution.py:773
  10.3 15.0 %collective-permute-start.7 = (f32[35,8,512]{2,1,0:T(8,128)S(1)}, f32[35,8,512]{2,1,0:T(8,128)S(1)}, u32[]{:S(2)}, u32[]{:S(2)}) collective-permute-start(f32[35,8,512]{2,1,0:T(8,128)S(1)} %get-tuple-element.46._.own_inner_ref), channel_id=1, source_target_pairs={{0,1},{1,0},{2,3},{3,2},{4,5},{5,4},{6,7},{7,6},{8,9},{9,8},{10,11... | collective-permute-start | bytes 1720328 | tf_op jit(solution)/shard_map/ppermute | solution.py:772
  10.8 3.0 %collective-permute-start.2 = (f32[8,24,128]{2,1,0:T(8,128)S(1)}, f32[8,24,128]{2,1,0:T(8,128)S(1)}, u32[]{:S(2)}, u32[]{:S(2)}) collective-permute-start(f32[8,24,128]{2,1,0:T(8,128)S(1)} %get-tuple-element.32), channel_id=1, source_target_pairs={{0,1},{1,0},{2,3},{3,2},{4,5},{5,4},{6,7},{7,6},{8,9},{9,8},{10,11... | collective-permute-start | bytes 294920 | tf_op jit(solution)/shard_map/ppermute | solution.py:761
  13.9 9.2 %collective-permute-start.3 = (f32[2,2,24,128]{3,2,1,0:T(8,128)S(1)}, f32[2,2,24,128]{3,2,1,0:T(8,128)S(1)}, u32[]{:S(2)}, u32[]{:S(2)}) collective-permute-start(f32[2,2,24,128]{3,2,1,0:T(8,128)S(1)} %get-tuple-element.34), channel_id=1, source_target_pairs={{0,4},{1,5},{2,6},{3,7},{4,8},{5,9},{6,10},{7,11},{8,12},{9,13},{1... | collective-permute-start | bytes 147464 | tf_op jit(solution)/shard_map/ppermute | solution.py:771
  15.7 7.4 %collective-permute-start.4 = (f32[2,2,24,128]{3,2,1,0:T(8,128)S(1)}, f32[2,2,24,128]{3,2,1,0:T(8,128)S(1)}, u32[]{:S(2)}, u32[]{:S(2)}) collective-permute-start(f32[2,2,24,128]{3,2,1,0:T(8,128)S(1)} %get-tuple-element.35), channel_id=1, source_target_pairs={{0,8},{1,9},{2,10},{3,11},{4,12},{5,13},{6,14},{7,15},{8,0},{9,1},... | collective-permute-start | bytes 147464 | tf_op jit(solution)/shard_map/ppermute | solution.py:771
  18.3 4.9 %collective-permute-start.5 = (f32[2,2,24,128]{3,2,1,0:T(8,128)S(1)}, f32[2,2,24,128]{3,2,1,0:T(8,128)S(1)}, u32[]{:S(2)}, u32[]{:S(2)}) collective-permute-start(f32[2,2,24,128]{3,2,1,0:T(8,128)S(1)} %get-tuple-element.36), channel_id=1, source_target_pairs={{0,12},{1,13},{2,14},{3,15},{4,0},{5,1},{6,2},{7,3},{8,4},{9,5},{1... | collective-permute-start | bytes 147464 | tf_op jit(solution)/shard_map/ppermute | solution.py:771
  23.2 5.4 %collective-permute-start.6 = (f32[4,2,24,128]{3,2,1,0:T(8,128)S(1)}, f32[4,2,24,128]{3,2,1,0:T(8,128)S(1)}, u32[]{:S(2)}, u32[]{:S(2)}) collective-permute-start(f32[4,2,24,128]{3,2,1,0:T(8,128)S(1)} %get-tuple-element.42), channel_id=1, source_target_pairs={{0,2},{1,3},{2,0},{3,1},{4,6},{5,7},{6,4},{7,5},{8,10},{9,11},{10,... | collective-permute-start | bytes 294920 | tf_op jit(solution)/shard_map/ppermute | solution.py:786

commit v7 on v6

--- a/solution.py
+++ b/solution.py
@@ -33,6 +33,33 @@
 
 def is_even():
     return lax.rem(lax.axis_index("lon"), 2) == 0
+
+
+def pack_kernel(old_in, force_in, coeff_in, mask_in, inner_ref, outer_ref, own_ref, *scratch):
+    old_ref, force_ref, coeff_ref, mask_ref, sems = scratch
+    copies = [
+        pltpu.make_async_copy(source, target, sems.at[place])
+        for place, (source, target) in enumerate(
+            zip((old_in, force_in, coeff_in, mask_in), (old_ref, force_ref, coeff_ref, mask_ref))
+        )
+    ]
+    for copy in copies:
+        copy.start()
+    for copy in copies:
+        copy.wait()
+    rows = old_ref.shape[0]
+    coeff = coeff_ref[...]
+    fields = (
+        coeff * old_ref[...] + force_ref[...],
+        coeff,
+        mask_ref[...].astype(jnp.float32),
+    )
+    for place, field in enumerate(fields):
+        low, high = field[:HALO], field[rows - HALO :]
+        part = slice(HALO * place, HALO * (place + 1))
+        inner_ref[part] = jnp.where(is_even(), high, low)
+        outer_ref[part] = jnp.where(is_even(), low, high)
+        own_ref[rows * place : rows * (place + 1)] = field
 
 
 def basis_kernel(
@@ -187,112 +214,52 @@
     return tile
 
 
-def load_kernel(
-    old_in,
-    force_in,
-    coeff_in,
-    mask_in,
-    tracers_in,
-    depth_in,
-    east_depth_in,
-    u_in,
-    v_in,
-    inner_ref,
-    outer_ref,
-    own_ref,
-    folded_ref,
-    tracers_ref,
-    depth_ref,
-    east_depth_ref,
-    u_ref,
-    v_ref,
-    edge_inner_ref,
-    edge_outer_ref,
-    old_ref,
-    force_ref,
-    coeff_ref,
-    mask_ref,
-    sems,
-):
-    kinds, levels, columns, rows = tracers_ref.shape
-    band = old_ref.shape[0]
-    moves = [
-        (old_in, old_ref),
-        (force_in, force_ref),
-        (coeff_in, coeff_ref),
-        (mask_in, mask_ref),
-        (depth_in, depth_ref),
-        (east_depth_in, east_depth_ref),
-        (u_in, u_ref),
-    ]
-    moves += [(tracers_in.at[kind], tracers_ref.at[kind]) for kind in range(kinds)]
-    moves += [(v_in, v_ref)]
-    copies = [
-        pltpu.make_async_copy(source, target, sems.at[place])
-        for place, (source, target) in enumerate(moves)
-    ]
-    for copy in copies:
-        copy.start()
-    for copy in copies[:4]:
-        copy.wait()
-    coeff = coeff_ref[...]
-    fields = (
-        coeff * old_ref[...] + force_ref[...],
-        coeff,
-        mask_ref[...].astype(jnp.float32),
-    )
-    for place, field in enumerate(fields):
-        low, high = field[:HALO], field[band - HALO :]
+def fold_kernel(high_ref, _, folded_ref):
+    tiles = high_ref.shape[1] // LANES
+    for place in range(3):
         part = slice(HALO * place, HALO * (place + 1))
-        inner_ref[part] = jnp.where(is_even(), high, low)
-        outer_ref[part] = jnp.where(is_even(), low, high)
-        own_ref[band * place : band * (place + 1)] = field
-        tiles = high.shape[1] // LANES
         for tile in range(tiles):
             other = tiles - 1 - tile
             folded_ref[part, tile * LANES : (tile + 1) * LANES] = reverse_tile(
-                high[:, other * LANES : (other + 1) * LANES]
+                high_ref[part, other * LANES : (other + 1) * LANES]
             )
-    for copy in copies[4:7]:
-        copy.wait()
-
-    def pack(kind, first, target_ref):
+
+
+def edge_kernel(tracers_ref, depth_ref, east_depth_ref, u_ref, _, inner_ref, outer_ref):
+    kinds, levels, columns, rows = tracers_ref.shape
+
+    def pack(first, target_ref):
         for side in range(2):
             column = first + side
             for z in range(levels):
                 wet = (z < depth_ref[column : column + 1]).astype(jnp.float32)
-                target_ref[2 * z + side, kind : kind + 1] = (
-                    tracers_ref[kind, z, column : column + 1] * wet
-                )
+                for kind in range(kinds):
+                    target_ref[2 * z + side, kind : kind + 1] = (
+                        tracers_ref[kind, z, column : column + 1] * wet
+                    )
 
     def pack_faces(target_ref):
         for z in range(levels):
             place = 2 * levels + z // SUBLANES
             row = z % SUBLANES
-            target_ref[place, row : row + 1] = u_ref[z, columns - 1 : columns]
+            target_ref[place, row : row + 1] = u_ref[z, columns - 1 :]
         place = 2 * levels + levels // SUBLANES
         target_ref[place] = jnp.broadcast_to(
             east_depth_ref[columns - 1 : columns].astype(jnp.float32), (SUBLANES, rows)
         )
 
-    pack_faces(edge_inner_ref)
-    pack_faces(edge_outer_ref)
-
-    def pack_all(inner_column, outer_column):
-        for kind in range(kinds):
-            copies[7 + kind].wait()
-            pack(kind, inner_column, edge_inner_ref)
-            pack(kind, outer_column, edge_outer_ref)
-
     @pl.when(is_even())
     def _():
-        pack_all(columns - 2, 0)
+        pack(columns - 2, inner_ref)
+        pack(0, outer_ref)
 
     @pl.when(jnp.logical_not(is_even()))
     def _():
-        pack_all(0, columns - 2)
-
-    copies[-1].wait()
+        pack(0, inner_ref)
+        pack(columns - 2, outer_ref)
+
+    pack_faces(inner_ref)
+    pack_faces(outer_ref)
 
 
 def grid_tiles(columns, rows):
@@ -371,7 +338,7 @@
     )
 
 
-def source_kernel(tracers_ref, depth_ref, _, base_ref):
+def source_kernel(tracers_ref, depth_ref, _, base_ref, masked_ref):
     kinds, levels, columns, rows = tracers_ref.shape
     places = grid_tiles(columns, rows)
 
@@ -387,12 +354,14 @@
             mix_up = wet * mix_up_level
             mix_down = jnp.where(level + 1 < depth_here, VERT_DIFF, 0.0)
             values = [tracers_ref[(kind, level) + at] for kind in range(kinds)]
-            sources = redox_sources([value * wet for value in values])
+            masked = [value * wet for value in values]
+            sources = redox_sources(masked)
             for kind in range(kinds):
+                masked_ref[(kind, level) + at] = masked[kind]
                 value = values[kind]
                 down = (tracers_ref[(kind, below) + at] - value) * mix_down
                 up = (value - tracers_ref[(kind, above) + at]) * mix_up
-                base_ref[(kind, level) + at] = value + (wet * sources[kind] + (down - up))
+                base_ref[(kind, level) + at] = value + (sources[kind] + (down - up))
 
 
 def turn(ref_block, target_ref, start=0):
@@ -415,20 +384,19 @@
 
 
 def north_kernel(
-    tracers_ref,
+    masked_in,
     depth_ref,
     v_ref,
     _,
     change_ref,
     face_ref,
     depth_turned_ref,
-    wet_ref,
     scale_ref,
     flow_ref,
     mix_ref,
     masked_ref,
 ):
-    kinds, levels, columns, rows = tracers_ref.shape
+    kinds, levels, columns, rows = masked_in.shape
     per_layer = LANES // columns
     layers = levels // per_layer
     blocks = rows // SUBLANES
@@ -445,7 +413,6 @@
             after = depth_turned_ref[row_tile(block + 1)] if block + 1 < blocks else None
             is_open = level < jnp.minimum(here, shifted(here, after, 1))
             scale = jnp.where(is_open, 1.0 / 12.0, 0.0)
-            wet_ref[layer, at] = jnp.where(level < here, 1.0, 0.0)
             scale_ref[layer, at] = scale
             mix_ref[layer, at] = jnp.where(is_open, HORIZ_DIFF, 0.0)
             flow_ref[layer, at] = flow_ref[layer, at] * scale
@@ -454,11 +421,8 @@
     def _(kind):
         for layer in range(layers):
             span = slice(layer * per_layer, (layer + 1) * per_layer)
-            turn(tracers_ref[kind, span].reshape(LANES, rows), masked_ref.at[layer])
-            tiles = [
-                masked_ref[layer, row_tile(block)] * wet_ref[layer, row_tile(block)]
-                for block in range(blocks)
-            ]
+            turn(masked_in[kind, span].reshape(LANES, rows), masked_ref.at[layer])
+            tiles = [masked_ref[layer, row_tile(block)] for block in range(blocks)]
             before = None
             for block in range(blocks):
                 at = row_tile(block)
@@ -475,8 +439,7 @@
 
 
 def east_kernel(
-    tracers_ref,
-    depth_ref,
+    masked_ref,
     east_depth_ref,
     u_ref,
     inner_ref,
@@ -493,7 +456,7 @@
     from_east_ref,
     own_west_ref,
 ):
-    kinds, levels, columns, rows = tracers_ref.shape
+    kinds, levels, columns, rows = masked_ref.shape
     blocks, count = columns // SUBLANES, rows // LANES
     places = grid_tiles(columns, rows)
     for place in range(inner_ref.shape[0]):
@@ -516,10 +479,9 @@
 
     @pl.loop(0, levels)
     def _(level):
-        wet, scale, mix = {}, {}, {}
+        scale, mix = {}, {}
         for p in places:
             at = tile_index(p)
-            wet[p] = jnp.where(level < depth_ref[at], 1.0, 0.0)
             is_open = level < east_depth_ref[at]
             scale[p] = jnp.where(is_open, 1.0 / 12.0, 0.0)
             mix[p] = jnp.where(is_open, HORIZ_DIFF, 0.0)
@@ -533,7 +495,7 @@
                     for tile in range(count)
                 ]
 
-            masked = {p: tracers_ref[(kind, level) + tile_index(p)] * wet[p] for p in places}
+            masked = {p: masked_ref[(kind, level) + tile_index(p)] for p in places}
             one = shift_columns(masked, 1, halo(from_east_ref, 2 * level), blocks, count)
             two = shift_columns(one, 1, halo(from_east_ref, 2 * level + 1), blocks, count)
             west = shift_columns(masked, -1, halo(from_west_ref, 2 * level + 1), blocks, count)
@@ -633,8 +595,11 @@
         for tile in range(count)
     ]
 
-    def copy(kind):
-        return pltpu.make_async_copy(result_ref.at[kind], out_ref.at[kind], sems.at[kind])
+    def copy(kind, layer):
+        span = (kind, pl.ds(layer * per_layer, per_layer))
+        return pltpu.make_async_copy(
+            result_ref.at[span], out_ref.at[span], sems.at[kind, layer]
+        )
 
     @pl.loop(0, kinds)
     def _(kind):
@@ -666,10 +631,11 @@
                         result_ref[at] = base_ref[at] + (
                             (shifted(flux, west, -1) - flux) + along[start : start + SUBLANES]
                         )
-        copy(kind).start()
+            copy(kind, layer).start()
 
     for kind in range(kinds):
-        copy(kind).wait()
+        for layer in range(layers):
+            copy(kind, layer).wait()
 
 
 def body(
@@ -722,29 +688,23 @@
     packed = sds((3 * HALO, width), f32)
     held = pltpu.VMEM(tracers.shape, f32)
 
-    def fetched(x):
-        return pltpu.VMEM(x.shape, x.dtype)
-
+    inner, outer, own = call(
+        pack_kernel,
+        (packed, packed, sds((3 * band, width), f32)),
+        "pack_edges",
+        fields,
+        scratch=[pltpu.VMEM(x.shape, x.dtype) for x in fields] + [pltpu.SemaphoreType.DMA((4,))],
+        far=range(4),
+        cost=2000,
+    )
     edges = sds((2 * levels + levels // SUBLANES + 1, kinds, rows), f32)
-    inputs = (tracers, column_depth, east_depth, u_clinic, v_clinic)
-    (inner, outer, own, folded, *inputs, own_inner, own_outer) = call(
-        load_kernel,
-        (
-            packed,
-            packed,
-            sds((3 * band, width), f32),
-            packed,
-            *(fetched(x) for x in inputs),
-            edges,
-            edges,
-        ),
-        "load",
-        (*fields, *inputs),
-        scratch=[pltpu.VMEM(x.shape, x.dtype) for x in fields]
-        + [pltpu.SemaphoreType.DMA((8 + kinds,))],
-        far=range(9),
-    )
-    tracers, column_depth, east_depth, u_clinic, v_clinic = inputs
+    own_inner, own_outer = call(
+        edge_kernel,
+        (edges, edges),
+        "pack_tracer_edges",
+        (tracers, column_depth, east_depth, u_clinic, outer),
+    )
+    (folded,) = call(fold_kernel, (packed,), "fold", (outer, own_outer))
     came_inner = lax.ppermute(inner, "lon", pairs_inner)
     came_outer = lax.ppermute(outer, "lon", pairs_outer)
 
@@ -771,14 +731,16 @@
         slabs.append(lax.ppermute(sends[step], "lon", pairs))
     edge_inner = lax.ppermute(own_inner, "lon", pairs_inner)
     edge_outer = lax.ppermute(own_outer, "lon", ring)
-    (base,) = call(source_kernel, (held,), "sources", (tracers, column_depth, own_inner), cost=2000)
+    base, masked = call(
+        source_kernel, (held, held), "sources", (tracers, column_depth, own_inner), cost=2000
+    )
     turned = (kinds, levels * columns // LANES, rows, LANES)
     change, face_north = call(
         north_kernel,
         (pltpu.VMEM(turned, f32), pltpu.VMEM(turned, f32)),
         "north_fluxes",
-        (tracers, column_depth, v_clinic, sends[0]),
-        scratch=[pltpu.VMEM((rows, LANES), f32)] + [pltpu.VMEM(turned[1:], f32)] * 5,
+        (masked, column_depth, v_clinic, sends[0]),
+        scratch=[pltpu.VMEM((rows, LANES), f32)] + [pltpu.VMEM(turned[1:], f32)] * 4,
         cost=2000,
     )
     quarter = sds((groups, 2, SLAB_ROWS, LANES), f32)
@@ -789,8 +751,7 @@
         (held, held, pltpu.VMEM((kinds, levels, rows), f32)),
         "east_fluxes",
         (
-            tracers,
-            column_depth,
+            masked,
             east_depth,
             u_clinic,
             edge_inner,
@@ -820,7 +781,7 @@
                 pltpu.VMEM((rows, LANES), f32),
                 pltpu.VMEM((rows, LANES), f32),
                 pltpu.VMEM(tracers.shape, f32),
-                pltpu.SemaphoreType.DMA((kinds,)),
+                pltpu.SemaphoreType.DMA((kinds, levels * columns // LANES)),
             ],
             limit=RESULT_VMEM,
         )

time: 32.6 us -> 30.5 us (0.936)
  Pallas kernels: 16.3 us -> 14.8 us
  starting transfers between devices: 15.3 us -> 13.8 us
  waiting for transfers between devices: 0.11 us -> 0.79 us
    pallas_call x8 -> x10, Pallas kernels: 16.3 us -> 14.8 us  [call(): pl.pallas_call(kernel, out_shape=out_shape, in_specs=[hbm if place in far...]
    ppermute x3, starting transfers between devices: 5.75 us -> 4.98 us  [body(): slabs.append(lax.ppermute(sends[step], 'lon', pairs))]
    ppermute x1, starting transfers between devices: 2.09 us -> 1.45 us  [body(): came = lax.ppermute(send, 'lon', [(i, i ^ 2) for i in range(count)])]
    ppermute x3, waiting for transfers between devices: 0.09 us -> 0.64 us  [body(): slabs.append(lax.ppermute(sends[step], 'lon', pairs))]
  transfers between devices with their start and end apart: 9 -> 9, of which waited for: 1 -> 2; matrix products, arithmetic and copies ran while one was open for 0% -> 0% of each run, Pallas kernels for 30% -> 33%
where the time goes in v7:
time: 30.5 us; the launch traced here: 30.3 us
  Pallas kernels  14.8 us (49%)
  starting transfers between devices  13.8 us (45%)
  waiting for transfers between devices  0.79 us (3%)
  between operations  0.78 us (3%)
    pallas_call x10, Pallas kernels, call(): pl.pallas_call(kernel, out_shape=out_shape, in_specs=[hbm if place in far...  14.8 us
    ppermute x1, starting transfers between devices, body(): edge_outer = lax.ppermute(own_outer, 'lon', ring)  5.57 us
    ppermute x3, starting transfers between devices, body(): slabs.append(lax.ppermute(sends[step], 'lon', pairs))  4.98 us
    ppermute x1, starting transfers between devices, body(): came = lax.ppermute(send, 'lon', [(i, i ^ 2) for i in range(count)])  1.45 us
    ppermute x1, starting transfers between devices, body(): came_outer = lax.ppermute(outer, 'lon', pairs_outer)  0.65 us
    ppermute x3, waiting for transfers between devices, body(): slabs.append(lax.ppermute(sends[step], 'lon', pairs))  0.64 us
  transfers between devices with their start and end apart: 9, of which 2 were waited for; matrix products, arithmetic and copies ran while one was open for 0% of the time, Pallas kernels for 33%

profile of v7, /device:TPU:0, one launch (start us, length us, event | category | flops | bytes accessed | tf_op | source)
XLA Modules:
  0.0 30.3 jit_solution(5651854668239910088)
XLA Ops:
  0.6 0.0 copy-start.3
  0.6 0.0 copy-start.1
  0.7 0.0 copy-start
  0.7 0.0 copy-start.2
  0.7 1.0 %pack_edges.1 = (f32[24,256]{1,0:T(8,128)S(1)}, f32[24,256]{1,0:T(8,128)S(1)}, f32[96,256]{1,0:T(8,128)S(1)}) custom-call(f32[32,256]{1,0:T(8,128)} %old_in.1, f32[32,256]{1,0:T(8,128)} %force_in.1, f32[32,256]{1,0:T(8,128)} %coeff_in.1, s32[32,256]{1,0:T(8,128)} %mask_in.1), custom_call_target="tpu_custom_call" | custom-call | flops 2097152000 | bytes 8388608 | tf_op jit(solution)/shard_map/pack_edges/pallas_call | solution.py:667
  1.7 0.5 %collective-permute-start = (f32[24,256]{1,0:T(8,128)S(1)}, f32[24,256]{1,0:T(8,128)S(1)}, u32[]{:S(2)}, u32[]{:S(2)}) collective-permute-start(f32[24,256]{1,0:T(8,128)S(1)} %get-tuple-element.24), channel_id=1, source_target_pairs={{0,1},{1,0},{2,3},{3,2},{4,5},{5,4},{6,7},{7,6},{8,9},{9,8},{10,11... | collective-permute-start | bytes 73736 | tf_op jit(solution)/shard_map/ppermute | solution.py:708
  2.2 0.7 %collective-permute-start.1 = (f32[24,256]{1,0:T(8,128)S(1)}, f32[24,256]{1,0:T(8,128)S(1)}, u32[]{:S(2)}, u32[]{:S(2)}) collective-permute-start(f32[24,256]{1,0:T(8,128)S(1)} %get-tuple-element.25._.high_ref), channel_id=1, source_target_pairs={{1,2},{2,1},{3,4},{4,3},{5,6},{6,5},{7,8},{8,7},{9,10},{10,9},{11,... | collective-permute-start | bytes 73736 | tf_op jit(solution)/shard_map/ppermute | solution.py:709
  2.9 0.2 copy-done
  3.1 0.3 %pack_tracer_edges.1 = (f32[35,8,512]{2,1,0:T(8,128)S(1)}, f32[35,8,512]{2,1,0:T(8,128)S(1)}) custom-call(f32[8,16,16,512]{3,2,1,0:T(8,128)S(1)} %copy-done, s32[16,512]{1,0:T(8,128)S(1)} %copy-done.3, s32[16,512]{1,0:T(8,128)S(1)} %copy-done.2, f32[16,16,512]{2,1,0:T(8,128)S(1)} %copy-done.1, f32[24,256]{1,0:T(8,128)S(1)} %get-tuple-element.25._.high_ref), custom_call_target="tpu_custom_call" | custom-call | tf_op jit(solution)/shard_map/pack_tracer_edges/pallas_call | solution.py:667
  3.4 5.6 %collective-permute-start.8 = (f32[35,8,512]{2,1,0:T(8,128)S(1)}, f32[35,8,512]{2,1,0:T(8,128)S(1)}, u32[]{:S(2)}, u32[]{:S(2)}) collective-permute-start(f32[35,8,512]{2,1,0:T(8,128)S(1)} %get-tuple-element.26._.own_outer_ref), channel_id=1, source_target_pairs={{0,15},{1,2},{2,1},{3,4},{4,3},{5,6},{6,5},{7,8},{8,7},{9,10},{10,... | collective-permute-start | bytes 1720328 | tf_op jit(solution)/shard_map/ppermute | solution.py:733
  9.0 0.0 collective-permute-start.7
  9.0 0.5 %fold.1.folded_ref = f32[24,256]{1,0:T(8,128)S(1)} custom-call(f32[24,256]{1,0:T(8,128)S(1)} %get-tuple-element.25._.high_ref, f32[35,8,512]{2,1,0:T(8,128)S(1)} %get-tuple-element.26._.own_outer_ref), custom_call_target="tpu_custom_call" | custom-call | tf_op jit(solution)/shard_map/fold/pallas_call | solution.py:667
  9.5 0.0 collective-permute-done.inner_ref
  9.5 0.0 collective-permute-done.1.outer_ref
  9.5 0.5 %solver_basis.1 = (f32[128,256]{1,0:T(8,128)S(1)}, f32[8,24,128]{2,1,0:T(8,128)S(1)}, f32[8,24,128]{2,1,0:T(8,128)S(1)}) custom-call(f32[96,256]{1,0:T(8,128)S(1)} %get-tuple-element.23.own_ref, f32[24,256]{1,0:T(8,128)S(1)} %collective-permute-done.inner_ref, f32[24,256]{1,0:T(8,128)S(1)} %collective-permute-done.1.outer_ref, f32[24,256]{1,0:T(8,128)S(1)} %fold.1.folded_ref), custom_call_target="tpu_custom_call" | custom-call | flops 2097152000 | bytes 8388608 | tf_op jit(solution)/shard_map/solver_basis/pallas_call | solution.py:667
  10.0 0.0 copy-start.4
  10.0 0.6 %collective-permute-start.2 = (f32[8,24,128]{2,1,0:T(8,128)S(1)}, f32[8,24,128]{2,1,0:T(8,128)S(1)}, u32[]{:S(2)}, u32[]{:S(2)}) collective-permute-start(f32[8,24,128]{2,1,0:T(8,128)S(1)} %get-tuple-element.28), channel_id=1, source_target_pairs={{0,1},{1,0},{2,3},{3,2},{4,5},{5,4},{6,7},{7,6},{8,9},{9,8},{10,11... | collective-permute-start | bytes 294920 | tf_op jit(solution)/shard_map/ppermute | solution.py:721
  10.6 2.3 %sources.1 = (f32[8,16,16,512]{3,2,1,0:T(8,128)S(1)}, f32[8,16,16,512]{3,2,1,0:T(8,128)S(1)}) custom-call(f32[8,16,16,512]{3,2,1,0:T(8,128)S(1)} %copy-done, s32[16,512]{1,0:T(8,128)S(1)} %copy-done.3, f32[35,8,512]{2,1,0:T(8,128)S(1)} %get-tuple-element.33._.own_inner_ref), custom_call_target="tpu_custom_call" | custom-call | flops 2097152000 | bytes 8388608 | tf_op jit(solution)/shard_map/sources/pallas_call | solution.py:667
  12.9 0.0 collective-permute-done.2.came_ref
  12.9 1.0 %collective-permute-start.3 = (f32[2,2,24,128]{3,2,1,0:T(8,128)S(1)}, f32[2,2,24,128]{3,2,1,0:T(8,128)S(1)}, u32[]{:S(2)}, u32[]{:S(2)}) collective-permute-start(f32[2,2,24,128]{3,2,1,0:T(8,128)S(1)} %get-tuple-element.30), channel_id=1, source_target_pairs={{0,4},{1,5},{2,6},{3,7},{4,8},{5,9},{6,10},{7,11},{8,12},{9,13},{1... | collective-permute-start | bytes 147464 | tf_op jit(solution)/shard_map/ppermute | solution.py:731
  14.0 2.6 %collective-permute-start.4 = (f32[2,2,24,128]{3,2,1,0:T(8,128)S(1)}, f32[2,2,24,128]{3,2,1,0:T(8,128)S(1)}, u32[]{:S(2)}, u32[]{:S(2)}) collective-permute-start(f32[2,2,24,128]{3,2,1,0:T(8,128)S(1)} %get-tuple-element.31), channel_id=1, source_target_pairs={{0,8},{1,9},{2,10},{3,11},{4,12},{5,13},{6,14},{7,15},{8,0},{9,1},... | collective-permute-start | bytes 147464 | tf_op jit(solution)/shard_map/ppermute | solution.py:731
  16.6 1.3 %collective-permute-start.5 = (f32[2,2,24,128]{3,2,1,0:T(8,128)S(1)}, f32[2,2,24,128]{3,2,1,0:T(8,128)S(1)}, u32[]{:S(2)}, u32[]{:S(2)}) collective-permute-start(f32[2,2,24,128]{3,2,1,0:T(8,128)S(1)} %get-tuple-element.32), channel_id=1, source_target_pairs={{0,12},{1,13},{2,14},{3,15},{4,0},{5,1},{6,2},{7,3},{8,4},{9,5},{1... | collective-permute-start | bytes 147464 | tf_op jit(solution)/shard_map/ppermute | solution.py:731
  17.9 3.3 %north_fluxes.1 = (f32[8,2,512,128]{3,2,1,0:T(8,128)S(1)}, f32[8,2,512,128]{3,2,1,0:T(8,128)S(1)}) custom-call(f32[8,16,16,512]{3,2,1,0:T(8,128)S(1)} %get-tuple-element.34.masked_in.masked_ref, s32[16,512]{1,0:T(8,128)S(1)} %copy-done.3, f32[16,16,512]{2,1,0:T(8,128)S(1)} %copy-done.4, f32[2,2,24,128]{3,2,1,0:T(8,128)S(1)} %get-tuple-element.29._.refs_0_), custom_call_target="tpu_custom_call" | custom-call | flops 2097152000 | bytes 8388608 | tf_op jit(solution)/shard_map/north_fluxes/pallas_call | solution.py:667
  21.2 0.6 %collective-permute-done.3.refs_1_ = f32[2,2,24,128]{3,2,1,0:T(8,128)S(1)} collective-permute-done((f32[2,2,24,128]{3,2,1,0:T(8,128)S(1)}, f32[2,2,24,128]{3,2,1,0:T(8,128)S(1)}, u32[]{:S(2)}, u32[]{:S(2)}) %collective-permute-start.3) | collective-permute-done | bytes 49184 | tf_op jit(solution)/shard_map/ppermute | solution.py:731
  21.9 0.0 collective-permute-done.4.refs_2_
  21.9 0.0 collective-permute-done.5.refs_3_
  21.9 1.5 %collective-permute-start.6 = (f32[4,2,24,128]{3,2,1,0:T(8,128)S(1)}, f32[4,2,24,128]{3,2,1,0:T(8,128)S(1)}, u32[]{:S(2)}, u32[]{:S(2)}) collective-permute-start(f32[4,2,24,128]{3,2,1,0:T(8,128)S(1)} %get-tuple-element.37), channel_id=1, source_target_pairs={{0,2},{1,3},{2,0},{3,1},{4,6},{5,7},{6,4},{7,5},{8,10},{9,11},{10,... | collective-permute-start | bytes 294920 | tf_op jit(solution)/shard_map/ppermute | solution.py:748
  23.4 0.0 collective-permute-done.8.outer_ref
  23.4 0.0 collective-permute-done.7.inner_ref
  23.4 3.1 %east_fluxes.1 = (f32[8,16,16,512]{3,2,1,0:T(8,128)S(1)}, f32[8,16,16,512]{3,2,1,0:T(8,128)S(1)}, f32[8,16,512]{2,1,0:T(8,128)S(1)}) custom-call(f32[8,16,16,512]{3,2,1,0:T(8,128)S(1)} %get-tuple-element.34.masked_in.masked_ref, s32[16,512]{1,0:T(8,128)S(1)} %copy-done.2, f32[16,16,512]{2,1,0:T(8,128)S(1)} %copy-done.1, ...), custom_call_target="tpu_custom_call" | custom-call | flops 2097152000 | bytes 8388608 | tf_op jit(solution)/shard_map/east_fluxes/pallas_call | solution.py:667
  26.4 0.1 collective-permute-done.6.came_ref
  26.6 3.8 %surface_update.1 = (f32[32,256]{1,0:T(8,128)}, f32[8,16,16,512]{3,2,1,0:T(8,128)}) custom-call(f32[4,2,24,128]{3,2,1,0:T(8,128)S(1)} %get-tuple-element.36._.kept_ref, f32[4,2,24,128]{3,2,1,0:T(8,128)S(1)} %collective-permute-done.6.came_ref, f32[128,256]{1,0:T(8,128)S(1)} %get-tuple-element.38.basis_ref, ...), custom_call_target="tpu_custom_call" | custom-call | tf_op jit(solution)/shard_map/surface_update/pallas_call | solution.py:667
  (6 shorter events, 0.1 us)
Async XLA Ops:
  0.6 2.2 %copy-start.3 = (s32[16,512]{1,0:T(8,128)S(1)}, s32[16,512]{1,0:T(8,128)}, u32[]{:S(2)}) copy-start(s32[16,512]{1,0:T(8,128)} %depth_ref.5) | copy-start | bytes 98308
  0.6 2.2 %copy-start.1 = (f32[16,16,512]{2,1,0:T(8,128)S(1)}, f32[16,16,512]{2,1,0:T(8,128)}, u32[]{:S(2)}) copy-start(f32[16,16,512]{2,1,0:T(8,128)} %u_ref.3) | copy-start | bytes 1572868
  0.7 2.4 %copy-start = (f32[8,16,16,512]{3,2,1,0:T(8,128)S(1)}, f32[8,16,16,512]{3,2,1,0:T(8,128)}, u32[]{:S(2)}) copy-start(f32[8,16,16,512]{3,2,1,0:T(8,128)} %tracers_ref.3) | copy-start | bytes 12582916
  0.7 2.4 %copy-start.2 = (s32[16,512]{1,0:T(8,128)S(1)}, s32[16,512]{1,0:T(8,128)}, u32[]{:S(2)}) copy-start(s32[16,512]{1,0:T(8,128)} %east_depth_ref.3) | copy-start | bytes 98308
  1.7 7.8 %collective-permute-start = (f32[24,256]{1,0:T(8,128)S(1)}, f32[24,256]{1,0:T(8,128)S(1)}, u32[]{:S(2)}, u32[]{:S(2)}) collective-permute-start(f32[24,256]{1,0:T(8,128)S(1)} %get-tuple-element.24), channel_id=1, source_target_pairs={{0,1},{1,0},{2,3},{3,2},{4,5},{5,4},{6,7},{7,6},{8,9},{9,8},{10,11... | collective-permute-start | bytes 73736 | tf_op jit(solution)/shard_map/ppermute | solution.py:708
  2.2 7.3 %collective-permute-start.1 = (f32[24,256]{1,0:T(8,128)S(1)}, f32[24,256]{1,0:T(8,128)S(1)}, u32[]{:S(2)}, u32[]{:S(2)}) collective-permute-start(f32[24,256]{1,0:T(8,128)S(1)} %get-tuple-element.25._.high_ref), channel_id=1, source_target_pairs={{1,2},{2,1},{3,4},{4,3},{5,6},{6,5},{7,8},{8,7},{9,10},{10,9},{11,... | collective-permute-start | bytes 73736 | tf_op jit(solution)/shard_map/ppermute | solution.py:709
  3.4 20.0 %collective-permute-start.8 = (f32[35,8,512]{2,1,0:T(8,128)S(1)}, f32[35,8,512]{2,1,0:T(8,128)S(1)}, u32[]{:S(2)}, u32[]{:S(2)}) collective-permute-start(f32[35,8,512]{2,1,0:T(8,128)S(1)} %get-tuple-element.26._.own_outer_ref), channel_id=1, source_target_pairs={{0,15},{1,2},{2,1},{3,4},{4,3},{5,6},{6,5},{7,8},{8,7},{9,10},{10,... | collective-permute-start | bytes 1720328 | tf_op jit(solution)/shard_map/ppermute | solution.py:733
  9.0 14.4 %collective-permute-start.7 = (f32[35,8,512]{2,1,0:T(8,128)S(1)}, f32[35,8,512]{2,1,0:T(8,128)S(1)}, u32[]{:S(2)}, u32[]{:S(2)}) collective-permute-start(f32[35,8,512]{2,1,0:T(8,128)S(1)} %get-tuple-element.33._.own_inner_ref), channel_id=1, source_target_pairs={{0,1},{1,0},{2,3},{3,2},{4,5},{5,4},{6,7},{7,6},{8,9},{9,8},{10,11... | collective-permute-start | bytes 1720328 | tf_op jit(solution)/shard_map/ppermute | solution.py:732
  10.0 8.0 %copy-start.4 = (f32[16,16,512]{2,1,0:T(8,128)S(1)}, f32[16,16,512]{2,1,0:T(8,128)}, u32[]{:S(2)}) copy-start(f32[16,16,512]{2,1,0:T(8,128)} %v_ref.1) | copy-start | bytes 1572868
  10.0 2.9 %collective-permute-start.2 = (f32[8,24,128]{2,1,0:T(8,128)S(1)}, f32[8,24,128]{2,1,0:T(8,128)S(1)}, u32[]{:S(2)}, u32[]{:S(2)}) collective-permute-start(f32[8,24,128]{2,1,0:T(8,128)S(1)} %get-tuple-element.28), channel_id=1, source_target_pairs={{0,1},{1,0},{2,3},{3,2},{4,5},{5,4},{6,7},{7,6},{8,9},{9,8},{10,11... | collective-permute-start | bytes 294920 | tf_op jit(solution)/shard_map/ppermute | solution.py:721
  12.9 8.9 %collective-permute-start.3 = (f32[2,2,24,128]{3,2,1,0:T(8,128)S(1)}, f32[2,2,24,128]{3,2,1,0:T(8,128)S(1)}, u32[]{:S(2)}, u32[]{:S(2)}) collective-permute-start(f32[2,2,24,128]{3,2,1,0:T(8,128)S(1)} %get-tuple-element.30), channel_id=1, source_target_pairs={{0,4},{1,5},{2,6},{3,7},{4,8},{5,9},{6,10},{7,11},{8,12},{9,13},{1... | collective-permute-start | bytes 147464 | tf_op jit(solution)/shard_map/ppermute | solution.py:731
  14.0 7.9 %collective-permute-start.4 = (f32[2,2,24,128]{3,2,1,0:T(8,128)S(1)}, f32[2,2,24,128]{3,2,1,0:T(8,128)S(1)}, u32[]{:S(2)}, u32[]{:S(2)}) collective-permute-start(f32[2,2,24,128]{3,2,1,0:T(8,128)S(1)} %get-tuple-element.31), channel_id=1, source_target_pairs={{0,8},{1,9},{2,10},{3,11},{4,12},{5,13},{6,14},{7,15},{8,0},{9,1},... | collective-permute-start | bytes 147464 | tf_op jit(solution)/shard_map/ppermute | solution.py:731
  16.6 5.3 %collective-permute-start.5 = (f32[2,2,24,128]{3,2,1,0:T(8,128)S(1)}, f32[2,2,24,128]{3,2,1,0:T(8,128)S(1)}, u32[]{:S(2)}, u32[]{:S(2)}) collective-permute-start(f32[2,2,24,128]{3,2,1,0:T(8,128)S(1)} %get-tuple-element.32), channel_id=1, source_target_pairs={{0,12},{1,13},{2,14},{3,15},{4,0},{5,1},{6,2},{7,3},{8,4},{9,5},{1... | collective-permute-start | bytes 147464 | tf_op jit(solution)/shard_map/ppermute | solution.py:731
  21.9 4.7 %collective-permute-start.6 = (f32[4,2,24,128]{3,2,1,0:T(8,128)S(1)}, f32[4,2,24,128]{3,2,1,0:T(8,128)S(1)}, u32[]{:S(2)}, u32[]{:S(2)}) collective-permute-start(f32[4,2,24,128]{3,2,1,0:T(8,128)S(1)} %get-tuple-element.37), channel_id=1, source_target_pairs={{0,2},{1,3},{2,0},{3,1},{4,6},{5,7},{6,4},{7,5},{8,10},{9,11},{10,... | collective-permute-start | bytes 294920 | tf_op jit(solution)/shard_map/ppermute | solution.py:748

commit v8 on v7

--- a/solution.py
+++ b/solution.py
@@ -216,13 +216,16 @@
 
 def fold_kernel(high_ref, _, folded_ref):
     tiles = high_ref.shape[1] // LANES
-    for place in range(3):
-        part = slice(HALO * place, HALO * (place + 1))
-        for tile in range(tiles):
-            other = tiles - 1 - tile
-            folded_ref[part, tile * LANES : (tile + 1) * LANES] = reverse_tile(
-                high_ref[part, other * LANES : (other + 1) * LANES]
-            )
+
+    @pl.when(lax.axis_index("lon") == lax.axis_size("lon") - 1)
+    def _():
+        for place in range(3):
+            part = slice(HALO * place, HALO * (place + 1))
+            for tile in range(tiles):
+                other = tiles - 1 - tile
+                folded_ref[part, tile * LANES : (tile + 1) * LANES] = reverse_tile(
+                    high_ref[part, other * LANES : (other + 1) * LANES]
+                )
 
 
 def edge_kernel(tracers_ref, depth_ref, east_depth_ref, u_ref, _, inner_ref, outer_ref):
@@ -520,13 +523,15 @@
     face_west_ref,
     change_ref,
     face_north_ref,
+    surface_out,
+    out_ref,
     surface_ref,
-    out_ref,
     slabs_ref,
     height_ref,
     flow_ref,
     turned_ref,
     result_ref,
+    surface_sem,
     sems,
 ):
     half = lax.rem(lax.axis_index("lon") // 2, 2)
@@ -556,6 +561,8 @@
         for k in range(1, BASIS):
             surface = surface + weights[k] * basis_ref[k * band : (k + 1) * band, part]
         surface_ref[:, part] = surface
+    surface_copy = pltpu.make_async_copy(surface_ref, surface_out, surface_sem)
+    surface_copy.start()
 
     fill = LANES // band
     group_full = lax.broadcasted_iota(jnp.int32, (slab_rows, LANES), 1) // band
@@ -636,6 +643,7 @@
     for kind in range(kinds):
         for layer in range(layers):
             copy(kind, layer).wait()
+    surface_copy.wait()
 
 
 def body(
@@ -668,7 +676,7 @@
             kernel,
             out_shape=out_shape,
             in_specs=[hbm if place in far else vmem for place in range(len(operands))],
-            out_specs=[pl.BlockSpec(memory_space=pl.ANY) if x is result else vmem for x in out_shape],
+            out_specs=[hbm if x is result or x is solved else vmem for x in out_shape],
             scratch_shapes=list(scratch),
             compiler_params=pltpu.CompilerParams(vmem_limit_bytes=limit),
             cost_estimate=pl.CostEstimate(
@@ -684,7 +692,7 @@
             )
         )
 
-    result = sds(tracers.shape, f32)
+    solved, result = sds((band, width), f32), sds(tracers.shape, f32)
     packed = sds((3 * HALO, width), f32)
     held = pltpu.VMEM(tracers.shape, f32)
 
@@ -772,15 +780,17 @@
     return tuple(
         call(
             update_kernel,
-            (sds((band, width), f32), result),
+            (solved, result),
             "surface_update",
             (keep, came, basis, base, face_east, face_west, change, face_north),
             scratch=[
+                pltpu.VMEM((band, width), f32),
                 pltpu.VMEM((count, SLAB_ROWS, LANES), f32),
                 pltpu.VMEM((LANES, rows), f32),
                 pltpu.VMEM((rows, LANES), f32),
                 pltpu.VMEM((rows, LANES), f32),
                 pltpu.VMEM(tracers.shape, f32),
+                pltpu.SemaphoreType.DMA,
                 pltpu.SemaphoreType.DMA((kinds, levels * columns // LANES)),
             ],
             limit=RESULT_VMEM,

time: 30.5 us -> 29.9 us (0.980)
  Pallas kernels: 14.8 us -> 13.7 us
  starting transfers between devices: 13.8 us -> 14.3 us
    pallas_call x10, Pallas kernels: 14.8 us -> 13.7 us  [call(): pl.pallas_call(kernel, out_shape=out_shape, in_specs=[hbm if place in far...]
    ppermute x3, starting transfers between devices: 4.98 us -> 5.48 us  [body(): slabs.append(lax.ppermute(sends[step], 'lon', pairs))]
  transfers between devices with their start and end apart: 9 -> 9, of which waited for: 2 -> 2; matrix products, arithmetic and copies ran while one was open for 0% -> 0% of each run, Pallas kernels for 33% -> 32%
where the time goes in v8:
time: 29.9 us; the launch traced here: 29.7 us
  starting transfers between devices  14.3 us (48%)
  Pallas kernels  13.7 us (46%)
  waiting for transfers between devices  0.79 us (3%)
  between operations  0.77 us (3%)
    pallas_call x10, Pallas kernels, call(): pl.pallas_call(kernel, out_shape=out_shape, in_specs=[hbm if place in far...  13.7 us
    ppermute x1, starting transfers between devices, body(): edge_outer = lax.ppermute(own_outer, 'lon', ring)  5.57 us
    ppermute x3, starting transfers between devices, body(): slabs.append(lax.ppermute(sends[step], 'lon', pairs))  5.48 us
    ppermute x1, starting transfers between devices, body(): came = lax.ppermute(send, 'lon', [(i, i ^ 2) for i in range(count)])  1.45 us
    ppermute x1, starting transfers between devices, body(): came_outer = lax.ppermute(outer, 'lon', pairs_outer)  0.65 us
    ppermute x3, waiting for transfers between devices, body(): slabs.append(lax.ppermute(sends[step], 'lon', pairs))  0.64 us
  transfers between devices with their start and end apart: 9, of which 2 were waited for; matrix products, arithmetic and copies ran while one was open for 0% of the time, Pallas kernels for 32%

profile of v8, /device:TPU:0, one launch (start us, length us, event | category | flops | bytes accessed | tf_op | source)
XLA Modules:
  0.0 29.7 jit_solution(6117703013860249241)
XLA Ops:
  0.6 0.0 copy-start.3
  0.6 0.0 copy-start.1
  0.7 0.0 copy-start
  0.7 0.0 copy-start.2
  0.7 1.0 %pack_edges.1 = (f32[24,256]{1,0:T(8,128)S(1)}, f32[24,256]{1,0:T(8,128)S(1)}, f32[96,256]{1,0:T(8,128)S(1)}) custom-call(f32[32,256]{1,0:T(8,128)} %old_in.1, f32[32,256]{1,0:T(8,128)} %force_in.1, f32[32,256]{1,0:T(8,128)} %coeff_in.1, s32[32,256]{1,0:T(8,128)} %mask_in.1), custom_call_target="tpu_custom_call" | custom-call | flops 2097152000 | bytes 8388608 | tf_op jit(solution)/shard_map/pack_edges/pallas_call | solution.py:675
  1.7 0.5 %collective-permute-start = (f32[24,256]{1,0:T(8,128)S(1)}, f32[24,256]{1,0:T(8,128)S(1)}, u32[]{:S(2)}, u32[]{:S(2)}) collective-permute-start(f32[24,256]{1,0:T(8,128)S(1)} %get-tuple-element.24), channel_id=1, source_target_pairs={{0,1},{1,0},{2,3},{3,2},{4,5},{5,4},{6,7},{7,6},{8,9},{9,8},{10,11... | collective-permute-start | bytes 73736 | tf_op jit(solution)/shard_map/ppermute | solution.py:716
  2.2 0.7 %collective-permute-start.1 = (f32[24,256]{1,0:T(8,128)S(1)}, f32[24,256]{1,0:T(8,128)S(1)}, u32[]{:S(2)}, u32[]{:S(2)}) collective-permute-start(f32[24,256]{1,0:T(8,128)S(1)} %get-tuple-element.25._.high_ref), channel_id=1, source_target_pairs={{1,2},{2,1},{3,4},{4,3},{5,6},{6,5},{7,8},{8,7},{9,10},{10,9},{11,... | collective-permute-start | bytes 73736 | tf_op jit(solution)/shard_map/ppermute | solution.py:717
  2.9 0.0 copy-done.3
  2.9 0.2 copy-done
  3.1 0.3 %pack_tracer_edges.1 = (f32[35,8,512]{2,1,0:T(8,128)S(1)}, f32[35,8,512]{2,1,0:T(8,128)S(1)}) custom-call(f32[8,16,16,512]{3,2,1,0:T(8,128)S(1)} %copy-done, s32[16,512]{1,0:T(8,128)S(1)} %copy-done.3, s32[16,512]{1,0:T(8,128)S(1)} %copy-done.2, f32[16,16,512]{2,1,0:T(8,128)S(1)} %copy-done.1, f32[24,256]{1,0:T(8,128)S(1)} %get-tuple-element.25._.high_ref), custom_call_target="tpu_custom_call" | custom-call | tf_op jit(solution)/shard_map/pack_tracer_edges/pallas_call | solution.py:675
  3.4 5.6 %collective-permute-start.8 = (f32[35,8,512]{2,1,0:T(8,128)S(1)}, f32[35,8,512]{2,1,0:T(8,128)S(1)}, u32[]{:S(2)}, u32[]{:S(2)}) collective-permute-start(f32[35,8,512]{2,1,0:T(8,128)S(1)} %get-tuple-element.26._.own_outer_ref), channel_id=1, source_target_pairs={{0,15},{1,2},{2,1},{3,4},{4,3},{5,6},{6,5},{7,8},{8,7},{9,10},{10,... | collective-permute-start | bytes 1720328 | tf_op jit(solution)/shard_map/ppermute | solution.py:741
  9.0 0.0 collective-permute-start.7
  9.0 0.0 collective-permute-done.inner_ref
  9.0 0.0 collective-permute-done.1.outer_ref
  9.0 0.5 %solver_basis.1 = (f32[128,256]{1,0:T(8,128)S(1)}, f32[8,24,128]{2,1,0:T(8,128)S(1)}, f32[8,24,128]{2,1,0:T(8,128)S(1)}) custom-call(f32[96,256]{1,0:T(8,128)S(1)} %get-tuple-element.23.own_ref, f32[24,256]{1,0:T(8,128)S(1)} %collective-permute-done.inner_ref, f32[24,256]{1,0:T(8,128)S(1)} %collective-permute-done.1.outer_ref, f32[24,256]{1,0:T(8,128)S(1)} %fold.1.folded_ref), custom_call_target="tpu_custom_call" | custom-call | flops 2097152000 | bytes 8388608 | tf_op jit(solution)/shard_map/solver_basis/pallas_call | solution.py:675
  9.5 0.0 copy-start.4
  9.5 0.6 %collective-permute-start.2 = (f32[8,24,128]{2,1,0:T(8,128)S(1)}, f32[8,24,128]{2,1,0:T(8,128)S(1)}, u32[]{:S(2)}, u32[]{:S(2)}) collective-permute-start(f32[8,24,128]{2,1,0:T(8,128)S(1)} %get-tuple-element.28), channel_id=1, source_target_pairs={{0,1},{1,0},{2,3},{3,2},{4,5},{5,4},{6,7},{7,6},{8,9},{9,8},{10,11... | collective-permute-start | bytes 294920 | tf_op jit(solution)/shard_map/ppermute | solution.py:729
  10.1 2.3 %sources.1 = (f32[8,16,16,512]{3,2,1,0:T(8,128)S(1)}, f32[8,16,16,512]{3,2,1,0:T(8,128)S(1)}) custom-call(f32[8,16,16,512]{3,2,1,0:T(8,128)S(1)} %copy-done, s32[16,512]{1,0:T(8,128)S(1)} %copy-done.3, f32[35,8,512]{2,1,0:T(8,128)S(1)} %get-tuple-element.33._.own_inner_ref), custom_call_target="tpu_custom_call" | custom-call | flops 2097152000 | bytes 8388608 | tf_op jit(solution)/shard_map/sources/pallas_call | solution.py:675
  12.4 0.0 collective-permute-done.2.came_ref
  12.4 1.5 %collective-permute-start.3 = (f32[2,2,24,128]{3,2,1,0:T(8,128)S(1)}, f32[2,2,24,128]{3,2,1,0:T(8,128)S(1)}, u32[]{:S(2)}, u32[]{:S(2)}) collective-permute-start(f32[2,2,24,128]{3,2,1,0:T(8,128)S(1)} %get-tuple-element.30), channel_id=1, source_target_pairs={{0,4},{1,5},{2,6},{3,7},{4,8},{5,9},{6,10},{7,11},{8,12},{9,13},{1... | collective-permute-start | bytes 147464 | tf_op jit(solution)/shard_map/ppermute | solution.py:739
  14.0 2.6 %collective-permute-start.4 = (f32[2,2,24,128]{3,2,1,0:T(8,128)S(1)}, f32[2,2,24,128]{3,2,1,0:T(8,128)S(1)}, u32[]{:S(2)}, u32[]{:S(2)}) collective-permute-start(f32[2,2,24,128]{3,2,1,0:T(8,128)S(1)} %get-tuple-element.31), channel_id=1, source_target_pairs={{0,8},{1,9},{2,10},{3,11},{4,12},{5,13},{6,14},{7,15},{8,0},{9,1},... | collective-permute-start | bytes 147464 | tf_op jit(solution)/shard_map/ppermute | solution.py:739
  16.6 1.3 %collective-permute-start.5 = (f32[2,2,24,128]{3,2,1,0:T(8,128)S(1)}, f32[2,2,24,128]{3,2,1,0:T(8,128)S(1)}, u32[]{:S(2)}, u32[]{:S(2)}) collective-permute-start(f32[2,2,24,128]{3,2,1,0:T(8,128)S(1)} %get-tuple-element.32), channel_id=1, source_target_pairs={{0,12},{1,13},{2,14},{3,15},{4,0},{5,1},{6,2},{7,3},{8,4},{9,5},{1... | collective-permute-start | bytes 147464 | tf_op jit(solution)/shard_map/ppermute | solution.py:739
  17.9 3.3 %north_fluxes.1 = (f32[8,2,512,128]{3,2,1,0:T(8,128)S(1)}, f32[8,2,512,128]{3,2,1,0:T(8,128)S(1)}) custom-call(f32[8,16,16,512]{3,2,1,0:T(8,128)S(1)} %get-tuple-element.34.masked_in.masked_ref, s32[16,512]{1,0:T(8,128)S(1)} %copy-done.3, f32[16,16,512]{2,1,0:T(8,128)S(1)} %copy-done.4, f32[2,2,24,128]{3,2,1,0:T(8,128)S(1)} %get-tuple-element.29._.refs_0_), custom_call_target="tpu_custom_call" | custom-call | flops 2097152000 | bytes 8388608 | tf_op jit(solution)/shard_map/north_fluxes/pallas_call | solution.py:675
  21.2 0.6 %collective-permute-done.3.refs_1_ = f32[2,2,24,128]{3,2,1,0:T(8,128)S(1)} collective-permute-done((f32[2,2,24,128]{3,2,1,0:T(8,128)S(1)}, f32[2,2,24,128]{3,2,1,0:T(8,128)S(1)}, u32[]{:S(2)}, u32[]{:S(2)}) %collective-permute-start.3) | collective-permute-done | bytes 49184 | tf_op jit(solution)/shard_map/ppermute | solution.py:739
  21.9 0.0 collective-permute-done.4.refs_2_
  21.9 0.0 collective-permute-done.5.refs_3_
  21.9 1.5 %collective-permute-start.6 = (f32[4,2,24,128]{3,2,1,0:T(8,128)S(1)}, f32[4,2,24,128]{3,2,1,0:T(8,128)S(1)}, u32[]{:S(2)}, u32[]{:S(2)}) collective-permute-start(f32[4,2,24,128]{3,2,1,0:T(8,128)S(1)} %get-tuple-element.37), channel_id=1, source_target_pairs={{0,2},{1,3},{2,0},{3,1},{4,6},{5,7},{6,4},{7,5},{8,10},{9,11},{10,... | collective-permute-start | bytes 294920 | tf_op jit(solution)/shard_map/ppermute | solution.py:756
  23.4 0.0 collective-permute-done.8.outer_ref
  23.4 0.0 collective-permute-done.7.inner_ref
  23.4 3.1 %east_fluxes.1 = (f32[8,16,16,512]{3,2,1,0:T(8,128)S(1)}, f32[8,16,16,512]{3,2,1,0:T(8,128)S(1)}, f32[8,16,512]{2,1,0:T(8,128)S(1)}) custom-call(f32[8,16,16,512]{3,2,1,0:T(8,128)S(1)} %get-tuple-element.34.masked_in.masked_ref, s32[16,512]{1,0:T(8,128)S(1)} %copy-done.2, f32[16,16,512]{2,1,0:T(8,128)S(1)} %copy-done.1, ...), custom_call_target="tpu_custom_call" | custom-call | flops 2097152000 | bytes 8388608 | tf_op jit(solution)/shard_map/east_fluxes/pallas_call | solution.py:675
  26.4 0.1 collective-permute-done.6.came_ref
  26.6 3.2 %surface_update.1 = (f32[32,256]{1,0:T(8,128)}, f32[8,16,16,512]{3,2,1,0:T(8,128)}) custom-call(f32[4,2,24,128]{3,2,1,0:T(8,128)S(1)} %get-tuple-element.36._.kept_ref, f32[4,2,24,128]{3,2,1,0:T(8,128)S(1)} %collective-permute-done.6.came_ref, f32[128,256]{1,0:T(8,128)S(1)} %get-tuple-element.38.basis_ref, ...), custom_call_target="tpu_custom_call" | custom-call | tf_op jit(solution)/shard_map/surface_update/pallas_call | solution.py:675
  (6 shorter events, 0.1 us)
Async XLA Ops:
  0.6 2.2 %copy-start.3 = (s32[16,512]{1,0:T(8,128)S(1)}, s32[16,512]{1,0:T(8,128)}, u32[]{:S(2)}) copy-start(s32[16,512]{1,0:T(8,128)} %depth_ref.5) | copy-start | bytes 98308
  0.6 2.2 %copy-start.1 = (f32[16,16,512]{2,1,0:T(8,128)S(1)}, f32[16,16,512]{2,1,0:T(8,128)}, u32[]{:S(2)}) copy-start(f32[16,16,512]{2,1,0:T(8,128)} %u_ref.3) | copy-start | bytes 1572868
  0.7 2.4 %copy-start = (f32[8,16,16,512]{3,2,1,0:T(8,128)S(1)}, f32[8,16,16,512]{3,2,1,0:T(8,128)}, u32[]{:S(2)}) copy-start(f32[8,16,16,512]{3,2,1,0:T(8,128)} %tracers_ref.3) | copy-start | bytes 12582916
  0.7 2.4 %copy-start.2 = (s32[16,512]{1,0:T(8,128)S(1)}, s32[16,512]{1,0:T(8,128)}, u32[]{:S(2)}) copy-start(s32[16,512]{1,0:T(8,128)} %east_depth_ref.3) | copy-start | bytes 98308
  1.7 7.3 %collective-permute-start = (f32[24,256]{1,0:T(8,128)S(1)}, f32[24,256]{1,0:T(8,128)S(1)}, u32[]{:S(2)}, u32[]{:S(2)}) collective-permute-start(f32[24,256]{1,0:T(8,128)S(1)} %get-tuple-element.24), channel_id=1, source_target_pairs={{0,1},{1,0},{2,3},{3,2},{4,5},{5,4},{6,7},{7,6},{8,9},{9,8},{10,11... | collective-permute-start | bytes 73736 | tf_op jit(solution)/shard_map/ppermute | solution.py:716
  2.2 6.8 %collective-permute-start.1 = (f32[24,256]{1,0:T(8,128)S(1)}, f32[24,256]{1,0:T(8,128)S(1)}, u32[]{:S(2)}, u32[]{:S(2)}) collective-permute-start(f32[24,256]{1,0:T(8,128)S(1)} %get-tuple-element.25._.high_ref), channel_id=1, source_target_pairs={{1,2},{2,1},{3,4},{4,3},{5,6},{6,5},{7,8},{8,7},{9,10},{10,9},{11,... | collective-permute-start | bytes 73736 | tf_op jit(solution)/shard_map/ppermute | solution.py:717
  3.4 20.0 %collective-permute-start.8 = (f32[35,8,512]{2,1,0:T(8,128)S(1)}, f32[35,8,512]{2,1,0:T(8,128)S(1)}, u32[]{:S(2)}, u32[]{:S(2)}) collective-permute-start(f32[35,8,512]{2,1,0:T(8,128)S(1)} %get-tuple-element.26._.own_outer_ref), channel_id=1, source_target_pairs={{0,15},{1,2},{2,1},{3,4},{4,3},{5,6},{6,5},{7,8},{8,7},{9,10},{10,... | collective-permute-start | bytes 1720328 | tf_op jit(solution)/shard_map/ppermute | solution.py:741
  9.0 14.4 %collective-permute-start.7 = (f32[35,8,512]{2,1,0:T(8,128)S(1)}, f32[35,8,512]{2,1,0:T(8,128)S(1)}, u32[]{:S(2)}, u32[]{:S(2)}) collective-permute-start(f32[35,8,512]{2,1,0:T(8,128)S(1)} %get-tuple-element.33._.own_inner_ref), channel_id=1, source_target_pairs={{0,1},{1,0},{2,3},{3,2},{4,5},{5,4},{6,7},{7,6},{8,9},{9,8},{10,11... | collective-permute-start | bytes 1720328 | tf_op jit(solution)/shard_map/ppermute | solution.py:740
  9.5 8.5 %copy-start.4 = (f32[16,16,512]{2,1,0:T(8,128)S(1)}, f32[16,16,512]{2,1,0:T(8,128)}, u32[]{:S(2)}) copy-start(f32[16,16,512]{2,1,0:T(8,128)} %v_ref.1) | copy-start | bytes 1572868
  9.5 2.9 %collective-permute-start.2 = (f32[8,24,128]{2,1,0:T(8,128)S(1)}, f32[8,24,128]{2,1,0:T(8,128)S(1)}, u32[]{:S(2)}, u32[]{:S(2)}) collective-permute-start(f32[8,24,128]{2,1,0:T(8,128)S(1)} %get-tuple-element.28), channel_id=1, source_target_pairs={{0,1},{1,0},{2,3},{3,2},{4,5},{5,4},{6,7},{7,6},{8,9},{9,8},{10,11... | collective-permute-start | bytes 294920 | tf_op jit(solution)/shard_map/ppermute | solution.py:729
  12.4 9.4 %collective-permute-start.3 = (f32[2,2,24,128]{3,2,1,0:T(8,128)S(1)}, f32[2,2,24,128]{3,2,1,0:T(8,128)S(1)}, u32[]{:S(2)}, u32[]{:S(2)}) collective-permute-start(f32[2,2,24,128]{3,2,1,0:T(8,128)S(1)} %get-tuple-element.30), channel_id=1, source_target_pairs={{0,4},{1,5},{2,6},{3,7},{4,8},{5,9},{6,10},{7,11},{8,12},{9,13},{1... | collective-permute-start | bytes 147464 | tf_op jit(solution)/shard_map/ppermute | solution.py:739
  14.0 7.9 %collective-permute-start.4 = (f32[2,2,24,128]{3,2,1,0:T(8,128)S(1)}, f32[2,2,24,128]{3,2,1,0:T(8,128)S(1)}, u32[]{:S(2)}, u32[]{:S(2)}) collective-permute-start(f32[2,2,24,128]{3,2,1,0:T(8,128)S(1)} %get-tuple-element.31), channel_id=1, source_target_pairs={{0,8},{1,9},{2,10},{3,11},{4,12},{5,13},{6,14},{7,15},{8,0},{9,1},... | collective-permute-start | bytes 147464 | tf_op jit(solution)/shard_map/ppermute | solution.py:739
  16.6 5.3 %collective-permute-start.5 = (f32[2,2,24,128]{3,2,1,0:T(8,128)S(1)}, f32[2,2,24,128]{3,2,1,0:T(8,128)S(1)}, u32[]{:S(2)}, u32[]{:S(2)}) collective-permute-start(f32[2,2,24,128]{3,2,1,0:T(8,128)S(1)} %get-tuple-element.32), channel_id=1, source_target_pairs={{0,12},{1,13},{2,14},{3,15},{4,0},{5,1},{6,2},{7,3},{8,4},{9,5},{1... | collective-permute-start | bytes 147464 | tf_op jit(solution)/shard_map/ppermute | solution.py:739
  21.9 4.7 %collective-permute-start.6 = (f32[4,2,24,128]{3,2,1,0:T(8,128)S(1)}, f32[4,2,24,128]{3,2,1,0:T(8,128)S(1)}, u32[]{:S(2)}, u32[]{:S(2)}) collective-permute-start(f32[4,2,24,128]{3,2,1,0:T(8,128)S(1)} %get-tuple-element.37), channel_id=1, source_target_pairs={{0,2},{1,3},{2,0},{3,1},{4,6},{5,7},{6,4},{7,5},{8,10},{9,11},{10,... | collective-permute-start | bytes 294920 | tf_op jit(solution)/shard_map/ppermute | solution.py:756

commit v9 on v8

--- a/solution.py
+++ b/solution.py
@@ -1,3 +1,5 @@
+import functools
+
 import jax
 import jax.numpy as jnp
 from jax import lax
@@ -19,6 +21,7 @@
 YIELD_NITROUS = 0.3
 
 
+SOLVER_ITERS = 4
 SUBLANES = 8
 LANES = 128
 SMALL_VMEM = 4 * 2**20
@@ -29,6 +32,7 @@
 CENTRE = 4.55
 SPREAD = 4.45
 PIVOT_FLOOR = 3e-7
+PIVOT_LEAST = 0.03
 
 
 def is_even():
@@ -197,7 +201,10 @@
         for i in range(n + 1, BASIS):
             value = value - factors[i][n] * weights[i]
         weights[n] = value
-    return weights
+    kept = matrix[0][0] > 0.0
+    for n in range(BASIS):
+        kept = kept & (matrix[n][n] > PIVOT_LEAST * start[n])
+    return weights, jnp.where(kept, 0.0, 1.0)
 
 
 def reverse_tile(tile):
@@ -341,12 +348,13 @@
     )
 
 
-def source_kernel(tracers_ref, depth_ref, _, base_ref, masked_ref):
+def source_kernel(first, tracers_ref, depth_ref, _, base_ref, masked_ref):
     kinds, levels, columns, rows = tracers_ref.shape
     places = grid_tiles(columns, rows)
 
-    @pl.loop(0, levels)
-    def _(level):
+    @pl.loop(0, base_ref.shape[1])
+    def _(place):
+        level = first + place
         above = jnp.maximum(level - 1, 0)
         below = jnp.minimum(level + 1, levels - 1)
         mix_up_level = jnp.where(level > 0, VERT_DIFF, 0.0)
@@ -360,11 +368,11 @@
             masked = [value * wet for value in values]
             sources = redox_sources(masked)
             for kind in range(kinds):
-                masked_ref[(kind, level) + at] = masked[kind]
+                masked_ref[(kind, place) + at] = masked[kind]
                 value = values[kind]
                 down = (tracers_ref[(kind, below) + at] - value) * mix_down
                 up = (value - tracers_ref[(kind, above) + at]) * mix_up
-                base_ref[(kind, level) + at] = value + (sources[kind] + (down - up))
+                base_ref[(kind, place) + at] = value + (sources[kind] + (down - up))
 
 
 def turn(ref_block, target_ref, start=0):
@@ -386,22 +394,11 @@
     return slice(block * SUBLANES, (block + 1) * SUBLANES)
 
 
-def north_kernel(
-    masked_in,
-    depth_ref,
-    v_ref,
-    _,
-    change_ref,
-    face_ref,
-    depth_turned_ref,
-    scale_ref,
-    flow_ref,
-    mix_ref,
-    masked_ref,
-):
-    kinds, levels, columns, rows = masked_in.shape
-    per_layer = LANES // columns
-    layers = levels // per_layer
+def north_kernel(depth_ref, v_ref, _, *refs):
+    masked_ins, refs = refs[:-7], refs[-7:]
+    change_ref, face_ref, depth_turned_ref, scale_ref, flow_ref, mix_ref, masked_ref = refs
+    kinds, per_layer, columns, rows = masked_ins[0].shape
+    layers = len(masked_ins)
     blocks = rows // SUBLANES
     depth = depth_ref[...].astype(jnp.float32)
     turn(jnp.concatenate([depth] * per_layer, axis=0), depth_turned_ref)
@@ -423,8 +420,7 @@
     @pl.loop(0, kinds)
     def _(kind):
         for layer in range(layers):
-            span = slice(layer * per_layer, (layer + 1) * per_layer)
-            turn(masked_in[kind, span].reshape(LANES, rows), masked_ref.at[layer])
+            turn(masked_ins[layer][kind].reshape(LANES, rows), masked_ref.at[layer])
             tiles = [masked_ref[layer, row_tile(block)] for block in range(blocks)]
             before = None
             for block in range(blocks):
@@ -442,24 +438,28 @@
 
 
 def east_kernel(
-    masked_ref,
+    layers,
     east_depth_ref,
     u_ref,
     inner_ref,
     outer_ref,
     own_inner_ref,
     own_outer_ref,
-    before_ref,
     _,
-    base_ref,
-    face_east_ref,
-    face_west_ref,
-    flux_west_ref,
-    from_west_ref,
-    from_east_ref,
-    own_west_ref,
+    *refs,
 ):
-    kinds, levels, columns, rows = masked_ref.shape
+    masked_refs, before_refs, refs = refs[:layers], refs[layers : 2 * layers], refs[2 * layers :]
+    (
+        base_ref,
+        face_east_ref,
+        face_west_ref,
+        flux_west_ref,
+        from_west_ref,
+        from_east_ref,
+        own_west_ref,
+    ) = refs
+    kinds, levels, columns, rows = base_ref.shape
+    per_layer = levels // layers
     blocks, count = columns // SUBLANES, rows // LANES
     places = grid_tiles(columns, rows)
     for place in range(inner_ref.shape[0]):
@@ -480,8 +480,9 @@
             face_west_ref[kind, z : z + 1] = face[kind : kind + 1]
         flux_west_ref[z] = u_west * face - mix_west * (east_one - center)
 
-    @pl.loop(0, levels)
-    def _(level):
+    def one_level(place, layer):
+        level = layer * per_layer + place
+        masked_ref, before_ref = masked_refs[layer], before_refs[layer]
         scale, mix = {}, {}
         for p in places:
             at = tile_index(p)
@@ -498,7 +499,7 @@
                     for tile in range(count)
                 ]
 
-            masked = {p: masked_ref[(kind, level) + tile_index(p)] for p in places}
+            masked = {p: masked_ref[(kind, place) + tile_index(p)] for p in places}
             one = shift_columns(masked, 1, halo(from_east_ref, 2 * level), blocks, count)
             two = shift_columns(one, 1, halo(from_east_ref, 2 * level + 1), blocks, count)
             west = shift_columns(masked, -1, halo(from_west_ref, 2 * level + 1), blocks, count)
@@ -511,7 +512,12 @@
             incoming = shift_columns(flux, -1, halo(flux_west_ref, level), blocks, count)
             for p in places:
                 at = (kind, level) + tile_index(p)
-                base_ref[at] = before_ref[at] + (incoming[p] - flux[p])
+                base_ref[at] = before_ref[(kind, place) + tile_index(p)] + (
+                    incoming[p] - flux[p]
+                )
+
+    for layer in range(layers):
+        pl.loop(0, per_layer)(functools.partial(one_level, layer=layer))
 
 
 def update_kernel(
@@ -525,6 +531,7 @@
     face_north_ref,
     surface_out,
     out_ref,
+    weak_ref,
     surface_ref,
     slabs_ref,
     height_ref,
@@ -548,9 +555,10 @@
     while len(parts) > 1:
         parts = [a + b for a, b in zip(parts[::2], parts[1::2])]
     dots = [jnp.broadcast_to(parts[0][:, m : m + 1], (1, LANES)) for m in range(2 * BASIS)]
-    weights = basis_weights(
+    weights, weak = basis_weights(
         dots[:2] + [2.0 * dots[m] - dots[m % 2] for m in range(2, 2 * BASIS)]
     )
+    weak_ref[...] = jnp.broadcast_to(weak, (SUBLANES, LANES))
     lane_group = lax.broadcasted_iota(jnp.int32, (1, LANES), 1) // band
     lane_weight = jnp.zeros((1, LANES), jnp.float32)
     for k in range(BASIS):
@@ -657,6 +665,17 @@
     u_clinic,
     v_clinic,
 ):
+    given = (
+        surface_old,
+        surface_forcing,
+        surface_coeff,
+        ocean_mask,
+        column_depth,
+        east_depth,
+        tracers,
+        u_clinic,
+        v_clinic,
+    )
     band, width = surface_old.shape
     kinds, levels, columns, rows = tracers.shape
     count = lax.axis_size("lon")
@@ -739,15 +758,25 @@
         slabs.append(lax.ppermute(sends[step], "lon", pairs))
     edge_inner = lax.ppermute(own_inner, "lon", pairs_inner)
     edge_outer = lax.ppermute(own_outer, "lon", ring)
-    base, masked = call(
-        source_kernel, (held, held), "sources", (tracers, column_depth, own_inner), cost=2000
-    )
+    layers = levels * columns // LANES
+    part = pltpu.VMEM((kinds, levels // layers, columns, rows), f32)
+    bases, masked = [], []
+    for layer in range(layers):
+        found = call(
+            functools.partial(source_kernel, layer * (levels // layers)),
+            (part, part),
+            f"sources_{layer}",
+            (tracers, column_depth, sends[0] if layer else own_inner),
+            cost=2000,
+        )
+        bases.append(found[0])
+        masked.append(found[1])
     turned = (kinds, levels * columns // LANES, rows, LANES)
     change, face_north = call(
         north_kernel,
         (pltpu.VMEM(turned, f32), pltpu.VMEM(turned, f32)),
         "north_fluxes",
-        (masked, column_depth, v_clinic, sends[0]),
+        (column_depth, v_clinic, sends[0], *masked),
         scratch=[pltpu.VMEM((rows, LANES), f32)] + [pltpu.VMEM(turned[1:], f32)] * 4,
         cost=2000,
     )
@@ -755,19 +784,19 @@
     keep, send = call(half_kernel, (quarter, quarter), "split_halves", (*slabs, change))
     came = lax.ppermute(send, "lon", [(i, i ^ 2) for i in range(count)])
     base, face_east, face_west = call(
-        east_kernel,
+        functools.partial(east_kernel, layers),
         (held, held, pltpu.VMEM((kinds, levels, rows), f32)),
         "east_fluxes",
         (
-            masked,
             east_depth,
             u_clinic,
             edge_inner,
             edge_outer,
             own_inner,
             own_outer,
-            base,
             keep,
+            *masked,
+            *bases,
         ),
         scratch=[
             pltpu.VMEM((levels, kinds, rows), f32),
@@ -777,10 +806,10 @@
         ],
         cost=2000,
     )
-    return tuple(
+    surface, tracers_new, weak = (
         call(
             update_kernel,
-            (solved, result),
+            (solved, result, sds((SUBLANES, LANES), f32)),
             "surface_update",
             (keep, came, basis, base, face_east, face_west, change, face_north),
             scratch=[
@@ -796,6 +825,176 @@
             limit=RESULT_VMEM,
         )
     )
+    return lax.cond(
+        weak[0, 0] > 0.0, lambda: plain_body(*given), lambda: (surface, tracers_new)
+    )
+
+
+def padded_2(block, sides, width, periodic):
+    for axis, dim in sides:
+        count = lax.axis_size(axis)
+        forward = [(i, i + 1) for i in range(count - 1)]
+        if periodic:
+            forward.append((count - 1, 0))
+        backward = [(target, source) for source, target in forward]
+        low = lax.ppermute(
+            lax.slice_in_dim(block, block.shape[dim] - width, None, axis=dim), axis, forward
+        )
+        high = lax.ppermute(lax.slice_in_dim(block, 0, width, axis=dim), axis, backward)
+        block = jnp.concatenate([low, block, high], axis=dim)
+    return block
+
+
+def apply_operator(values_in, mask_float, coeff):
+    masked = mask_float * values_in
+    padded = padded_2(masked, (("lon", 0),), 1, False)
+    top_device = lax.axis_index("lon") == lax.axis_size("lon") - 1
+    folded = jnp.where(top_device, masked[-1:, ::-1], padded[-1:])
+    northern = jnp.concatenate([padded[2:-1], folded], axis=0)
+    southern = padded[:-2]
+    eastern = jnp.roll(masked, -1, axis=1)
+    western = jnp.roll(masked, 1, axis=1)
+    return (coeff + 4.0 * mask_float) * values_in - mask_float * (
+        northern + southern + eastern + western
+    )
+
+
+def squared_total(residual):
+    return lax.psum(jnp.sum(residual * residual), "lon")
+
+
+def plain_solve(right_side, mask_float, coeff):
+    solution = jnp.zeros_like(right_side)
+    residual = right_side
+    direction = right_side
+    norm_now = squared_total(residual)
+    for sweep in range(SOLVER_ITERS):
+        applied = apply_operator(direction, mask_float, coeff)
+        curvature = lax.psum(jnp.sum(direction * applied), "lon")
+        step_size = norm_now / curvature
+        solution = solution + step_size * direction
+        residual = residual - step_size * applied
+        norm_next = squared_total(residual)
+        direction = residual + norm_next / norm_now * direction
+        norm_now = norm_next
+    return solution
+
+
+def open_faces(column_depth, east_depth, east_baro, north_baro, u_clinic, v_clinic):
+    level_index = lax.broadcasted_iota(jnp.int32, u_clinic.shape, 0)
+    wet = (level_index < column_depth[None]).astype(jnp.float32)
+    east_open = (level_index < east_depth[None]).astype(jnp.float32)
+    north_open = wet * jnp.concatenate([wet[:, :, 1:], jnp.zeros_like(wet[:, :, :1])], axis=2)
+    below_open = wet * jnp.concatenate([wet[1:], jnp.zeros_like(wet[:1])], axis=0)
+    east_flow = (u_clinic + east_baro[None]) * east_open
+    north_flow = (v_clinic + north_baro[None]) * north_open
+    return (wet, east_open, north_open, below_open, east_flow, north_flow)
+
+
+def meridional_vertical(masked, north_flow, north_open, below_open):
+    count_rows = masked.shape[-1]
+    pad_widths = [(0, 0)] * (masked.ndim - 1) + [(2, 2)]
+    padded = jnp.pad(masked, pad_widths)
+    south_one = padded[..., 1 : count_rows + 1]
+    north_one = padded[..., 3 : count_rows + 3]
+    north_two = padded[..., 4 : count_rows + 4]
+    face_north = (7.0 * (masked + north_one) - (south_one + north_two)) / 12.0
+    flux_north = north_flow * face_north - HORIZ_DIFF * (north_one - masked) * north_open
+    flux_south = jnp.concatenate(
+        [jnp.zeros_like(flux_north[..., :1]), flux_north[..., :-1]], axis=-1
+    )
+    below = jnp.concatenate([masked[..., 1:, :, :], jnp.zeros_like(masked[..., :1, :, :])], axis=-3)
+    flux_down = VERT_DIFF * (below - masked) * below_open
+    flux_up = jnp.concatenate(
+        [jnp.zeros_like(flux_down[..., :1, :, :]), flux_down[..., :-1, :, :]], axis=-3
+    )
+    return flux_south - flux_north + (flux_down - flux_up)
+
+
+def plain_sources(masked):
+    oxygen = masked[0]
+    nitrate = masked[1]
+    nitrite = masked[2]
+    ammonium = masked[3]
+    carbon = masked[5]
+    sulfide = masked[6]
+    nitrous = masked[7]
+    breakdown = RATE_CARBON * carbon
+    with_oxygen = oxygen / (oxygen + HALF_OXYGEN)
+    with_nitrate = (1.0 - with_oxygen) * nitrate / (nitrate + HALF_NITRATE)
+    with_nitrite = (1.0 - with_oxygen - with_nitrate) * nitrite / (nitrite + HALF_NITRITE)
+    with_sulfate = 1.0 - with_oxygen - with_nitrate - with_nitrite
+    first_nitr = RATE_AMMONIUM * ammonium * with_oxygen
+    second_nitr = RATE_NITRITE * nitrite * with_oxygen
+    sulfide_ox = RATE_SULFIDE * sulfide * with_oxygen
+    return jnp.stack(
+        [
+            -1.3 * breakdown * with_oxygen
+            - 1.5 * first_nitr
+            - 0.5 * second_nitr
+            - 2.0 * sulfide_ox,
+            -0.9 * breakdown * with_nitrate + second_nitr,
+            0.9 * breakdown * with_nitrate
+            - 0.6 * breakdown * with_nitrite
+            + (1.0 - YIELD_NITROUS) * first_nitr
+            - second_nitr,
+            0.15 * breakdown - first_nitr,
+            0.1 * breakdown,
+            -breakdown,
+            0.5 * breakdown * with_sulfate - sulfide_ox,
+            YIELD_NITROUS * first_nitr - RATE_NITROUS * nitrous * (1.0 - with_oxygen),
+        ]
+    )
+
+
+def plain_body(
+    surface_old,
+    surface_forcing,
+    surface_coeff,
+    ocean_mask,
+    column_depth,
+    east_depth,
+    tracers,
+    u_clinic,
+    v_clinic,
+):
+    mask_float = ocean_mask.astype(jnp.float32)
+    right_side = surface_coeff * surface_old + surface_forcing
+    surface = plain_solve(right_side, mask_float, surface_coeff)
+    band_flow = -BARO_GAIN * (jnp.roll(surface, -1, axis=1) - surface)
+    moved = lax.all_to_all(
+        jnp.stack([surface, band_flow]), "lon", split_axis=2, concat_axis=1, tiled=True
+    )
+    strip_surface = moved[0].T
+    east_baro = moved[1].T
+    above_surface = jnp.concatenate([strip_surface[:, 1:], strip_surface[:, -1:]], axis=1)
+    north_baro = -BARO_GAIN * (above_surface - strip_surface)
+    wet, east_open, north_open, below_open, east_flow, north_flow = open_faces(
+        column_depth, east_depth, east_baro, north_baro, u_clinic, v_clinic
+    )
+    masked = tracers * wet[None]
+    tracer_count = masked.shape[0]
+    columns_here = masked.shape[2]
+    stacked = jnp.concatenate([masked, east_flow[None], east_open[None]], axis=0)
+    padded = padded_2(stacked, (("lon", 2),), 2, True)
+    tracer_pad = padded[:tracer_count]
+    west_flow = padded[tracer_count, :, 1:2]
+    west_open = padded[tracer_count + 1, :, 1:2]
+    flow_all = jnp.concatenate([west_flow, east_flow], axis=1)
+    open_all = jnp.concatenate([west_open, east_open], axis=1)
+    center = tracer_pad[:, :, 1 : columns_here + 2]
+    east_one = tracer_pad[:, :, 2 : columns_here + 3]
+    west_one = tracer_pad[:, :, 0 : columns_here + 1]
+    east_two = tracer_pad[:, :, 3 : columns_here + 4]
+    face_east = (7.0 * (center + east_one) - (west_one + east_two)) / 12.0
+    flux_all = flow_all[None] * face_east - HORIZ_DIFF * (east_one - center) * open_all[None]
+    conv_east = flux_all[:, :, :-1] - flux_all[:, :, 1:]
+    transport = conv_east + meridional_vertical(
+        masked, north_flow[None], north_open[None], below_open[None]
+    )
+    tendency = transport + plain_sources(masked)
+    tracers_new = tracers + wet[None] * tendency
+    return (surface, tracers_new)
 
 
 def solution(mesh):

time: 29.9 us -> 31.7 us (1.060)
  between operations: 0.77 us -> 1.63 us
  local copies, waits for them, and re-layouts: 0.21 us -> 0.77 us
    ppermute x1, starting transfers between devices: 0.01 us -> 3.99 us  [body(): edge_inner = lax.ppermute(own_inner, 'lon', pairs_inner)]
    ppermute x1, starting transfers between devices: 5.57 us -> 3.5 us  [body(): edge_outer = lax.ppermute(own_outer, 'lon', ring)]
    ppermute x3, starting transfers between devices: 5.48 us -> 4.12 us  [body(): slabs.append(lax.ppermute(sends[step], 'lon', pairs))]
    slice x0 -> x1, local copies, waits for them, and re-layouts: none -> 0.58 us  [body(): weak[0, 0] > 0.0]
    ppermute x1, starting transfers between devices: 0.58 us -> 0.07 us  [body(): came = lax.ppermute(send, 'lon', pairs_inner)]
    pallas_call x10 -> x11, Pallas kernels: 13.7 us -> 13.8 us  [call(): pl.pallas_call(kernel, out_shape=out_shape, in_specs=[hbm if place in far...]
  transfers between devices with their start and end apart: 9 -> 9, of which waited for: 2 -> 3; matrix products, arithmetic and copies ran while one was open for 0% -> 0% of each run, Pallas kernels for 32% -> 30%
where the time goes in v9:
time: 31.7 us; the launch traced here: 31.5 us
  starting transfers between devices  14.1 us (44%)
  Pallas kernels  13.8 us (44%)
  between operations  1.63 us (5%)
  waiting for transfers between devices  0.99 us (3%)
  local copies, waits for them, and re-layouts  0.77 us (2%)
    pallas_call x11, Pallas kernels, call(): pl.pallas_call(kernel, out_shape=out_shape, in_specs=[hbm if place in far...  13.8 us
    ppermute x3, starting transfers between devices, body(): slabs.append(lax.ppermute(sends[step], 'lon', pairs))  4.12 us
    ppermute x1, starting transfers between devices, body(): edge_inner = lax.ppermute(own_inner, 'lon', pairs_inner)  3.99 us
    ppermute x1, starting transfers between devices, body(): edge_outer = lax.ppermute(own_outer, 'lon', ring)  3.5 us
    ppermute x1, starting transfers between devices, body(): came = lax.ppermute(send, 'lon', [(i, i ^ 2) for i in range(count)])  1.29 us
    ppermute x1, starting transfers between devices, body(): came_outer = lax.ppermute(outer, 'lon', pairs_outer)  0.65 us
  transfers between devices with their start and end apart: 9, of which 3 were waited for; matrix products, arithmetic and copies ran while one was open for 0% of the time, Pallas kernels for 30%

profile of v9, /device:TPU:0, one launch (start us, length us, event | category | flops | bytes accessed | tf_op | source)
XLA Modules:
  0.0 31.5 jit_solution(17186813529537334517)
XLA Ops:
  0.6 0.0 copy-start.2
  0.7 1.0 %pack_edges.1 = (f32[24,256]{1,0:T(8,128)S(1)}, f32[24,256]{1,0:T(8,128)S(1)}, f32[96,256]{1,0:T(8,128)S(1)}) custom-call(f32[32,256]{1,0:T(8,128)} %old_in.1, f32[32,256]{1,0:T(8,128)} %force_in.1, f32[32,256]{1,0:T(8,128)} %coeff_in.1, s32[32,256]{1,0:T(8,128)} %mask_in.1), custom_call_target="tpu_custom_call" | custom-call | flops 2097152000 | bytes 8388608 | tf_op jit(solution)/shard_map/pack_edges/pallas_call | solution.py:694
  1.7 0.5 %collective-permute-start.10 = (f32[24,256]{1,0:T(8,128)S(1)}, f32[24,256]{1,0:T(8,128)S(1)}, u32[]{:S(2)}, u32[]{:S(2)}) collective-permute-start(f32[24,256]{1,0:T(8,128)S(1)} %get-tuple-element.60), channel_id=1, source_target_pairs={{0,1},{1,0},{2,3},{3,2},{4,5},{5,4},{6,7},{7,6},{8,9},{9,8},{10,11... | collective-permute-start | bytes 73736 | tf_op jit(solution)/shard_map/ppermute | solution.py:735
  2.2 0.7 %collective-permute-start.11 = (f32[24,256]{1,0:T(8,128)S(1)}, f32[24,256]{1,0:T(8,128)S(1)}, u32[]{:S(2)}, u32[]{:S(2)}) collective-permute-start(f32[24,256]{1,0:T(8,128)S(1)} %get-tuple-element.61._.high_ref), channel_id=1, source_target_pairs={{1,2},{2,1},{3,4},{4,3},{5,6},{6,5},{7,8},{8,7},{9,10},{10,9},{11,... | collective-permute-start | bytes 73736 | tf_op jit(solution)/shard_map/ppermute | solution.py:736
  2.9 0.0 copy-done.2
  2.9 0.1 copy-done.7
  3.0 0.3 pack_tracer_edges.1
  3.3 4.0 %collective-permute-start.17 = (f32[35,8,512]{2,1,0:T(8,128)S(1)}, f32[35,8,512]{2,1,0:T(8,128)S(1)}, u32[]{:S(2)}, u32[]{:S(2)}) collective-permute-start(f32[35,8,512]{2,1,0:T(8,128)S(1)} %get-tuple-element.69._.own_inner_ref), channel_id=1, source_target_pairs={{0,1},{1,0},{2,3},{3,2},{4,5},{5,4},{6,7},{7,6},{8,9},{9,8},{10,11... | collective-permute-start | bytes 1720328 | tf_op jit(solution)/shard_map/ppermute | solution.py:759
  7.3 3.5 %collective-permute-start.18 = (f32[35,8,512]{2,1,0:T(8,128)S(1)}, f32[35,8,512]{2,1,0:T(8,128)S(1)}, u32[]{:S(2)}, u32[]{:S(2)}) collective-permute-start(f32[35,8,512]{2,1,0:T(8,128)S(1)} %get-tuple-element.62._.own_outer_ref), channel_id=1, source_target_pairs={{0,15},{1,2},{2,1},{3,4},{4,3},{5,6},{6,5},{7,8},{8,7},{9,10},{10,... | collective-permute-start | bytes 1720328 | tf_op jit(solution)/shard_map/ppermute | solution.py:760
  10.8 0.0 collective-permute-done.10.inner_ref
  10.8 0.0 collective-permute-done.11.outer_ref
  10.8 0.5 %solver_basis.1 = (f32[128,256]{1,0:T(8,128)S(1)}, f32[8,24,128]{2,1,0:T(8,128)S(1)}, f32[8,24,128]{2,1,0:T(8,128)S(1)}) custom-call(f32[96,256]{1,0:T(8,128)S(1)} %get-tuple-element.59.own_ref, f32[24,256]{1,0:T(8,128)S(1)} %collective-permute-done.10.inner_ref, f32[24,256]{1,0:T(8,128)S(1)} %collective-permute-done.11.outer_ref, f32[24,256]{1,0:T(8,128)S(1)} %fold.1.folded_ref), custom_call_target="tpu_custom_call" | custom-call | flops 2097152000 | bytes 8388608 | tf_op jit(solution)/shard_map/solver_basis/pallas_call | solution.py:694
  11.3 0.1 collective-permute-start.12
  11.4 1.2 %sources_0.1 = (f32[8,8,16,512]{3,2,1,0:T(8,128)S(1)}, f32[8,8,16,512]{3,2,1,0:T(8,128)S(1)}) custom-call(f32[8,16,16,512]{3,2,1,0:T(8,128)S(1)} %copy-done.2, s32[16,512]{1,0:T(8,128)S(1)} %copy-done.14, f32[35,8,512]{2,1,0:T(8,128)S(1)} %get-tuple-element.69._.own_inner_ref), custom_call_target="tpu_custom_call" | custom-call | flops 2097152000 | bytes 8388608 | tf_op jit(solution)/shard_map/sources_0/pallas_call | solution.py:694
  12.6 0.0 copy-start.12
  12.6 0.1 collective-permute-done.12.came_ref
  12.7 0.2 collective-permute-start.13
  12.9 2.6 %collective-permute-start.14 = (f32[2,2,24,128]{3,2,1,0:T(8,128)S(1)}, f32[2,2,24,128]{3,2,1,0:T(8,128)S(1)}, u32[]{:S(2)}, u32[]{:S(2)}) collective-permute-start(f32[2,2,24,128]{3,2,1,0:T(8,128)S(1)} %get-tuple-element.67), channel_id=1, source_target_pairs={{0,8},{1,9},{2,10},{3,11},{4,12},{5,13},{6,14},{7,15},{8,0},{9,1},... | collective-permute-start | bytes 147464 | tf_op jit(solution)/shard_map/ppermute | solution.py:758
  15.5 1.3 %collective-permute-start.15 = (f32[2,2,24,128]{3,2,1,0:T(8,128)S(1)}, f32[2,2,24,128]{3,2,1,0:T(8,128)S(1)}, u32[]{:S(2)}, u32[]{:S(2)}) collective-permute-start(f32[2,2,24,128]{3,2,1,0:T(8,128)S(1)} %get-tuple-element.68), channel_id=1, source_target_pairs={{0,12},{1,13},{2,14},{3,15},{4,0},{5,1},{6,2},{7,3},{8,4},{9,5},{1... | collective-permute-start | bytes 147464 | tf_op jit(solution)/shard_map/ppermute | solution.py:758
  16.8 1.2 %sources_1.1 = (f32[8,8,16,512]{3,2,1,0:T(8,128)S(1)}, f32[8,8,16,512]{3,2,1,0:T(8,128)S(1)}) custom-call(f32[8,16,16,512]{3,2,1,0:T(8,128)S(1)} %copy-done.2, s32[16,512]{1,0:T(8,128)S(1)} %copy-done.14, f32[2,2,24,128]{3,2,1,0:T(8,128)S(1)} %get-tuple-element.65._.refs_0_), custom_call_target="tpu_custom_call" | custom-call | flops 2097152000 | bytes 8388608 | tf_op jit(solution)/shard_map/sources_1/pallas_call | solution.py:694
  18.0 3.3 %north_fluxes.1 = (f32[8,2,512,128]{3,2,1,0:T(8,128)S(1)}, f32[8,2,512,128]{3,2,1,0:T(8,128)S(1)}) custom-call(s32[16,512]{1,0:T(8,128)S(1)} %copy-done.14, f32[16,16,512]{2,1,0:T(8,128)S(1)} %copy-done.12, f32[2,2,24,128]{3,2,1,0:T(8,128)S(1)} %get-tuple-element.65._.refs_0_, f32[8,8,16,512]{3,2,1,0:T(8,128)S(1)} %get-tuple-element.70.refs_0_, ...), custom_call_target="tpu_custom_call" | custom-call | flops 2097152000 | bytes 8388608 | tf_op jit(solution)/shard_map/north_fluxes/pallas_call | solution.py:694
  21.3 0.6 %collective-permute-done.13.refs_1_ = f32[2,2,24,128]{3,2,1,0:T(8,128)S(1)} collective-permute-done((f32[2,2,24,128]{3,2,1,0:T(8,128)S(1)}, f32[2,2,24,128]{3,2,1,0:T(8,128)S(1)}, u32[]{:S(2)}, u32[]{:S(2)}) %collective-permute-start.13) | collective-permute-done | bytes 49184 | tf_op jit(solution)/shard_map/ppermute | solution.py:758
  22.0 0.0 collective-permute-done.14.refs_2_
  22.0 0.0 collective-permute-done.15.refs_3_
  22.0 1.3 %collective-permute-start.16 = (f32[4,2,24,128]{3,2,1,0:T(8,128)S(1)}, f32[4,2,24,128]{3,2,1,0:T(8,128)S(1)}, u32[]{:S(2)}, u32[]{:S(2)}) collective-permute-start(f32[4,2,24,128]{3,2,1,0:T(8,128)S(1)} %get-tuple-element.74), channel_id=1, source_target_pairs={{0,2},{1,3},{2,0},{3,1},{4,6},{5,7},{6,4},{7,5},{8,10},{9,11},{10,... | collective-permute-start | bytes 294920 | tf_op jit(solution)/shard_map/ppermute | solution.py:785
  23.3 0.0 collective-permute-done.17.inner_ref
  23.3 0.0 collective-permute-done.18.outer_ref
  23.3 3.1 %east_fluxes.1 = (f32[8,16,16,512]{3,2,1,0:T(8,128)S(1)}, f32[8,16,16,512]{3,2,1,0:T(8,128)S(1)}, f32[8,16,512]{2,1,0:T(8,128)S(1)}) custom-call(s32[16,512]{1,0:T(8,128)S(1)} %copy-done.9, f32[16,16,512]{2,1,0:T(8,128)S(1)} %copy-done.7, f32[35,8,512]{2,1,0:T(8,128)S(1)} %collective-permute-done.17.inner_ref, ...), custom_call_target="tpu_custom_call" | custom-call | flops 2097152000 | bytes 8388608 | tf_op jit(solution)/shard_map/east_fluxes/pallas_call | solution.py:694
  26.4 0.3 collective-permute-done.16.came_ref
  26.7 3.2 %surface_update.1 = (f32[32,256]{1,0:T(8,128)}, f32[8,16,16,512]{3,2,1,0:T(8,128)}, f32[8,128]{1,0:T(8,128)S(1)}) custom-call(f32[4,2,24,128]{3,2,1,0:T(8,128)S(1)} %get-tuple-element.73._.kept_ref, f32[4,2,24,128]{3,2,1,0:T(8,128)S(1)} %collective-permute-done.16.came_ref, f32[128,256]{1,0:T(8,128)S(1)} %get-tuple-element.75.basis_ref, ...), custom_call_target="tpu_custom_call" | custom-call | tf_op jit(solution)/shard_map/surface_update/pallas_call | solution.py:694
  29.9 0.6 %slice.211 = f32[1,1]{1,0:T(1,128)} slice(f32[8,128]{1,0:T(8,128)S(1)} %get-tuple-element.82), slice={[0:1], [0:1]} | slice | bytes 8 | tf_op jit(solution)/shard_map/slice | solution.py:829
  31.1 0.2 conditional.1
  (17 shorter events, 0.1 us)
Async XLA Ops:
  0.6 2.3 %copy-start.2 = (f32[8,16,16,512]{3,2,1,0:T(8,128)S(1)}, f32[8,16,16,512]{3,2,1,0:T(8,128)}, u32[]{:S(2)}) copy-start(f32[8,16,16,512]{3,2,1,0:T(8,128)} %tracers_ref.5) | copy-start | bytes 12582916
  0.6 2.2 %copy-start.14 = (s32[16,512]{1,0:T(8,128)S(1)}, s32[16,512]{1,0:T(8,128)}, u32[]{:S(2)}) copy-start(s32[16,512]{1,0:T(8,128)} %depth_ref.7) | copy-start | bytes 98308
  0.7 2.2 %copy-start.9 = (s32[16,512]{1,0:T(8,128)S(1)}, s32[16,512]{1,0:T(8,128)}, u32[]{:S(2)}) copy-start(s32[16,512]{1,0:T(8,128)} %east_depth_ref.3) | copy-start | bytes 98308
  0.7 2.4 %copy-start.7 = (f32[16,16,512]{2,1,0:T(8,128)S(1)}, f32[16,16,512]{2,1,0:T(8,128)}, u32[]{:S(2)}) copy-start(f32[16,16,512]{2,1,0:T(8,128)} %u_ref.3) | copy-start | bytes 1572868
  1.7 9.1 %collective-permute-start.10 = (f32[24,256]{1,0:T(8,128)S(1)}, f32[24,256]{1,0:T(8,128)S(1)}, u32[]{:S(2)}, u32[]{:S(2)}) collective-permute-start(f32[24,256]{1,0:T(8,128)S(1)} %get-tuple-element.60), channel_id=1, source_target_pairs={{0,1},{1,0},{2,3},{3,2},{4,5},{5,4},{6,7},{7,6},{8,9},{9,8},{10,11... | collective-permute-start | bytes 73736 | tf_op jit(solution)/shard_map/ppermute | solution.py:735
  2.2 8.6 %collective-permute-start.11 = (f32[24,256]{1,0:T(8,128)S(1)}, f32[24,256]{1,0:T(8,128)S(1)}, u32[]{:S(2)}, u32[]{:S(2)}) collective-permute-start(f32[24,256]{1,0:T(8,128)S(1)} %get-tuple-element.61._.high_ref), channel_id=1, source_target_pairs={{1,2},{2,1},{3,4},{4,3},{5,6},{6,5},{7,8},{8,7},{9,10},{10,9},{11,... | collective-permute-start | bytes 73736 | tf_op jit(solution)/shard_map/ppermute | solution.py:736
  3.3 19.9 %collective-permute-start.17 = (f32[35,8,512]{2,1,0:T(8,128)S(1)}, f32[35,8,512]{2,1,0:T(8,128)S(1)}, u32[]{:S(2)}, u32[]{:S(2)}) collective-permute-start(f32[35,8,512]{2,1,0:T(8,128)S(1)} %get-tuple-element.69._.own_inner_ref), channel_id=1, source_target_pairs={{0,1},{1,0},{2,3},{3,2},{4,5},{5,4},{6,7},{7,6},{8,9},{9,8},{10,11... | collective-permute-start | bytes 1720328 | tf_op jit(solution)/shard_map/ppermute | solution.py:759
  7.3 16.0 %collective-permute-start.18 = (f32[35,8,512]{2,1,0:T(8,128)S(1)}, f32[35,8,512]{2,1,0:T(8,128)S(1)}, u32[]{:S(2)}, u32[]{:S(2)}) collective-permute-start(f32[35,8,512]{2,1,0:T(8,128)S(1)} %get-tuple-element.62._.own_outer_ref), channel_id=1, source_target_pairs={{0,15},{1,2},{2,1},{3,4},{4,3},{5,6},{6,5},{7,8},{8,7},{9,10},{10,... | collective-permute-start | bytes 1720328 | tf_op jit(solution)/shard_map/ppermute | solution.py:760
  11.3 1.4 %collective-permute-start.12 = (f32[8,24,128]{2,1,0:T(8,128)S(1)}, f32[8,24,128]{2,1,0:T(8,128)S(1)}, u32[]{:S(2)}, u32[]{:S(2)}) collective-permute-start(f32[8,24,128]{2,1,0:T(8,128)S(1)} %get-tuple-element.64), channel_id=1, source_target_pairs={{0,1},{1,0},{2,3},{3,2},{4,5},{5,4},{6,7},{7,6},{8,9},{9,8},{10,11... | collective-permute-start | bytes 294920 | tf_op jit(solution)/shard_map/ppermute | solution.py:748
  12.6 5.4 %copy-start.12 = (f32[16,16,512]{2,1,0:T(8,128)S(1)}, f32[16,16,512]{2,1,0:T(8,128)}, u32[]{:S(2)}) copy-start(f32[16,16,512]{2,1,0:T(8,128)} %v_ref.1) | copy-start | bytes 1572868
  12.7 9.2 %collective-permute-start.13 = (f32[2,2,24,128]{3,2,1,0:T(8,128)S(1)}, f32[2,2,24,128]{3,2,1,0:T(8,128)S(1)}, u32[]{:S(2)}, u32[]{:S(2)}) collective-permute-start(f32[2,2,24,128]{3,2,1,0:T(8,128)S(1)} %get-tuple-element.66), channel_id=1, source_target_pairs={{0,4},{1,5},{2,6},{3,7},{4,8},{5,9},{6,10},{7,11},{8,12},{9,13},{1... | collective-permute-start | bytes 147464 | tf_op jit(solution)/shard_map/ppermute | solution.py:758
  12.9 9.0 %collective-permute-start.14 = (f32[2,2,24,128]{3,2,1,0:T(8,128)S(1)}, f32[2,2,24,128]{3,2,1,0:T(8,128)S(1)}, u32[]{:S(2)}, u32[]{:S(2)}) collective-permute-start(f32[2,2,24,128]{3,2,1,0:T(8,128)S(1)} %get-tuple-element.67), channel_id=1, source_target_pairs={{0,8},{1,9},{2,10},{3,11},{4,12},{5,13},{6,14},{7,15},{8,0},{9,1},... | collective-permute-start | bytes 147464 | tf_op jit(solution)/shard_map/ppermute | solution.py:758
  15.5 6.5 %collective-permute-start.15 = (f32[2,2,24,128]{3,2,1,0:T(8,128)S(1)}, f32[2,2,24,128]{3,2,1,0:T(8,128)S(1)}, u32[]{:S(2)}, u32[]{:S(2)}) collective-permute-start(f32[2,2,24,128]{3,2,1,0:T(8,128)S(1)} %get-tuple-element.68), channel_id=1, source_target_pairs={{0,12},{1,13},{2,14},{3,15},{4,0},{5,1},{6,2},{7,3},{8,4},{9,5},{1... | collective-permute-start | bytes 147464 | tf_op jit(solution)/shard_map/ppermute | solution.py:758
  22.0 4.7 %collective-permute-start.16 = (f32[4,2,24,128]{3,2,1,0:T(8,128)S(1)}, f32[4,2,24,128]{3,2,1,0:T(8,128)S(1)}, u32[]{:S(2)}, u32[]{:S(2)}) collective-permute-start(f32[4,2,24,128]{3,2,1,0:T(8,128)S(1)} %get-tuple-element.74), channel_id=1, source_target_pairs={{0,2},{1,3},{2,0},{3,1},{4,6},{5,7},{6,4},{7,5},{8,10},{9,11},{10,... | collective-permute-start | bytes 294920 | tf_op jit(solution)/shard_map/ppermute | solution.py:785
  26.7 4.4 %copy-start.8 = (s32[32,256]{1,0:T(8,128)S(1)}, s32[32,256]{1,0:T(8,128)}, u32[]{:S(2)}) copy-start(s32[32,256]{1,0:T(8,128)} %mask_in.1) | copy-start | bytes 98308
  26.7 4.4 %copy-start.10 = (f32[32,256]{1,0:T(8,128)S(1)}, f32[32,256]{1,0:T(8,128)}, u32[]{:S(2)}) copy-start(f32[32,256]{1,0:T(8,128)} %coeff_in.1) | copy-start | bytes 98308
  26.7 4.4 %copy-start.15 = (f32[32,256]{1,0:T(8,128)S(1)}, f32[32,256]{1,0:T(8,128)}, u32[]{:S(2)}) copy-start(f32[32,256]{1,0:T(8,128)} %old_in.1) | copy-start | bytes 98308
  26.7 4.4 %copy-start.16 = (f32[32,256]{1,0:T(8,128)S(1)}, f32[32,256]{1,0:T(8,128)}, u32[]{:S(2)}) copy-start(f32[32,256]{1,0:T(8,128)} %force_in.1) | copy-start | bytes 98308

commit v10 on v9

--- a/solution.py
+++ b/solution.py
@@ -558,7 +558,7 @@
     weights, weak = basis_weights(
         dots[:2] + [2.0 * dots[m] - dots[m % 2] for m in range(2, 2 * BASIS)]
     )
-    weak_ref[...] = jnp.broadcast_to(weak, (SUBLANES, LANES))
+    weak_ref[...] = weak[:, :1]
     lane_group = lax.broadcasted_iota(jnp.int32, (1, LANES), 1) // band
     lane_weight = jnp.zeros((1, LANES), jnp.float32)
     for k in range(BASIS):
@@ -809,7 +809,7 @@
     surface, tracers_new, weak = (
         call(
             update_kernel,
-            (solved, result, sds((SUBLANES, LANES), f32)),
+            (solved, result, sds((1, 1), f32)),
             "surface_update",
             (keep, came, basis, base, face_east, face_west, change, face_north),
             scratch=[
@@ -826,7 +826,7 @@
         )
     )
     return lax.cond(
-        weak[0, 0] > 0.0, lambda: plain_body(*given), lambda: (surface, tracers_new)
+        weak.reshape(()) > 0.0, lambda: plain_body(*given), lambda: (surface, tracers_new)
     )
 
 

time: 31.7 us -> 31.7 us (level)
  local copies, waits for them, and re-layouts: 0.77 us -> 0.19 us
  Pallas kernels: 13.8 us -> 14.3 us
    slice x1 -> x0, local copies, waits for them, and re-layouts: 0.58 us -> none  [body(): weak[0, 0] > 0.0]
    pallas_call x11, Pallas kernels: 13.8 us -> 14.3 us  [call(): pl.pallas_call(kernel, out_shape=out_shape, in_specs=[hbm if place in far...]
where the time goes in v10:
time: 31.7 us; the launch traced here: 31.5 us
  Pallas kernels  14.3 us (45%)
  starting transfers between devices  14.1 us (44%)
  between operations  1.63 us (5%)
  waiting for transfers between devices  0.99 us (3%)
    pallas_call x11, Pallas kernels, call(): pl.pallas_call(kernel, out_shape=out_shape, in_specs=[hbm if place in far...  14.3 us
    ppermute x3, starting transfers between devices, body(): slabs.append(lax.ppermute(sends[step], 'lon', pairs))  4.12 us
    ppermute x1, starting transfers between devices, body(): edge_inner = lax.ppermute(own_inner, 'lon', pairs_inner)  3.99 us
    ppermute x1, starting transfers between devices, body(): edge_outer = lax.ppermute(own_outer, 'lon', ring)  3.5 us
    ppermute x1, starting transfers between devices, body(): came = lax.ppermute(send, 'lon', [(i, i ^ 2) for i in range(count)])  1.29 us
    ppermute x1, starting transfers between devices, body(): came_outer = lax.ppermute(outer, 'lon', pairs_outer)  0.65 us
  transfers between devices with their start and end apart: 9, of which 3 were waited for; matrix products, arithmetic and copies ran while one was open for 0% of the time, Pallas kernels for 30%

profile of v10, /device:TPU:0, one launch (start us, length us, event | category | flops | bytes accessed | tf_op | source)
XLA Modules:
  0.0 31.5 jit_solution(15361560461603103542)
XLA Ops:
  0.6 0.0 copy-start.2
  0.7 1.0 %pack_edges.1 = (f32[24,256]{1,0:T(8,128)S(1)}, f32[24,256]{1,0:T(8,128)S(1)}, f32[96,256]{1,0:T(8,128)S(1)}) custom-call(f32[32,256]{1,0:T(8,128)} %old_in.1, f32[32,256]{1,0:T(8,128)} %force_in.1, f32[32,256]{1,0:T(8,128)} %coeff_in.1, s32[32,256]{1,0:T(8,128)} %mask_in.1), custom_call_target="tpu_custom_call" | custom-call | flops 2097152000 | bytes 8388608 | tf_op jit(solution)/shard_map/pack_edges/pallas_call | solution.py:694
  1.7 0.5 %collective-permute-start.10 = (f32[24,256]{1,0:T(8,128)S(1)}, f32[24,256]{1,0:T(8,128)S(1)}, u32[]{:S(2)}, u32[]{:S(2)}) collective-permute-start(f32[24,256]{1,0:T(8,128)S(1)} %get-tuple-element.60), channel_id=1, source_target_pairs={{0,1},{1,0},{2,3},{3,2},{4,5},{5,4},{6,7},{7,6},{8,9},{9,8},{10,11... | collective-permute-start | bytes 73736 | tf_op jit(solution)/shard_map/ppermute | solution.py:735
  2.2 0.7 %collective-permute-start.11 = (f32[24,256]{1,0:T(8,128)S(1)}, f32[24,256]{1,0:T(8,128)S(1)}, u32[]{:S(2)}, u32[]{:S(2)}) collective-permute-start(f32[24,256]{1,0:T(8,128)S(1)} %get-tuple-element.61._.high_ref), channel_id=1, source_target_pairs={{1,2},{2,1},{3,4},{4,3},{5,6},{6,5},{7,8},{8,7},{9,10},{10,9},{11,... | collective-permute-start | bytes 73736 | tf_op jit(solution)/shard_map/ppermute | solution.py:736
  2.9 0.0 copy-done.2
  2.9 0.0 copy-done.14
  2.9 0.1 copy-done.7
  3.0 0.3 pack_tracer_edges.1
  3.3 4.0 %collective-permute-start.17 = (f32[35,8,512]{2,1,0:T(8,128)S(1)}, f32[35,8,512]{2,1,0:T(8,128)S(1)}, u32[]{:S(2)}, u32[]{:S(2)}) collective-permute-start(f32[35,8,512]{2,1,0:T(8,128)S(1)} %get-tuple-element.69._.own_inner_ref), channel_id=1, source_target_pairs={{0,1},{1,0},{2,3},{3,2},{4,5},{5,4},{6,7},{7,6},{8,9},{9,8},{10,11... | collective-permute-start | bytes 1720328 | tf_op jit(solution)/shard_map/ppermute | solution.py:759
  7.3 3.5 %collective-permute-start.18 = (f32[35,8,512]{2,1,0:T(8,128)S(1)}, f32[35,8,512]{2,1,0:T(8,128)S(1)}, u32[]{:S(2)}, u32[]{:S(2)}) collective-permute-start(f32[35,8,512]{2,1,0:T(8,128)S(1)} %get-tuple-element.62._.own_outer_ref), channel_id=1, source_target_pairs={{0,15},{1,2},{2,1},{3,4},{4,3},{5,6},{6,5},{7,8},{8,7},{9,10},{10,... | collective-permute-start | bytes 1720328 | tf_op jit(solution)/shard_map/ppermute | solution.py:760
  10.8 0.0 collective-permute-done.10.inner_ref
  10.8 0.0 collective-permute-done.11.outer_ref
  10.8 0.5 %solver_basis.1 = (f32[128,256]{1,0:T(8,128)S(1)}, f32[8,24,128]{2,1,0:T(8,128)S(1)}, f32[8,24,128]{2,1,0:T(8,128)S(1)}) custom-call(f32[96,256]{1,0:T(8,128)S(1)} %get-tuple-element.59.own_ref, f32[24,256]{1,0:T(8,128)S(1)} %collective-permute-done.10.inner_ref, f32[24,256]{1,0:T(8,128)S(1)} %collective-permute-done.11.outer_ref, f32[24,256]{1,0:T(8,128)S(1)} %fold.1.folded_ref), custom_call_target="tpu_custom_call" | custom-call | flops 2097152000 | bytes 8388608 | tf_op jit(solution)/shard_map/solver_basis/pallas_call | solution.py:694
  11.3 0.1 collective-permute-start.12
  11.4 1.2 %sources_0.1 = (f32[8,8,16,512]{3,2,1,0:T(8,128)S(1)}, f32[8,8,16,512]{3,2,1,0:T(8,128)S(1)}) custom-call(f32[8,16,16,512]{3,2,1,0:T(8,128)S(1)} %copy-done.2, s32[16,512]{1,0:T(8,128)S(1)} %copy-done.14, f32[35,8,512]{2,1,0:T(8,128)S(1)} %get-tuple-element.69._.own_inner_ref), custom_call_target="tpu_custom_call" | custom-call | flops 2097152000 | bytes 8388608 | tf_op jit(solution)/shard_map/sources_0/pallas_call | solution.py:694
  12.6 0.0 copy-start.12
  12.6 0.1 collective-permute-done.12.came_ref
  12.7 0.2 collective-permute-start.13
  12.9 2.6 %collective-permute-start.14 = (f32[2,2,24,128]{3,2,1,0:T(8,128)S(1)}, f32[2,2,24,128]{3,2,1,0:T(8,128)S(1)}, u32[]{:S(2)}, u32[]{:S(2)}) collective-permute-start(f32[2,2,24,128]{3,2,1,0:T(8,128)S(1)} %get-tuple-element.67), channel_id=1, source_target_pairs={{0,8},{1,9},{2,10},{3,11},{4,12},{5,13},{6,14},{7,15},{8,0},{9,1},... | collective-permute-start | bytes 147464 | tf_op jit(solution)/shard_map/ppermute | solution.py:758
  15.5 1.3 %collective-permute-start.15 = (f32[2,2,24,128]{3,2,1,0:T(8,128)S(1)}, f32[2,2,24,128]{3,2,1,0:T(8,128)S(1)}, u32[]{:S(2)}, u32[]{:S(2)}) collective-permute-start(f32[2,2,24,128]{3,2,1,0:T(8,128)S(1)} %get-tuple-element.68), channel_id=1, source_target_pairs={{0,12},{1,13},{2,14},{3,15},{4,0},{5,1},{6,2},{7,3},{8,4},{9,5},{1... | collective-permute-start | bytes 147464 | tf_op jit(solution)/shard_map/ppermute | solution.py:758
  16.8 1.2 %sources_1.1 = (f32[8,8,16,512]{3,2,1,0:T(8,128)S(1)}, f32[8,8,16,512]{3,2,1,0:T(8,128)S(1)}) custom-call(f32[8,16,16,512]{3,2,1,0:T(8,128)S(1)} %copy-done.2, s32[16,512]{1,0:T(8,128)S(1)} %copy-done.14, f32[2,2,24,128]{3,2,1,0:T(8,128)S(1)} %get-tuple-element.65._.refs_0_), custom_call_target="tpu_custom_call" | custom-call | flops 2097152000 | bytes 8388608 | tf_op jit(solution)/shard_map/sources_1/pallas_call | solution.py:694
  18.0 3.3 %north_fluxes.1 = (f32[8,2,512,128]{3,2,1,0:T(8,128)S(1)}, f32[8,2,512,128]{3,2,1,0:T(8,128)S(1)}) custom-call(s32[16,512]{1,0:T(8,128)S(1)} %copy-done.14, f32[16,16,512]{2,1,0:T(8,128)S(1)} %copy-done.12, f32[2,2,24,128]{3,2,1,0:T(8,128)S(1)} %get-tuple-element.65._.refs_0_, f32[8,8,16,512]{3,2,1,0:T(8,128)S(1)} %get-tuple-element.70.refs_0_, ...), custom_call_target="tpu_custom_call" | custom-call | flops 2097152000 | bytes 8388608 | tf_op jit(solution)/shard_map/north_fluxes/pallas_call | solution.py:694
  21.3 0.6 %collective-permute-done.13.refs_1_ = f32[2,2,24,128]{3,2,1,0:T(8,128)S(1)} collective-permute-done((f32[2,2,24,128]{3,2,1,0:T(8,128)S(1)}, f32[2,2,24,128]{3,2,1,0:T(8,128)S(1)}, u32[]{:S(2)}, u32[]{:S(2)}) %collective-permute-start.13) | collective-permute-done | bytes 49184 | tf_op jit(solution)/shard_map/ppermute | solution.py:758
  22.0 0.0 collective-permute-done.14.refs_2_
  22.0 0.0 collective-permute-done.15.refs_3_
  22.0 1.3 %collective-permute-start.16 = (f32[4,2,24,128]{3,2,1,0:T(8,128)S(1)}, f32[4,2,24,128]{3,2,1,0:T(8,128)S(1)}, u32[]{:S(2)}, u32[]{:S(2)}) collective-permute-start(f32[4,2,24,128]{3,2,1,0:T(8,128)S(1)} %get-tuple-element.74), channel_id=1, source_target_pairs={{0,2},{1,3},{2,0},{3,1},{4,6},{5,7},{6,4},{7,5},{8,10},{9,11},{10,... | collective-permute-start | bytes 294920 | tf_op jit(solution)/shard_map/ppermute | solution.py:785
  23.3 0.0 collective-permute-done.17.inner_ref
  23.3 0.0 collective-permute-done.18.outer_ref
  23.3 3.1 %east_fluxes.1 = (f32[8,16,16,512]{3,2,1,0:T(8,128)S(1)}, f32[8,16,16,512]{3,2,1,0:T(8,128)S(1)}, f32[8,16,512]{2,1,0:T(8,128)S(1)}) custom-call(s32[16,512]{1,0:T(8,128)S(1)} %copy-done.9, f32[16,16,512]{2,1,0:T(8,128)S(1)} %copy-done.7, f32[35,8,512]{2,1,0:T(8,128)S(1)} %collective-permute-done.17.inner_ref, ...), custom_call_target="tpu_custom_call" | custom-call | flops 2097152000 | bytes 8388608 | tf_op jit(solution)/shard_map/east_fluxes/pallas_call | solution.py:694
  26.4 0.3 collective-permute-done.16.came_ref
  26.7 3.7 %surface_update.1 = (f32[32,256]{1,0:T(8,128)}, f32[8,16,16,512]{3,2,1,0:T(8,128)}, f32[1,1]{1,0:T(1,128)}) custom-call(f32[4,2,24,128]{3,2,1,0:T(8,128)S(1)} %get-tuple-element.73._.kept_ref, f32[4,2,24,128]{3,2,1,0:T(8,128)S(1)} %collective-permute-done.16.came_ref, f32[128,256]{1,0:T(8,128)S(1)} %get-tuple-element.75.basis_ref, ...), custom_call_target="tpu_custom_call" | custom-call | tf_op jit(solution)/shard_map/surface_update/pallas_call | solution.py:694
  31.1 0.2 conditional.1
  (16 shorter events, 0.1 us)
Async XLA Ops:
  0.6 2.3 %copy-start.2 = (f32[8,16,16,512]{3,2,1,0:T(8,128)S(1)}, f32[8,16,16,512]{3,2,1,0:T(8,128)}, u32[]{:S(2)}) copy-start(f32[8,16,16,512]{3,2,1,0:T(8,128)} %tracers_ref.5) | copy-start | bytes 12582916
  0.6 2.2 %copy-start.14 = (s32[16,512]{1,0:T(8,128)S(1)}, s32[16,512]{1,0:T(8,128)}, u32[]{:S(2)}) copy-start(s32[16,512]{1,0:T(8,128)} %depth_ref.7) | copy-start | bytes 98308
  0.7 2.2 %copy-start.9 = (s32[16,512]{1,0:T(8,128)S(1)}, s32[16,512]{1,0:T(8,128)}, u32[]{:S(2)}) copy-start(s32[16,512]{1,0:T(8,128)} %east_depth_ref.3) | copy-start | bytes 98308
  0.7 2.4 %copy-start.7 = (f32[16,16,512]{2,1,0:T(8,128)S(1)}, f32[16,16,512]{2,1,0:T(8,128)}, u32[]{:S(2)}) copy-start(f32[16,16,512]{2,1,0:T(8,128)} %u_ref.3) | copy-start | bytes 1572868
  1.7 9.1 %collective-permute-start.10 = (f32[24,256]{1,0:T(8,128)S(1)}, f32[24,256]{1,0:T(8,128)S(1)}, u32[]{:S(2)}, u32[]{:S(2)}) collective-permute-start(f32[24,256]{1,0:T(8,128)S(1)} %get-tuple-element.60), channel_id=1, source_target_pairs={{0,1},{1,0},{2,3},{3,2},{4,5},{5,4},{6,7},{7,6},{8,9},{9,8},{10,11... | collective-permute-start | bytes 73736 | tf_op jit(solution)/shard_map/ppermute | solution.py:735
  2.2 8.6 %collective-permute-start.11 = (f32[24,256]{1,0:T(8,128)S(1)}, f32[24,256]{1,0:T(8,128)S(1)}, u32[]{:S(2)}, u32[]{:S(2)}) collective-permute-start(f32[24,256]{1,0:T(8,128)S(1)} %get-tuple-element.61._.high_ref), channel_id=1, source_target_pairs={{1,2},{2,1},{3,4},{4,3},{5,6},{6,5},{7,8},{8,7},{9,10},{10,9},{11,... | collective-permute-start | bytes 73736 | tf_op jit(solution)/shard_map/ppermute | solution.py:736
  3.3 19.9 %collective-permute-start.17 = (f32[35,8,512]{2,1,0:T(8,128)S(1)}, f32[35,8,512]{2,1,0:T(8,128)S(1)}, u32[]{:S(2)}, u32[]{:S(2)}) collective-permute-start(f32[35,8,512]{2,1,0:T(8,128)S(1)} %get-tuple-element.69._.own_inner_ref), channel_id=1, source_target_pairs={{0,1},{1,0},{2,3},{3,2},{4,5},{5,4},{6,7},{7,6},{8,9},{9,8},{10,11... | collective-permute-start | bytes 1720328 | tf_op jit(solution)/shard_map/ppermute | solution.py:759
  7.3 16.0 %collective-permute-start.18 = (f32[35,8,512]{2,1,0:T(8,128)S(1)}, f32[35,8,512]{2,1,0:T(8,128)S(1)}, u32[]{:S(2)}, u32[]{:S(2)}) collective-permute-start(f32[35,8,512]{2,1,0:T(8,128)S(1)} %get-tuple-element.62._.own_outer_ref), channel_id=1, source_target_pairs={{0,15},{1,2},{2,1},{3,4},{4,3},{5,6},{6,5},{7,8},{8,7},{9,10},{10,... | collective-permute-start | bytes 1720328 | tf_op jit(solution)/shard_map/ppermute | solution.py:760
  11.3 1.4 %collective-permute-start.12 = (f32[8,24,128]{2,1,0:T(8,128)S(1)}, f32[8,24,128]{2,1,0:T(8,128)S(1)}, u32[]{:S(2)}, u32[]{:S(2)}) collective-permute-start(f32[8,24,128]{2,1,0:T(8,128)S(1)} %get-tuple-element.64), channel_id=1, source_target_pairs={{0,1},{1,0},{2,3},{3,2},{4,5},{5,4},{6,7},{7,6},{8,9},{9,8},{10,11... | collective-permute-start | bytes 294920 | tf_op jit(solution)/shard_map/ppermute | solution.py:748
  12.6 5.4 %copy-start.12 = (f32[16,16,512]{2,1,0:T(8,128)S(1)}, f32[16,16,512]{2,1,0:T(8,128)}, u32[]{:S(2)}) copy-start(f32[16,16,512]{2,1,0:T(8,128)} %v_ref.1) | copy-start | bytes 1572868
  12.7 9.2 %collective-permute-start.13 = (f32[2,2,24,128]{3,2,1,0:T(8,128)S(1)}, f32[2,2,24,128]{3,2,1,0:T(8,128)S(1)}, u32[]{:S(2)}, u32[]{:S(2)}) collective-permute-start(f32[2,2,24,128]{3,2,1,0:T(8,128)S(1)} %get-tuple-element.66), channel_id=1, source_target_pairs={{0,4},{1,5},{2,6},{3,7},{4,8},{5,9},{6,10},{7,11},{8,12},{9,13},{1... | collective-permute-start | bytes 147464 | tf_op jit(solution)/shard_map/ppermute | solution.py:758
  12.9 9.0 %collective-permute-start.14 = (f32[2,2,24,128]{3,2,1,0:T(8,128)S(1)}, f32[2,2,24,128]{3,2,1,0:T(8,128)S(1)}, u32[]{:S(2)}, u32[]{:S(2)}) collective-permute-start(f32[2,2,24,128]{3,2,1,0:T(8,128)S(1)} %get-tuple-element.67), channel_id=1, source_target_pairs={{0,8},{1,9},{2,10},{3,11},{4,12},{5,13},{6,14},{7,15},{8,0},{9,1},... | collective-permute-start | bytes 147464 | tf_op jit(solution)/shard_map/ppermute | solution.py:758
  15.5 6.5 %collective-permute-start.15 = (f32[2,2,24,128]{3,2,1,0:T(8,128)S(1)}, f32[2,2,24,128]{3,2,1,0:T(8,128)S(1)}, u32[]{:S(2)}, u32[]{:S(2)}) collective-permute-start(f32[2,2,24,128]{3,2,1,0:T(8,128)S(1)} %get-tuple-element.68), channel_id=1, source_target_pairs={{0,12},{1,13},{2,14},{3,15},{4,0},{5,1},{6,2},{7,3},{8,4},{9,5},{1... | collective-permute-start | bytes 147464 | tf_op jit(solution)/shard_map/ppermute | solution.py:758
  22.0 4.7 %collective-permute-start.16 = (f32[4,2,24,128]{3,2,1,0:T(8,128)S(1)}, f32[4,2,24,128]{3,2,1,0:T(8,128)S(1)}, u32[]{:S(2)}, u32[]{:S(2)}) collective-permute-start(f32[4,2,24,128]{3,2,1,0:T(8,128)S(1)} %get-tuple-element.74), channel_id=1, source_target_pairs={{0,2},{1,3},{2,0},{3,1},{4,6},{5,7},{6,4},{7,5},{8,10},{9,11},{10,... | collective-permute-start | bytes 294920 | tf_op jit(solution)/shard_map/ppermute | solution.py:785
  26.7 4.4 %copy-start.8 = (s32[32,256]{1,0:T(8,128)S(1)}, s32[32,256]{1,0:T(8,128)}, u32[]{:S(2)}) copy-start(s32[32,256]{1,0:T(8,128)} %mask_in.1) | copy-start | bytes 98308
  26.7 4.4 %copy-start.10 = (f32[32,256]{1,0:T(8,128)S(1)}, f32[32,256]{1,0:T(8,128)}, u32[]{:S(2)}) copy-start(f32[32,256]{1,0:T(8,128)} %coeff_in.1) | copy-start | bytes 98308
  26.7 4.4 %copy-start.15 = (f32[32,256]{1,0:T(8,128)S(1)}, f32[32,256]{1,0:T(8,128)}, u32[]{:S(2)}) copy-start(f32[32,256]{1,0:T(8,128)} %old_in.1) | copy-start | bytes 98308
  26.7 4.4 %copy-start.16 = (f32[32,256]{1,0:T(8,128)S(1)}, f32[32,256]{1,0:T(8,128)}, u32[]{:S(2)}) copy-start(f32[32,256]{1,0:T(8,128)} %force_in.1) | copy-start | bytes 98308
